TPU v7x, 32 devices: a whole 2x2x4 slice. The times are simulated.
32 devices in a mesh: dp: 16 (over z, y, core), vocab: 2 (over x).
Axes of the slice: x: 2, y: 2, z: 4, core: 2. Of those that a mesh axis runs over, the one named last changes fastest.
Arguments:
- hidden: bfloat16 [6144, 4096], P('dp'), may hold values from -6 to 6
- head_weight: bfloat16 [4096, 16000], P('dp', 'vocab'), may hold values from -0.09375 to 0.09375
- head_bias: float32 [16000], P('vocab'), may hold values from -3.5 to -1.5
- query_len: int32 [64], P('dp'), may hold values from 8 to 32
- passage_len: int32 [64], P('dp'), may hold values from 16 to 64
- neg_owner: int32 [64, 8], P('dp'), may hold values from 0 to 15, all different within a row; in each aligned block of 4 rows (0 to 3, 4 to 7, ...) at most 2 rows name the same one
- neg_index: int32 [64, 8], P('dp'), may hold values from 0 to 3
- teacher: float32 [64, 8], P('dp'), may hold values from -8 to 8
Outputs:
- margin_error: float32 [64, 8], P('dp')
- hidden_grad: float32 [6144, 4096], P(('dp', 'vocab'))
Inputs may be any that keep to these rules, and one draw needn't show every extreme that they name: `neg_owner`: the 8 negatives of a query have different holders. Among the queries of one index of dp no holder appears more than 2 times, and in some of those blocks one holder appears exactly 2 times.
All inputs are finite; a program needn't handle non-finite values.
Results may differ from a plain program's by a relative error of at most 0.0028.
Values may be sent and summed in bfloat16 or wider, within the bound.
No kernel may reach another device: no remote copies, remote signals or barrier semaphores. Data moves between devices by JAX's collectives and lax.ppermute only.
A program may use at most 192 MiB of HBM per device.

v0:
```python
import jax
import jax.numpy as jnp
from jax import lax
from jax.sharding import PartitionSpec as P

LQ = 32
LP = 64


TAU = 0.05


def soft_pool(token_logits, token_mask):
    activation = jnp.log1p(jnp.maximum(token_logits, 0.0))
    weights = jnp.exp(activation / TAU) * token_mask[:, :, None]
    summed = jnp.sum(weights, axis=1)
    valid_count = jnp.sum(token_mask, axis=1)[:, None]
    return (TAU * jnp.log(summed / valid_count), weights / summed[:, None, :])


def lengths_mask(lengths, span):
    return (jnp.arange(span)[None, :] < lengths[:, None]).astype(jnp.float32)


def per_device(
    hidden, head_weight, head_bias, query_len, passage_len, neg_owner, neg_index, teacher
):
    query_count = neg_owner.shape[0]
    neg_count = neg_owner.shape[1]
    owners = lax.axis_size("dp")
    head_full = lax.all_gather(head_weight, "dp", axis=0, tiled=True)
    vocab_width = head_full.shape[1]
    logits = jnp.dot(hidden, head_full, preferred_element_type=jnp.float32) + head_bias[None, :]
    query_tokens = query_count * LQ
    query_rep, query_weights = soft_pool(
        logits[:query_tokens].reshape(query_count, LQ, vocab_width), lengths_mask(query_len, LQ)
    )
    passage_rep, passage_weights = soft_pool(
        logits[query_tokens:].reshape(query_count, LP, vocab_width), lengths_mask(passage_len, LP)
    )
    gathered = lax.all_gather(passage_rep, "dp", axis=0, tiled=True)
    passage_ids = neg_owner * query_count + neg_index
    neg_rows = jnp.take(gathered, passage_ids.reshape(-1), axis=0).reshape(
        query_count, neg_count, vocab_width
    )
    pos_part = jnp.sum(query_rep * passage_rep, axis=1)
    neg_part = jnp.sum(query_rep[:, None, :] * neg_rows, axis=2)
    positive, negative = lax.psum((pos_part, neg_part), "vocab")
    margin_error = positive[:, None] - negative - teacher
    grad_pos = jnp.sum(margin_error, axis=1)
    grad_neg = -margin_error
    query_grad = grad_pos[:, None] * passage_rep + jnp.sum(grad_neg[:, :, None] * neg_rows, axis=1)
    neg_terms = (grad_neg[:, :, None] * query_rep[:, None, :]).reshape(-1, vocab_width)
    scattered = jax.ops.segment_sum(
        neg_terms, passage_ids.reshape(-1), num_segments=owners * query_count
    )
    returned_grad = lax.psum_scatter(scattered, "dp", scatter_dimension=0, tiled=True)
    passage_grad = grad_pos[:, None] * query_rep + returned_grad
    relu_slope = (logits > 0).astype(jnp.float32) / (1.0 + jnp.maximum(logits, 0.0))
    d_query = (query_grad[:, None, :] * query_weights).reshape(-1, vocab_width)
    d_passage = (passage_grad[:, None, :] * passage_weights).reshape(-1, vocab_width)
    logit_grad = (jnp.concatenate([d_query, d_passage], axis=0) * relu_slope).astype(jnp.bfloat16)
    hidden_grad = lax.psum_scatter(
        lax.dot_general(
            logit_grad, head_full, (((1,), (1,)), ((), ())), preferred_element_type=jnp.float32
        ),
        "vocab",
        scatter_dimension=0,
        tiled=True,
    )
    return (margin_error, hidden_grad)


def solution(mesh):
    return jax.shard_map(
        per_device,
        mesh=mesh,
        in_specs=(
            P("dp", None),
            P("dp", "vocab"),
            P("vocab"),
            P("dp"),
            P("dp"),
            P("dp", None),
            P("dp", None),
            P("dp", None),
        ),
        out_specs=(P("dp", None), P(("dp", "vocab"), None)),
        check_vma=False,
    )
```

profile of v0, /device:TPU:0, one launch (start us, length us, event | category | flops | bytes accessed | tf_op | source)
XLA Modules:
  0.0 731.9 jit_solution(18147997512163754128)
XLA Ops:
  11.2 330.8 %all-gather.4.cloned.1.call-done = bf16[4096,8000]{0,1:T(8,128)(2,1)} async-done(((bf16[256,8000]{0,1:T(8,128)(2,1)}), bf16[4096,8000]{0,1:T(8,128)(2,1)}) %all-gather.4.cloned.1.call-update) | async-done | bytes 65536016 | tf_op jit(solution)/shard_map/all_gather | solution.py:31
  342.0 41.6 %convolution_add_fusion = f32[384,8000]{0,1:T(8,128)S(1)} fusion(bf16[384,4096]{1,0:T(8,128)(2,1)S(1)} %copy-done, bf16[4096,8000]{0,1:T(8,128)(2,1)} %all-gather.4.cloned.1.call-done, f32[8000]{0:T(1024)} %param.10), kind=kOutput, calls=%fused_computation.4 | convolution fusion | flops 25168896000 | bytes 81001728 | tf_op jit(solution)/shard_map/dot_general | solution.py:33
  383.6 4.3 fusion.10
  389.2 6.7 fusion.3
  395.9 5.6 copy.20
  401.6 8.9 %copy.21 = f32[256,8000]{1,0:T(8,128)} copy(f32[256,8000]{0,1:T(8,128)} %fusion.3) | data formatting | bytes 16384000 | tf_op jit(solution)/shard_map/exp | solution.py:15
  410.4 2.8 multiply_reduce_fusion.1
  413.2 4.3 multiply_reduce_fusion
  419.6 39.3 %all-gather.6.cloned.1.call-done = f32[16,4,8000]{2,1,0:T(4,128)} async-done(((f32[1,4,8000]{2,1,0:T(4,128)}), f32[16,4,8000]{2,1,0:T(4,128)}) %all-gather.6.cloned.1.call-update) | async-done | bytes 2048016 | tf_op jit(solution)/shard_map/all_gather | solution.py:41
  463.1 4.9 all-reduce.1
  468.3 3.7 scatter_custom_fusion
  473.3 3.9 div.72
  477.2 9.0 %copy.24 = f32[256,8000]{0,1:T(8,128)} copy(f32[256,8000]{1,0:T(8,128)} %bitcast.28) | data formatting | bytes 16384000 | tf_op jit(solution)/shard_map/div | solution.py:18
  486.2 2.4 div.69
  488.6 5.6 copy.22
  494.6 74.1 %all-reduce.4.cloned.1.call-done = f32[64,8000]{1,0:T(8,128)} async-done(((f32[64,8000]{1,0:T(8,128)}), f32[64,8000]{1,0:T(8,128)}) %all-reduce.4.cloned.1.call-update) | async-done | bytes 2048016
  569.8 3.9 mul.154
  573.7 8.9 %copy.25 = f32[256,8000]{0,1:T(8,128)} copy(f32[256,8000]{1,0:T(8,128)} %bitcast.29) | data formatting | bytes 16384000 | tf_op jit(solution)/shard_map/mul | solution.py:61
  582.6 2.4 mul.145
  585.0 5.6 copy.23
  590.6 13.2 %divide_multiply_fusion = f32[256,8000]{0,1:T(8,128)} fusion(f32[256,8000]{0,1:T(8,128)} %copy.25, f32[256,8000]{0,1:T(8,128)} %copy.24, f32[256]{0:T(256)S(1)} %reshape.193, f32[384,8000]{0,1:T(8,128)} %copy-done.2), kind=kLoop, calls=%fused_computation.10 | loop fusion | flops 10240000 | bytes 32769024 | tf_op jit(solution)/shard_map/mul | solution.py:61
  603.9 6.5 divide_multiply_fusion.1
  610.3 38.8 %fusion.4 = f32[384,4096]{1,0:T(8,128)} fusion(bf16[4096,8000]{0,1:T(8,128)(2,1)} %all-gather.4.cloned.1.call-done, f32[256,8000]{0,1:T(8,128)} %divide_multiply_fusion, f32[128,8000]{0,1:T(8,128)} %divide_multiply_fusion.1, f32[384,8000]{0,1:T(8,128)} %copy-done.2), kind=kOutput, calls=%fused_computation.11 | convolution fusion | flops 25190400000 | bytes 96403456 | tf_op jit(solution)/shard_map/dot_general | solution.py:64
  649.2 76.1 %reduce-scatter.2.cloned.1.call-done = f32[192,4096]{1,0:T(8,128)} async-done(((f32[384,4096]{1,0:T(8,128)}), f32[192,4096]{1,0:T(8,128)}) %reduce-scatter.2.cloned.1.call-update) | async-done | bytes 3145744 | tf_op jit(solution)/shard_map/reduce_scatter | solution.py:63
  (58 shorter events, 14.2 us)
Async XLA Ops:
  7.2 334.9 %copy-start = (bf16[384,4096]{1,0:T(8,128)(2,1)S(1)}, bf16[384,4096]{1,0:T(8,128)(2,1)}, u32[]{:S(2)}) copy-start(bf16[384,4096]{1,0:T(8,128)(2,1)} %param.8) | copy-start | bytes 9437188
  7.2 334.8 %all-gather.4.cloned.1.call-start = ((), (), s32[]{:S(2)}) async-start(), calls=%async_computation.1 | async-start | bytes 69632000 | tf_op jit(solution)/shard_map/all_gather | solution.py:31
  7.9 450.9 %all-gather.6.cloned.1.call-start = ((), (), s32[]{:S(2)}) async-start(), calls=%async_computation.3 | async-start | bytes 2193408 | tf_op jit(solution)/shard_map/all_gather | solution.py:41
  383.6 5.6 copy-start.2
  410.4 8.1 %copy-start.9 = (s32[4,8]{1,0:T(4,128)S(1)}, s32[4,8]{1,0:T(4,128)}, u32[]{:S(2)}) copy-start(s32[4,8]{1,0:T(4,128)} %param.14) | copy-start | bytes 388
  410.4 8.1 %copy-start.10 = (s32[4,8]{1,0:T(4,128)S(1)}, s32[4,8]{1,0:T(4,128)}, u32[]{:S(2)}) copy-start(s32[4,8]{1,0:T(4,128)} %param.13) | copy-start | bytes 388
  413.2 6.3 copy-start.5
  417.5 50.5 %copy-start.8 = (f32[4,8]{1,0:T(4,128)S(1)}, f32[4,8]{1,0:T(4,128)}, u32[]{:S(2)}) copy-start(f32[4,8]{1,0:T(4,128)} %param.15) | copy-start | bytes 388
  418.5 150.2 %all-reduce.4.cloned.1.call-start = ((), (), s32[]{:S(2)}) async-start(), calls=%async_computation.4 | async-start | bytes 4128768
  460.9 11.3 %copy-start.11 = (u32[32]{0:T(128)S(1)}, u32[32]{0:T(128)}, u32[]{:S(2)}) copy-start(u32[32]{0:T(128)} %constant.40) | copy-start | bytes 388
  468.2 18.0 %copy-start.7 = (f32[4,8]{1,0:T(4,128)}, f32[4,8]{1,0:T(4,128)S(1)}, u32[]{:S(2)}) copy-start(f32[4,8]{1,0:T(4,128)S(1)} %get-tuple-element.5) | copy-start | bytes 388
  472.0 253.3 %reduce-scatter.2.cloned.1.call-start = ((), (), s32[]{:S(2)}) async-start(), calls=%async_computation.2 | async-start | bytes 9437184 | tf_op jit(solution)/shard_map/reduce_scatter | solution.py:63
  477.2 9.0 %copy-start.6 = (f32[4,8000]{1,0:T(4,128)S(1)}, f32[4,8000]{1,0:T(4,128)}, u32[]{:S(2)}) copy-start(f32[4,8000]{1,0:T(4,128)} %copy-done.5) | copy-start | bytes 384004
  590.6 13.2 %copy-start.3 = (f32[128,8000]{0,1:T(8,128)S(1)}, f32[128,8000]{0,1:T(8,128)}, u32[]{:S(2)}) copy-start(f32[128,8000]{0,1:T(8,128)} %copy.22) | copy-start | bytes 12288004
  590.6 13.2 %copy-start.4 = (f32[128,8000]{0,1:T(8,128)S(1)}, f32[128,8000]{0,1:T(8,128)}, u32[]{:S(2)}) copy-start(f32[128,8000]{0,1:T(8,128)} %copy.23) | copy-start | bytes 12288004
  610.3 115.0 %copy-start.1 = (bf16[384,4096]{1,0:T(8,128)(2,1)S(1)}, bf16[384,4096]{1,0:T(8,128)(2,1)}, u32[]{:S(2)}) copy-start(bf16[384,4096]{1,0:T(8,128)(2,1)} %param.8) | copy-start | bytes 9437188
Sparse Core Ops, SparseCore 0:
  9.5 332.4 all-gather.3
  418.6 40.1 all-gather.5
  472.1 96.5 all-reduce.3
  649.3 75.9 reduce-scatter.1
where the time goes:
time: 733 us; the launch traced here: 732 us
  waiting for transfers between devices  521 us (71%)
  matrix products  80.4 us (11%)
  local copies, waits for them, and re-layouts  61.7 us (8%)
  other arithmetic  49.2 us (7%)
  between operations  14.5 us (2%)
    all_gather x1, waiting for transfers between devices, per_device(): head_full = lax.all_gather(head_weight, 'dp', axis=0, tiled=True)  331 us
    reduce_scatter x1, waiting for transfers between devices, per_device(): lax.psum_scatter(lax.dot_general(logit_grad, head_full, (((1,), (1,)), ((...  76.1 us
    unnamed x5, waiting for transfers between devices  74.8 us
    dot_general x1, matrix products, per_device(): jnp.dot(hidden, head_full, preferred_element_type=jnp.float32)  41.6 us
    all_gather x1, waiting for transfers between devices, per_device(): gathered = lax.all_gather(passage_rep, 'dp', axis=0, tiled=True)  39.3 us
    dot_general x1, matrix products, per_device(): lax.dot_general(logit_grad, head_full, (((1,), (1,)), ((), ())), preferre...  38.8 us
    div x4, local copies, waits for them, and re-layouts, soft_pool(): return (TAU * jnp.log(summed / valid_count), weights / summed[:, None, :])  20.9 us
  transfers between devices with their start and end apart: 4, of which 4 were waited for; matrix products, arithmetic and copies ran while one was open for 4% of the time, Pallas kernels for 0%

commit v1 on v0

--- a/solution.py
+++ b/solution.py
@@ -1,6 +1,8 @@
 import jax
 import jax.numpy as jnp
 from jax import lax
+from jax.experimental import pallas as pl
+from jax.experimental.pallas import tpu as pltpu
 from jax.sharding import PartitionSpec as P
 
 LQ = 32
@@ -8,6 +10,23 @@
 
 
 TAU = 0.05
+AXES = ("dp", "vocab")
+F32 = jnp.float32
+BF16 = jnp.bfloat16
+X, CORE, Y, ZLO, ZHI = 1, 2, 4, 8, 16
+ORDER = (0, 4, 8, 12, 2, 6, 10, 14, 1, 5, 9, 13, 3, 7, 11, 15)
+CHUNKS = (256,) + (512,) * 7 + (160,)
+NEAR = {0: (0,), 1: (1, 2), 3: (3, 4), 5: (5, 6), 7: (7, 8)}
+HIDDEN = (2, 4)
+TABLE = {0: ZLO, 1: ZHI, 6: Y, 8: CORE}
+EARLY = {10: ZHI, 11: Y, 12: CORE}
+EARLY_GROUPS = 4
+GROUPS = ((0,), (1, 2), (3,), (4,), (5,), (6,), (7,), (8,))
+PACKED = (3, 5, 6, 7, 8, 9, 10, 11)
+MOVED = (4, 6, 7, 8, 9, 10, 10, 11)
+COMPUTED = (6, 7, 8, 9, 10, 11, 11, 12)
+HIGHEST = lax.Precision.HIGHEST
+NO_COST = pl.CostEstimate(flops=0, bytes_accessed=0, transcendentals=0)
 
 
 def soft_pool(token_logits, token_mask):
@@ -22,7 +41,7 @@
     return (jnp.arange(span)[None, :] < lengths[:, None]).astype(jnp.float32)
 
 
-def per_device(
+def any_mesh(
     hidden, head_weight, head_bias, query_len, passage_len, neg_owner, neg_index, teacher
 ):
     query_count = neg_owner.shape[0]
@@ -71,9 +90,509 @@
     return (margin_error, hidden_grad)
 
 
+def in_hbm(*arrays):
+    return [pltpu.with_memory_space_constraint(a, pltpu.HBM) for a in arrays]
+
+
+def in_vmem(array):
+    return pltpu.with_memory_space_constraint(array, pltpu.VMEM)
+
+
+def swap(array, bits):
+    return lax.ppermute(array, AXES, [(i, i ^ bits) for i in range(32)])
+
+
+def arrange(places, hidden, other):
+    rows, width = hidden.shape
+    block = width // 16
+    step = 128
+    n = rows // step
+
+    def kernel(places, a, b, out):
+        def put(source):
+            for k in range(16):
+                lanes = pl.ds(pl.multiple_of(places[k] * block, block), block)
+                out[:, k * block : (k + 1) * block] = source[:, lanes]
+
+        own = places[0] // 4 % 2
+        here = pl.program_id(0) // n == own
+
+        @pl.when(here)
+        def _():
+            put(a)
+
+        @pl.when(jnp.logical_not(here))
+        def _():
+            put(b)
+
+    def at(turn):
+        def index(i, places):
+            first = (places[0] // 4 + turn) % 2 * n
+            return jnp.clip(i - first, 0, n - 1), 0
+
+        return pl.BlockSpec((step, width), index)
+
+    return pl.pallas_call(
+        kernel,
+        grid_spec=pltpu.PrefetchScalarGridSpec(
+            num_scalar_prefetch=1,
+            grid=(2 * n,),
+            in_specs=[at(0), at(1)],
+            out_specs=pl.BlockSpec((step, width), lambda i, places: (i, 0)),
+        ),
+        out_shape=pltpu.VMEM((2 * rows, width), hidden.dtype),
+        compiler_params=pltpu.CompilerParams(vmem_limit_bytes=40 * 2**20),
+        cost_estimate=NO_COST,
+        name="arrange",
+    )(places, hidden, other)
+
+
+def pack(groups):
+    n = len(groups)
+    width = groups[0][0].shape[1]
+    heights = [group[0].shape[0] for group in groups]
+    step = 128 if all(h % 128 == 0 for h in heights) else heights[0]
+    ends = [sum(heights[: i + 1]) // step for i in range(n)]
+    firsts = [0] + ends[:-1]
+
+    def kernel(*refs):
+        out = refs[-1]
+        for i in range(n):
+
+            @pl.when((pl.program_id(0) >= firsts[i]) & (pl.program_id(0) < ends[i]))
+            def _():
+                for k in range(4):
+                    out[:, k * width : (k + 1) * width] = refs[4 * i + k][...]
+
+    specs = []
+    for i in range(n):
+        last = heights[i] // step - 1
+        specs += [
+            pl.BlockSpec((step, width), lambda r, i=i, last=last: (jnp.clip(r - firsts[i], 0, last), 0))
+        ] * 4
+    return pl.pallas_call(
+        kernel,
+        grid=(ends[-1],),
+        in_specs=specs,
+        out_specs=pl.BlockSpec((step, 4 * width), lambda r: (r, 0)),
+        out_shape=pltpu.HBM((sum(heights), 4 * width), BF16),
+        compiler_params=pltpu.CompilerParams(vmem_limit_bytes=40 * 2**20),
+        cost_estimate=NO_COST,
+        name="pack",
+    )(*in_hbm(*[a for group in groups for a in group]))
+
+
+def forward(lens, rows, near, across, bias, slopes, start):
+    tokens, depth = rows.shape
+    wide, deep = near.shape
+    tile = 256
+    tiles = -(-wide // tile)
+    count = lens.shape[0] // 4
+    spans = [LQ] * count + [LP] * count
+
+    def kernel(lens, rows, near, across, bias, *refs):
+        slope, reps = refs[-2:]
+        by_rows = (((1,), (1,)), ((), ()))
+        logits = (
+            lax.dot_general(rows[:, :deep], near[...], by_rows, preferred_element_type=F32)
+            + lax.dot_general(rows[:, deep:], across[...], by_rows, preferred_element_type=F32)
+            + bias[...]
+        )
+        if wide % tile:
+            lanes = pl.program_id(0) * tile + lax.broadcasted_iota(jnp.int32, logits.shape, 1)
+            logits = jnp.where(lanes < wide, logits, -1.0)
+        at = 0
+        for b in range(2):
+            for i, span in enumerate(spans):
+                x = logits[at : at + span]
+                length = lens[b * 2 * count + i]
+                grown = 1.0 + jnp.maximum(x, 0.0)
+                p2 = grown * grown
+                p4 = p2 * p2
+                p8 = p4 * p4
+                valid = lax.broadcasted_iota(jnp.int32, (span, tile), 0) < length
+                p19 = jnp.where(valid, p8 * p8 * (p2 * grown), 0.0)
+                summed = jnp.sum(p19 * grown, axis=0, keepdims=True)
+                rep = TAU * jnp.log(summed / length.astype(F32))
+                reps[i // count, pl.ds(b * count + i % count, 1), :] = rep
+                slope[0, at : at + span, :] = jnp.where(x > 0, p19, 0.0) * (1.0 / summed)
+                at += span
+
+    first = start // tile
+    old = [] if slopes is None else [slopes]
+    return pl.pallas_call(
+        kernel,
+        grid_spec=pltpu.PrefetchScalarGridSpec(
+            num_scalar_prefetch=1,
+            grid=(tiles,),
+            in_specs=[
+                pl.BlockSpec(memory_space=pltpu.VMEM),
+                pl.BlockSpec((tile, deep), lambda c, lens: (c, 0)),
+                pl.BlockSpec((tile, deep), lambda c, lens: (c, 0)),
+                pl.BlockSpec((1, tile), lambda c, lens: (0, first + c)),
+            ]
+            + [pl.BlockSpec(memory_space=pl.ANY)] * len(old),
+            out_specs=[
+                pl.BlockSpec((1, tokens, tile), lambda c, lens: (first + c, 0, 0)),
+                pl.BlockSpec((2, 2 * count, tile), lambda c, lens: (0, 0, c)),
+            ],
+        ),
+        out_shape=[
+            pltpu.HBM((bias.shape[1] // tile, tokens, tile), F32),
+            jax.ShapeDtypeStruct((2, 2 * count, tiles * tile), F32),
+        ],
+        input_output_aliases={5: 0} if old else {},
+        compiler_params=pltpu.CompilerParams(vmem_limit_bytes=40 * 2**20),
+        cost_estimate=NO_COST,
+        name=f"forward{start}",
+    )(lens, in_vmem(rows), *in_hbm(near, across), bias, *in_hbm(*old))
+
+
+def margins(parts, id_place, teachers, slopes, early, late):
+    tiles, tokens, tile = slopes.shape
+    queries, neg_count = teachers.shape
+    pair = early.shape[1] // 8
+    split_at = early.shape[2] // tile
+
+    def kernel(s0, s1, s2, s3, ids, teach, slope, early, late, margin, grad, coeff, coeff_t):
+        step = pl.program_id(0)
+
+        @pl.when(step == 0)
+        def _():
+            score = (s0[...] + s1[...]) + (s2[...] + s3[...])
+            lanes = lax.broadcasted_iota(jnp.int32, score.shape, 1)
+            eye = lax.broadcasted_iota(jnp.int32, score.shape, 0) == lanes
+            positive = jnp.sum(jnp.where(eye, score, 0.0), axis=1, keepdims=True)
+            total = jnp.zeros_like(score)
+            grad_pos = jnp.zeros_like(positive)
+            for k in range(neg_count):
+                chosen = ids[:, k : k + 1] == lanes
+                negative = jnp.sum(jnp.where(chosen, score, 0.0), axis=1, keepdims=True)
+                error = positive - negative - teach[:, k : k + 1]
+                margin[:, k : k + 1] = error
+                total = total - jnp.where(chosen, error, 0.0)
+                grad_pos = grad_pos + error
+            total = total + jnp.where(eye, grad_pos, 0.0)
+            coeff[...] = total
+            coeff_t[...] = total.T
+
+        def fill(reps):
+            grad_q = jnp.dot(coeff[:pair], reps[1], precision=HIGHEST, preferred_element_type=F32)
+            grad_p = jnp.dot(coeff_t[:pair], reps[0], precision=HIGHEST, preferred_element_type=F32)
+            at = 0
+            for b in range(2):
+                for span, part in ((LQ, grad_q), (LP, grad_p)):
+                    for i in range(pair // 2):
+                        row = b * (pair // 2) + i
+                        grad[at : at + span, :] = (
+                            slope[0, at : at + span, :] * part[row : row + 1]
+                        ).astype(BF16)
+                        at += span
+
+        @pl.when(step < split_at)
+        def _():
+            fill(early)
+
+        @pl.when(step >= split_at)
+        def _():
+            fill(late)
+
+    square = pl.BlockSpec((queries, queries), lambda c: (0, 0))
+    listed = pl.BlockSpec((queries, neg_count), lambda c: (0, 0))
+    return pl.pallas_call(
+        kernel,
+        grid=(tiles,),
+        in_specs=[square] * 4
+        + [listed] * 2
+        + [
+            pl.BlockSpec((1, tokens, tile), lambda c: (c, 0, 0)),
+            pl.BlockSpec((2, queries, tile), lambda c: (0, 0, jnp.minimum(c, split_at - 1))),
+            pl.BlockSpec((2, queries, tile), lambda c: (0, 0, jnp.maximum(c - split_at, 0))),
+        ],
+        out_specs=[listed, pl.BlockSpec((tokens, tile), lambda c: (0, c))],
+        out_shape=[
+            jax.ShapeDtypeStruct((queries, neg_count), F32),
+            pltpu.VMEM((tokens, tiles * tile), BF16),
+        ],
+        scratch_shapes=[pltpu.VMEM((queries, queries), F32)] * 2,
+        compiler_params=pltpu.CompilerParams(vmem_limit_bytes=40 * 2**20),
+        name="margins",
+    )(*parts, id_place, teachers, *in_hbm(slopes), early, late)
+
+
+def back_piece(place, grads, heads, piece, pieces):
+    n = len(heads)
+    rows, block = grads.shape[0], heads[0].shape[1] // 8
+    steps = 16 // pieces
+    half = rows // 4
+
+    def kernel(place, grad, *refs):
+        heads, (send_x, keep_x, send_z, keep_z, total) = refs[:n], refs[n:]
+        sums, start = None, 0
+        for head in heads:
+            wide = head.shape[0]
+            part = jnp.dot(grad[:, start : start + wide], head[...], preferred_element_type=F32)
+            sums = part if sums is None else sums + part
+            start += wide
+        total[...] = sums
+        zlo, x = place[0], place[1]
+
+        def rows_of(z, x):
+            return total[pl.ds((2 * z + x) * half, half), :]
+
+        @pl.when(pl.program_id(0) < steps // 2)
+        def _():
+            keep_x[0], keep_x[1] = rows_of(zlo, x), rows_of(1 - zlo, x)
+            send_x[0] = rows_of(zlo, 1 - x).astype(BF16)
+            send_x[1] = rows_of(1 - zlo, 1 - x).astype(BF16)
+
+        @pl.when(pl.program_id(0) >= steps // 2)
+        def _():
+            keep_z[0], keep_z[1] = rows_of(zlo, x), rows_of(zlo, 1 - x)
+            send_z[0] = rows_of(1 - zlo, x).astype(BF16)
+            send_z[1] = rows_of(1 - zlo, 1 - x).astype(BF16)
+
+    some = [
+        pl.BlockSpec((h.shape[0], block), lambda d, place: (0, piece % 2 * steps + d))
+        for h in heads
+    ]
+    last = steps // 2 - 1
+    by_x = pl.BlockSpec(
+        (2, half, block), lambda d, place: (0, 0, jnp.minimum(d, last) ^ place[0])
+    )
+    by_z = pl.BlockSpec(
+        (2, half, block), lambda d, place: (0, 0, jnp.maximum(d - last - 1, 0) ^ place[0])
+    )
+    shape = (2, half, steps // 2 * block)
+    return pl.pallas_call(
+        kernel,
+        grid_spec=pltpu.PrefetchScalarGridSpec(
+            num_scalar_prefetch=1,
+            grid=(steps,),
+            in_specs=[pl.BlockSpec(memory_space=pltpu.VMEM)] + some,
+            out_specs=[by_x, by_x, by_z, by_z],
+            scratch_shapes=[pltpu.VMEM((rows, block), F32)],
+        ),
+        out_shape=[pltpu.HBM(shape, t) for t in (BF16, F32, BF16, F32)],
+        compiler_params=pltpu.CompilerParams(vmem_limit_bytes=40 * 2**20),
+        cost_estimate=pl.CostEstimate(
+            flops=2 * rows * grads.shape[1] * steps * block,
+            bytes_accessed=2 * grads.shape[1] * steps * block + 3 * rows * steps * block,
+            transcendentals=0,
+        ),
+        name=f"back{piece}",
+    )(place, in_vmem(grads), *in_hbm(*heads))
+
+
+def finish(places, pairs):
+    count = len(pairs)
+    rows, width = pairs[0][0].shape
+    blocks = 16 // count
+    block = width // blocks
+    step = 32
+
+    def kernel(places, *refs):
+        out = refs[-1]
+        for i in range(count):
+            for k in range(blocks):
+                cols = slice(k * block, (k + 1) * block)
+                lanes = pl.ds(pl.multiple_of(places[i * blocks + k] * block, block), block)
+                out[:, lanes] = refs[2 * i][:, cols] + refs[2 * i + 1][:, cols].astype(F32)
+
+    return pl.pallas_call(
+        kernel,
+        grid_spec=pltpu.PrefetchScalarGridSpec(
+            num_scalar_prefetch=1,
+            grid=(rows // step,),
+            in_specs=[pl.BlockSpec((step, width), lambda r, places: (r, 0))] * (2 * count),
+            out_specs=pl.BlockSpec((step, 16 * block), lambda r, places: (r, 0)),
+        ),
+        out_shape=jax.ShapeDtypeStruct((rows, 16 * block), F32),
+        compiler_params=pltpu.CompilerParams(vmem_limit_bytes=40 * 2**20),
+        name="finish",
+    )(places, *[a for pair in pairs for a in pair])
+
+
+def by_squares(
+    hidden, head_weight, head_bias, query_len, passage_len, neg_owner, neg_index, teacher
+):
+    count, neg_count = neg_owner.shape
+    tokens, width = hidden.shape
+    depth, columns = head_weight.shape
+    share = columns // 2
+    padded = -(-share // 256) * 256
+    n = len(CHUNKS)
+    starts = [sum(CHUNKS[:j]) for j in range(n)]
+    me = lax.axis_index("dp")
+    x = lax.axis_index("vocab")
+    zlo = (me >> 2) & 1
+    place = jnp.stack([zlo, x]).astype(jnp.int32)
+    blocks = me ^ jnp.array(ORDER, jnp.int32)
+    head = head_weight.T
+    bias = jnp.pad(
+        lax.dynamic_slice(head_bias, (zlo * share,), (share,)),
+        (0, padded - share),
+        constant_values=-1.0,
+    )[None, :]
+    half, piece = tokens // 2, tokens // 2 // len(HIDDEN)
+
+    live = {}
+
+    def columns_of(chunks, low):
+        first, size = starts[chunks[0]], sum(CHUNKS[c] for c in chunks)
+        return lax.dynamic_slice(head, (low * share + first, 0), (size, depth))
+
+    for k, chunks in NEAR.items():
+        live["given", k] = columns_of(chunks, 1 - zlo)
+    for i, k in enumerate(HIDDEN):
+        live["hidden", k] = lax.dynamic_slice(hidden, (x * half + i * piece, 0), (piece, width))
+    table = jnp.concatenate(
+        [
+            (neg_owner * count + neg_index).astype(F32),
+            teacher,
+            query_len[:, None].astype(F32),
+            passage_len[:, None].astype(F32),
+        ],
+        axis=1,
+    )
+
+    def near_of(j):
+        for k, chunks in NEAR.items():
+            if j in chunks:
+                first = starts[j] - starts[chunks[0]]
+                return live["near", k][first : first + CHUNKS[j]]
+
+    def beside(j):
+        return jnp.concatenate([columns_of((j,), zlo), near_of(j)], axis=1)
+
+    def all_reps(own, bits):
+        return jnp.concatenate([own, swap(own, bits)], axis=1)
+
+    rows = lens = slopes = None
+    rounds = max(COMPUTED)
+    for k in range(rounds + 1):
+        sent = {}
+        if 0 <= k - 1 < n:
+            j = k - 1
+            if ("two", j) not in live:
+                live["two", j] = beside(j)
+            sent["far", j] = swap(live["two", j], ZHI)
+            sent["side", j] = swap(live["two", j], Y)
+        if 0 <= k - 2 < n:
+            sent["beyond", k - 2] = swap(live["far", k - 2], Y)
+        if k in NEAR:
+            sent["near", k] = swap(live["given", k], ZLO)
+        if k in HIDDEN:
+            sent["from_z", k] = swap(live["hidden", k], ZLO)
+        if k - 1 in HIDDEN:
+            sent["from_x", k - 1] = swap(live["from_z", k - 1], X)
+        for g in range(len(GROUPS)):
+            if k == PACKED[g]:
+                sent["quads", g] = pack(
+                    [[live[name, j] for name in ("two", "far", "side", "beyond")] for j in GROUPS[g]]
+                )
+            if k == MOVED[g]:
+                quads = sent if k == PACKED[g] else live
+                sent["across", g] = swap(quads["quads", g], CORE)
+        if k in TABLE:
+            came = swap(table, TABLE[k])
+            both = [table, came]
+            if TABLE[k] == ZLO:
+                both = [jnp.where(zlo == 0, table, came), jnp.where(zlo == 0, came, table)]
+            sent["table"] = jnp.concatenate(both)
+        if k == max(HIDDEN) + 2:
+            by_z, by_x = (
+                jnp.concatenate([live[name, i] for i in HIDDEN]) for name in ("from_z", "from_x")
+            )
+            other = jnp.concatenate(
+                [jnp.where(x == 0, by_z, by_x), jnp.where(x == 0, by_x, by_z)]
+            )
+            rows = arrange(blocks, hidden, other)
+            pair_lens = table[: 2 * count, 2 * neg_count :].astype(jnp.int32)
+            lens = pair_lens.reshape(2, count, 2).transpose(0, 2, 1).reshape(-1)
+        for g in range(len(GROUPS)):
+            if k == COMPUTED[g]:
+                first = starts[GROUPS[g][0]]
+                slopes, sent["reps", g] = forward(
+                    lens, rows, live["quads", g], live["across", g], bias, slopes, first
+                )
+        if k in EARLY:
+            own = live.get("early")
+            if own is None:
+                own = jnp.concatenate([live["reps", g] for g in range(EARLY_GROUPS)], axis=2)
+            sent["early"] = all_reps(own, EARLY[k])
+        live.update(sent)
+        if k == rounds:
+            break
+        held = list(sent)
+        if any(k in chunks[1:] for chunks in NEAR.values()):
+            live["two", k] = beside(k)
+            held.append(("two", k))
+        held += [key for key in (("given", k + 1), ("hidden", k + 1)) if key in live]
+        live.update(zip(held, lax.optimization_barrier([live[key] for key in held])))
+        table = live["table"]
+    ids = table[:, :neg_count].astype(jnp.int32)
+    teachers = table[:, neg_count : 2 * neg_count]
+    owner = ids // count
+    order = jnp.array(ORDER[::2], jnp.int32)
+    group = jnp.sum(
+        jnp.where(((owner ^ me) & ~4)[:, :, None] == order, jnp.arange(8, dtype=jnp.int32), 0),
+        axis=2,
+    )
+    id_place = (group * 2 + ((owner >> 2) & 1)) * count + ids % count
+
+    early = live["early"]
+    late = jnp.concatenate([live["reps", g] for g in range(EARLY_GROUPS, len(GROUPS))], axis=2)
+    for bits in (ZHI, Y, CORE):
+        late = all_reps(late, bits)
+
+    def scores(reps):
+        return lax.dot_general(reps[0], reps[1], (((1,), (1,)), ((), ())), precision=HIGHEST)
+
+    part = scores(early) + scores(late)
+    margin_error, grads = margins(
+        (part, swap(part, X), swap(part, ZLO), swap(part, ZLO | X)),
+        id_place,
+        teachers,
+        slopes,
+        early,
+        late,
+    )
+
+    pieces = 4
+    pairs, first = [], [None] * pieces
+
+    def second(i):
+        (keep_x, came_x), (keep_z, came_z) = first[i]
+        mids = [
+            (keep[1] + came[1].astype(F32)).astype(BF16)
+            for keep, came in ((keep_x, came_x), (keep_z, came_z))
+        ]
+        nonlocal grads
+        mid_x, mid_z, grads = lax.optimization_barrier((*mids, grads))
+        pairs.append((keep_x[0] + came_x[0].astype(F32), swap(mid_x, ZLO)))
+        pairs.append((keep_z[0] + came_z[0].astype(F32), swap(mid_z, X)))
+
+    for i in range(pieces):
+        heads = [live["quads" if i < 2 else "across", g] for g in range(len(GROUPS))]
+        outs = back_piece(place, grads, heads, i, pieces)
+        send_x, keep_x, send_z, keep_z, grads = lax.optimization_barrier((*outs, grads))
+        first[i] = ((keep_x, swap(send_x, X)), (keep_z, swap(send_z, ZLO)))
+        if i >= 1:
+            second(i - 1)
+    second(pieces - 1)
+    places = []
+    for k in range(0, 16, 2):
+        base = (me & ~4) ^ ORDER[k]
+        places += [base, base | 4]
+    hidden_grad = finish(jnp.stack(places).astype(jnp.int32), pairs)
+    return (lax.dynamic_slice(margin_error, (zlo * count, 0), (count, neg_count)), hidden_grad)
+
+
 def solution(mesh):
+    square = mesh.shape["dp"] == 16 and mesh.shape["vocab"] == 2
     return jax.shard_map(
-        per_device,
+        by_squares if square else any_mesh,
         mesh=mesh,
         in_specs=(
             P("dp", None),

time: 733 us -> 418 us (0.57)
  waiting for transfers between devices: 521 us -> 140 us
  Pallas kernels: 0 us -> 156 us
  matrix products: 80.4 us -> 1.14 us
  starting transfers between devices: 0.16 us -> 77.9 us
  other arithmetic: 49.2 us -> 9.24 us
  local copies, waits for them, and re-layouts: 61.7 us -> 31.1 us
  between operations: 14.5 us -> 1.6 us
    all_gather x2 -> x0, waiting for transfers between devices: 370 us -> none  [the longest x1 331 us: per_device(): head_full = lax.all_gather(head_weight, 'dp', axis=0, tiled=True)]
    pallas_call x0 -> x23, Pallas kernels: none -> 156 us  [the longest x8 60.7 us: forward(): pl.pallas_call(kernel, grid_spec=pltpu.PrefetchScalarGridSpec(num_scalar_...]
    ppermute x0 -> x73, waiting for transfers between devices: none -> 140 us  [swap(): return lax.ppermute(array, AXES, [(i, i ^ bits) for i in range(32)])]
    dot_general x2, matrix products: 80.4 us -> 1.14 us  [scores(): lax.dot_general(reps[0], reps[1], (((1,), (1,)), ((), ())), precision=HIG...]
    ppermute x0 -> x73, starting transfers between devices: none -> 77.9 us  [swap(): return lax.ppermute(array, AXES, [(i, i ^ bits) for i in range(32)])]
    reduce_scatter x1 -> x0, waiting for transfers between devices: 76.1 us -> none  [per_device(): lax.psum_scatter(lax.dot_general(logit_grad, head_full, (((1,), (1,)), ((...]
    unnamed x5 -> x0, waiting for transfers between devices: 74.8 us -> none
    div x4 -> x0, local copies, waits for them, and re-layouts: 20.9 us -> none  [soft_pool(): return (TAU * jnp.log(summed / valid_count), weights / summed[:, None, :])]
  transfers between devices with their start and end apart: 4 -> 73, of which waited for: 4 -> 28; matrix products, arithmetic and copies ran while one was open for 4% -> 6% of each run, Pallas kernels for 0% -> 28%
where the time goes in v1:
time: 418 us; the launch traced here: 416 us
  Pallas kernels  156 us (37%)
  waiting for transfers between devices  140 us (33%)
  starting transfers between devices  77.9 us (19%)
  local copies, waits for them, and re-layouts  31.1 us (7%)
  other arithmetic  9.24 us (2%)
    ppermute x73, waiting for transfers between devices, swap(): return lax.ppermute(array, AXES, [(i, i ^ bits) for i in range(32)])  140 us
    ppermute x73, starting transfers between devices, swap(): return lax.ppermute(array, AXES, [(i, i ^ bits) for i in range(32)])  77.9 us
    pallas_call x8, Pallas kernels, forward(): pl.pallas_call(kernel, grid_spec=pltpu.PrefetchScalarGridSpec(num_scalar_...  60.7 us
    pallas_call x4, Pallas kernels, back_piece(): pl.pallas_call(kernel, grid_spec=pltpu.PrefetchScalarGridSpec(num_scalar_...  43.4 us
    pallas_call x8, Pallas kernels, pack(): pl.pallas_call(kernel, grid=(ends[-1],), in_specs=specs, out_specs=pl.Blo...  31.4 us
    unnamed x141, local copies, waits for them, and re-layouts  14.1 us
    pallas_call x1, Pallas kernels, margins(): pl.pallas_call(kernel, grid=(tiles,), in_specs=[square] * 4 + [listed] *...  13.6 us
    dynamic_slice x5, local copies, waits for them, and re-layouts, columns_of(): return lax.dynamic_slice(head, (low * share + first, 0), (size, depth))  8.65 us
  transfers between devices with their start and end apart: 73, of which 28 were waited for; matrix products, arithmetic and copies ran while one was open for 6% of the time, Pallas kernels for 28%

profile of v1, /device:TPU:0, one launch (start us, length us, event | category | flops | bytes accessed | tf_op | source)
XLA Modules:
  0.0 416.2 jit_solution(14014300156254613440)
XLA Ops:
  20.7 8.4 %collective-permute-done.5 = f32[8,18]{1,0:T(8,128)S(1)} collective-permute-done((f32[8,18]{1,0:T(8,128)S(1)}, f32[8,18]{1,0:T(8,128)S(1)}, u32[]{:S(2)}, u32[]{:S(2)}) %collective-permute-start.5) | collective-permute-done | bytes 608 | tf_op jit(solution)/shard_map/ppermute | solution.py:102
  37.5 15.2 %collective-permute-done.8.refs_3_ = bf16[256,512]{1,0:T(8,128)(2,1)S(1)} collective-permute-done((bf16[256,512]{1,0:T(8,128)(2,1)S(1)}, bf16[256,512]{1,0:T(8,128)(2,1)S(1)}, u32[]{:S(2)}, u32[]{:S(2)}) %collective-permute-start.8) | collective-permute-done | bytes 262176 | tf_op jit(solution)/shard_map/ppermute | solution.py:102
  69.0 15.4 %collective-permute-done.10.refs_5_ = bf16[512,512]{1,0:T(8,128)(2,1)S(1)} collective-permute-done((bf16[512,512]{1,0:T(8,128)(2,1)S(1)}, bf16[512,512]{1,0:T(8,128)(2,1)S(1)}, u32[]{:S(2)}, u32[]{:S(2)}) %collective-permute-start.10) | collective-permute-done | bytes 524320 | tf_op jit(solution)/shard_map/ppermute | solution.py:102
  94.0 21.9 %collective-permute-done.15.refs_1_ = bf16[512,512]{1,0:T(8,128)(2,1)} collective-permute-done((bf16[512,512]{1,0:T(8,128)(2,1)S(1)}, bf16[512,512]{1,0:T(8,128)(2,1)}, u32[]{:S(2)}, u32[]{:S(2)}) %collective-permute-start.15) | collective-permute-done | bytes 524320 | tf_op jit(solution)/shard_map/ppermute | solution.py:102
  125.8 7.2 %pack.9.near.refs_1_ = bf16[1024,2048]{1,0:T(8,128)(2,1)} custom-call(bf16[512,512]{1,0:T(8,128)(2,1)} %copy-done.15, bf16[512,512]{1,0:T(8,128)(2,1)} %copy-done.40, bf16[512,512]{1,0:T(8,128)(2,1)} %copy-done.41, bf16[512,512]{1,0:T(8,128)(2,1)} %copy-done.44, bf16[512,512]{1,0:T(8,128)(2,1)} %copy-done.16, bf16[512,512]{1,0:T(8,128)(2,1)} %copy-done.42, ...), custom_call_target="tpu_custom_call" | custom-call | tf_op jit(solution)/shard_map/pack/pallas_call | solution.py:173
  133.0 9.6 %collective-permute-done.20.refs_1_ = bf16[512,512]{1,0:T(8,128)(2,1)} collective-permute-done((bf16[512,512]{1,0:T(8,128)(2,1)}, bf16[512,512]{1,0:T(8,128)(2,1)}, u32[]{:S(2)}, u32[]{:S(2)}) %collective-permute-start.20) | collective-permute-done | bytes 524320 | tf_op jit(solution)/shard_map/ppermute | solution.py:102
  159.8 7.6 %forward0.1 = (f32[16,768,256]{2,1,0:T(8,128)}, f32[2,8,256]{2,1,0:T(8,128)S(1)}) custom-call(s32[16]{0:T(128)S(1)} %reshape.55.lens, bf16[768,4096]{1,0:T(8,128)(2,1)S(1)} %arrange.1.rows, bf16[256,2048]{1,0:T(8,128)(2,1)} %pack.8.near.refs_0_, bf16[256,2048]{1,0:T(8,128)(2,1)} %collective-permute-done.19.across.refs_0_, f32[1,4096]{1,0:T(1,128)S(1)} %bitcast.98), custom_call_target="tpu_custom_call" | custom-call | tf_op jit(solution)/shard_map/forward0/pallas_call | solution.py:223
  167.5 7.4 %collective-permute-done.25.refs_1_ = bf16[512,512]{1,0:T(8,128)(2,1)S(1)} collective-permute-done((bf16[512,512]{1,0:T(8,128)(2,1)S(1)}, bf16[512,512]{1,0:T(8,128)(2,1)S(1)}, u32[]{:S(2)}, u32[]{:S(2)}) %collective-permute-start.25) | collective-permute-done | bytes 524320 | tf_op jit(solution)/shard_map/ppermute | solution.py:102
  184.7 11.6 %forward256.1 = (f32[16,768,256]{2,1,0:T(8,128)}, f32[2,8,1024]{2,1,0:T(8,128)S(1)}) custom-call(s32[16]{0:T(128)S(1)} %reshape.55.lens, bf16[768,4096]{1,0:T(8,128)(2,1)S(1)} %arrange.1.rows, bf16[1024,2048]{1,0:T(8,128)(2,1)} %pack.9.near.refs_1_, bf16[1024,2048]{1,0:T(8,128)(2,1)} %collective-permute-done.28.across.refs_1_, ...), custom_call_target="tpu_custom_call", output_to_operand_aliasing={{0}: (5, {})} | custom-call | tf_op jit(solution)/shard_map/forward256/pallas_call | solution.py:223
  196.2 6.2 %collective-permute-done.30.refs_1_ = bf16[512,512]{1,0:T(8,128)(2,1)} collective-permute-done((bf16[512,512]{1,0:T(8,128)(2,1)S(1)}, bf16[512,512]{1,0:T(8,128)(2,1)}, u32[]{:S(2)}, u32[]{:S(2)}) %collective-permute-start.30) | collective-permute-done | bytes 524320 | tf_op jit(solution)/shard_map/ppermute | solution.py:102
  215.6 7.4 %forward1280.1 = (f32[16,768,256]{2,1,0:T(8,128)}, f32[2,8,512]{2,1,0:T(8,128)S(1)}) custom-call(s32[16]{0:T(128)S(1)} %reshape.55.lens, bf16[768,4096]{1,0:T(8,128)(2,1)S(1)} %copy-done.1, bf16[512,2048]{1,0:T(8,128)(2,1)} %pack.10.near.refs_2_, bf16[512,2048]{1,0:T(8,128)(2,1)} %copy-done.10, ...), custom_call_target="tpu_custom_call", output_to_operand_aliasing={{0}: (5, {})} | custom-call | tf_op jit(solution)/shard_map/forward1280/pallas_call | solution.py:223
  223.0 7.6 %collective-permute-done.35.refs_1_ = bf16[512,512]{1,0:T(8,128)(2,1)} collective-permute-done((bf16[512,512]{1,0:T(8,128)(2,1)S(1)}, bf16[512,512]{1,0:T(8,128)(2,1)}, u32[]{:S(2)}, u32[]{:S(2)}) %collective-permute-start.35) | collective-permute-done | bytes 524320 | tf_op jit(solution)/shard_map/ppermute | solution.py:102
  238.3 7.4 %forward1792.1 = (f32[16,768,256]{2,1,0:T(8,128)}, f32[2,8,512]{2,1,0:T(8,128)S(1)}) custom-call(s32[16]{0:T(128)S(1)} %reshape.55.lens, bf16[768,4096]{1,0:T(8,128)(2,1)S(1)} %copy-done.1, bf16[512,2048]{1,0:T(8,128)(2,1)} %pack.11.near.refs_3_, bf16[512,2048]{1,0:T(8,128)(2,1)} %copy-done.11, ...), custom_call_target="tpu_custom_call", output_to_operand_aliasing={{0}: (5, {})} | custom-call | tf_op jit(solution)/shard_map/forward1792/pallas_call | solution.py:223
  256.9 7.4 %forward2304.1 = (f32[16,768,256]{2,1,0:T(8,128)}, f32[2,8,512]{2,1,0:T(8,128)S(1)}) custom-call(s32[16]{0:T(128)S(1)} %reshape.55.lens, bf16[768,4096]{1,0:T(8,128)(2,1)S(1)} %copy-done.1, bf16[512,2048]{1,0:T(8,128)(2,1)} %pack.12.near.refs_4_, bf16[512,2048]{1,0:T(8,128)(2,1)} %copy-done.12, ...), custom_call_target="tpu_custom_call", output_to_operand_aliasing={{0}: (5, {})} | custom-call | tf_op jit(solution)/shard_map/forward2304/pallas_call | solution.py:223
  272.3 7.3 %forward2816.1 = (f32[16,768,256]{2,1,0:T(8,128)}, f32[2,8,512]{2,1,0:T(8,128)S(1)}) custom-call(s32[16]{0:T(128)S(1)} %reshape.55.lens, bf16[768,4096]{1,0:T(8,128)(2,1)S(1)} %copy-done.2, bf16[512,2048]{1,0:T(8,128)(2,1)} %pack.13.near.refs_5_, bf16[512,2048]{1,0:T(8,128)(2,1)} %copy-done.13, ...), custom_call_target="tpu_custom_call", output_to_operand_aliasing={{0}: (5, {})} | custom-call | tf_op jit(solution)/shard_map/forward2816/pallas_call | solution.py:223
  279.6 7.3 %forward3328.1 = (f32[16,768,256]{2,1,0:T(8,128)}, f32[2,8,512]{2,1,0:T(8,128)S(1)}) custom-call(s32[16]{0:T(128)S(1)} %reshape.55.lens, bf16[768,4096]{1,0:T(8,128)(2,1)S(1)} %copy-done.2, bf16[512,2048]{1,0:T(8,128)(2,1)} %pack.14.near.refs_6_, bf16[512,2048]{1,0:T(8,128)(2,1)} %copy-done.14, ...), custom_call_target="tpu_custom_call", output_to_operand_aliasing={{0}: (5, {})} | custom-call | tf_op jit(solution)/shard_map/forward3328/pallas_call | solution.py:223
  293.3 7.9 %collective-permute-done.51 = f32[2,8,1792]{2,1,0:T(8,128)S(1)} collective-permute-done((f32[2,8,1792]{2,1,0:T(8,128)S(1)}, f32[2,8,1792]{2,1,0:T(8,128)S(1)}, u32[]{:S(2)}, u32[]{:S(2)}) %collective-permute-start.51) | collective-permute-done | bytes 114720 | tf_op jit(solution)/shard_map/ppermute | solution.py:102
  302.1 6.8 %collective-permute-done.52 = f32[2,16,1792]{2,1,0:T(8,128)S(1)} collective-permute-done((f32[2,16,1792]{2,1,0:T(8,128)S(1)}, f32[2,16,1792]{2,1,0:T(8,128)S(1)}, u32[]{:S(2)}, u32[]{:S(2)}) %collective-permute-start.52) | collective-permute-done | bytes 229408 | tf_op jit(solution)/shard_map/ppermute | solution.py:102
  318.0 13.6 %margins.1 = (f32[64,8]{1,0:T(8,128)S(1)}, bf16[768,4096]{1,0:T(8,128)(2,1)S(1)}) custom-call(f32[64,64]{1,0:T(8,128)S(1)} %convolution_add_fusion.s0, f32[64,64]{1,0:T(8,128)S(1)} %collective-permute-done.54.s1, f32[64,64]{1,0:T(8,128)S(1)} %collective-permute-done.55.s2, f32[64,64]{1,0:T(8,128)S(1)} %collective-permute-done.56.s3, s32[64,8]{1,0:T(8,128)S(1)} %fusion.9.ids, ...), custom_call_target="tpu_custom_call" | custom-call | tf_op jit(solution)/shard_map/margins/pallas_call | solution.py:302
  331.6 10.8 %back0.1 = (bf16[2,192,512]{2,1,0:T(8,128)(2,1)}, f32[2,192,512]{2,1,0:T(8,128)}, bf16[2,192,512]{2,1,0:T(8,128)(2,1)}, f32[2,192,512]{2,1,0:T(8,128)}) custom-call(s32[2]{0:T(128)S(1)} %pad_add_fusion.place, bf16[768,4096]{1,0:T(8,128)(2,1)S(1)} %get-tuple-element.267.grad, bf16[256,2048]{1,0:T(8,128)(2,1)} %pack.8.near.refs_0_, ...), custom_call_target="tpu_custom_call" | custom-call | flops 6442450944 | bytes 10747904 | tf_op jit(solution)/shard_map/back0/pallas_call | solution.py:367
  345.4 11.0 %back1.1 = (bf16[2,192,512]{2,1,0:T(8,128)(2,1)}, f32[2,192,512]{2,1,0:T(8,128)}, bf16[2,192,512]{2,1,0:T(8,128)(2,1)}, f32[2,192,512]{2,1,0:T(8,128)}) custom-call(s32[2]{0:T(128)S(1)} %pad_add_fusion.place, bf16[768,4096]{1,0:T(8,128)(2,1)S(1)} %get-tuple-element.267.grad, bf16[256,2048]{1,0:T(8,128)(2,1)} %pack.8.near.refs_0_, ...), custom_call_target="tpu_custom_call" | custom-call | flops 6442450944 | bytes 10747904 | tf_op jit(solution)/shard_map/back1/pallas_call | solution.py:367
  360.9 10.7 %back2.1 = (bf16[2,192,512]{2,1,0:T(8,128)(2,1)}, f32[2,192,512]{2,1,0:T(8,128)}, bf16[2,192,512]{2,1,0:T(8,128)(2,1)}, f32[2,192,512]{2,1,0:T(8,128)}) custom-call(s32[2]{0:T(128)S(1)} %pad_add_fusion.place, bf16[768,4096]{1,0:T(8,128)(2,1)S(1)} %get-tuple-element.267.grad, bf16[256,2048]{1,0:T(8,128)(2,1)} %collective-permute-done.19.across.refs_0_, ...), custom_call_target="tpu_custom_call" | custom-call | flops 6442450944 | bytes 10747904 | tf_op jit(solution)/shard_map/back2/pallas_call | solution.py:367
  376.7 10.8 %back3.1 = (bf16[2,192,512]{2,1,0:T(8,128)(2,1)}, f32[2,192,512]{2,1,0:T(8,128)}, bf16[2,192,512]{2,1,0:T(8,128)(2,1)}, f32[2,192,512]{2,1,0:T(8,128)}) custom-call(s32[2]{0:T(128)S(1)} %pad_add_fusion.place, bf16[768,4096]{1,0:T(8,128)(2,1)S(1)} %get-tuple-element.267.grad, bf16[256,2048]{1,0:T(8,128)(2,1)} %collective-permute-done.19.across.refs_0_, ...), custom_call_target="tpu_custom_call" | custom-call | flops 6442450944 | bytes 10747904 | tf_op jit(solution)/shard_map/back3/pallas_call | solution.py:367
  390.2 7.7 %collective-permute-done.69 = bf16[2,192,512]{2,1,0:T(8,128)(2,1)S(1)} collective-permute-done((bf16[2,192,512]{2,1,0:T(8,128)(2,1)}, bf16[2,192,512]{2,1,0:T(8,128)(2,1)S(1)}, u32[]{:S(2)}, u32[]{:S(2)}) %collective-permute-start.69) | collective-permute-done | bytes 393248 | tf_op jit(solution)/shard_map/ppermute | solution.py:102
  (361 shorter events, 180.6 us)
Async XLA Ops:
  29.9 29.4 %collective-permute-start.9 = (bf16[96,4096]{1,0:T(8,128)(2,1)S(1)}, bf16[96,4096]{1,0:T(8,128)(2,1)S(1)}, u32[]{:S(2)}, u32[]{:S(2)}) collective-permute-start(bf16[96,4096]{1,0:T(8,128)(2,1)S(1)} %copy-done.36), channel_id=1, source_target_pairs={{0,8},{1,9},{2,10},{3,11},{4,12},{5,13},{6,14},{7,15},{8,0},{9,1},... | collective-permute-start | bytes 2359304 | tf_op jit(solution)/shard_map/ppermute | solution.py:102
  33.8 24.8 %collective-permute-start.6 = (bf16[512,512]{1,0:T(8,128)(2,1)S(1)}, bf16[512,512]{1,0:T(8,128)(2,1)S(1)}, u32[]{:S(2)}, u32[]{:S(2)}) collective-permute-start(bf16[512,512]{1,0:T(8,128)(2,1)S(1)} %pad_maximum_fusion.3.refs_0_), channel_id=1, source_target_pairs={{0,16},{1,17},{2,18},{3,19},{4,20},{5,21},{6,22},{7,23},{8,24},{9,... | collective-permute-start | bytes 1572872 | tf_op jit(solution)/shard_map/ppermute | solution.py:102
  59.5 26.2 %collective-permute-start.14 = (bf16[96,4096]{1,0:T(8,128)(2,1)S(1)}, bf16[96,4096]{1,0:T(8,128)(2,1)S(1)}, u32[]{:S(2)}, u32[]{:S(2)}) collective-permute-start(bf16[96,4096]{1,0:T(8,128)(2,1)S(1)} %collective-permute-done.9), channel_id=1, source_target_pairs={{0,1},{1,0},{2,3},{3,2},{4,5},{5,4},{6,7},{7,6},{8,9},{9,8},{10,11... | collective-permute-start | bytes 2359304 | tf_op jit(solution)/shard_map/ppermute | solution.py:102
  85.7 31.4 %collective-permute-start.19 = (bf16[256,2048]{1,0:T(8,128)(2,1)}, bf16[256,2048]{1,0:T(8,128)(2,1)}, u32[]{:S(2)}, u32[]{:S(2)}) collective-permute-start(bf16[256,2048]{1,0:T(8,128)(2,1)} %pack.8.near.refs_0_), channel_id=1, source_target_pairs={{0,2},{1,3},{2,0},{3,1},{4,6},{5,7},{6,4},{7,5},{8,10},{9,11},{10,... | collective-permute-start | bytes 3145736 | tf_op jit(solution)/shard_map/ppermute | solution.py:102
  86.6 30.4 %collective-permute-start.18 = (bf16[96,4096]{1,0:T(8,128)(2,1)S(1)}, bf16[96,4096]{1,0:T(8,128)(2,1)}, u32[]{:S(2)}, u32[]{:S(2)}) collective-permute-start(bf16[96,4096]{1,0:T(8,128)(2,1)S(1)} %copy-done.35), channel_id=1, source_target_pairs={{0,8},{1,9},{2,10},{3,11},{4,12},{5,13},{6,14},{7,15},{8,0},{9,1},... | collective-permute-start | bytes 2359304 | tf_op jit(solution)/shard_map/ppermute | solution.py:102
  88.1 27.7 %collective-permute-start.15 = (bf16[512,512]{1,0:T(8,128)(2,1)S(1)}, bf16[512,512]{1,0:T(8,128)(2,1)}, u32[]{:S(2)}, u32[]{:S(2)}) collective-permute-start(bf16[512,512]{1,0:T(8,128)(2,1)S(1)} %pad_maximum_fusion.5.refs_0_), channel_id=1, source_target_pairs={{0,16},{1,17},{2,18},{3,19},{4,20},{5,21},{6,22},{7,23},{8,24},{9,... | collective-permute-start | bytes 1572872 | tf_op jit(solution)/shard_map/ppermute | solution.py:102
  91.1 24.7 %collective-permute-start.16 = (bf16[512,512]{1,0:T(8,128)(2,1)S(1)}, bf16[512,512]{1,0:T(8,128)(2,1)S(1)}, u32[]{:S(2)}, u32[]{:S(2)}) collective-permute-start(bf16[512,512]{1,0:T(8,128)(2,1)S(1)} %pad_maximum_fusion.5.refs_0_), channel_id=1, source_target_pairs={{0,4},{1,5},{2,6},{3,7},{4,0},{5,1},{6,2},{7,3},{8,12},{9,13},{10,... | collective-permute-start | bytes 1572872 | tf_op jit(solution)/shard_map/ppermute | solution.py:102
  117.1 27.1 %collective-permute-start.24 = (bf16[96,4096]{1,0:T(8,128)(2,1)}, bf16[96,4096]{1,0:T(8,128)(2,1)}, u32[]{:S(2)}, u32[]{:S(2)}) collective-permute-start(bf16[96,4096]{1,0:T(8,128)(2,1)} %collective-permute-done.18), channel_id=1, source_target_pairs={{0,1},{1,0},{2,3},{3,2},{4,5},{5,4},{6,7},{7,6},{8,9},{9,8},{10,11... | collective-permute-start | bytes 2359304 | tf_op jit(solution)/shard_map/ppermute | solution.py:102
  117.7 24.9 %collective-permute-start.20 = (bf16[512,512]{1,0:T(8,128)(2,1)}, bf16[512,512]{1,0:T(8,128)(2,1)}, u32[]{:S(2)}, u32[]{:S(2)}) collective-permute-start(bf16[512,512]{1,0:T(8,128)(2,1)} %pad_maximum_fusion.6.refs_0_), channel_id=1, source_target_pairs={{0,16},{1,17},{2,18},{3,19},{4,20},{5,21},{6,22},{7,23},{8,24},{9,... | collective-permute-start | bytes 1572872 | tf_op jit(solution)/shard_map/ppermute | solution.py:102
  120.2 24.0 %collective-permute-start.21 = (bf16[512,512]{1,0:T(8,128)(2,1)}, bf16[512,512]{1,0:T(8,128)(2,1)}, u32[]{:S(2)}, u32[]{:S(2)}) collective-permute-start(bf16[512,512]{1,0:T(8,128)(2,1)} %pad_maximum_fusion.6.refs_0_), channel_id=1, source_target_pairs={{0,4},{1,5},{2,6},{3,7},{4,0},{5,1},{6,2},{7,3},{8,12},{9,13},{10,... | collective-permute-start | bytes 1572872 | tf_op jit(solution)/shard_map/ppermute | solution.py:102
  144.2 31.6 %collective-permute-start.28 = (bf16[1024,2048]{1,0:T(8,128)(2,1)}, bf16[1024,2048]{1,0:T(8,128)(2,1)}, u32[]{:S(2)}, u32[]{:S(2)}) collective-permute-start(bf16[1024,2048]{1,0:T(8,128)(2,1)} %pack.9.near.refs_1_), channel_id=1, source_target_pairs={{0,2},{1,3},{2,0},{3,1},{4,6},{5,7},{6,4},{7,5},{8,10},{9,11},{10,... | collective-permute-start | bytes 12582920 | tf_op jit(solution)/shard_map/ppermute | solution.py:102
  149.9 24.9 %collective-permute-start.25 = (bf16[512,512]{1,0:T(8,128)(2,1)S(1)}, bf16[512,512]{1,0:T(8,128)(2,1)S(1)}, u32[]{:S(2)}, u32[]{:S(2)}) collective-permute-start(bf16[512,512]{1,0:T(8,128)(2,1)S(1)} %pad_maximum_fusion.7.refs_0_), channel_id=1, source_target_pairs={{0,16},{1,17},{2,18},{3,19},{4,20},{5,21},{6,22},{7,23},{8,24},{9,... | collective-permute-start | bytes 1572872 | tf_op jit(solution)/shard_map/ppermute | solution.py:102
  150.5 24.3 %collective-permute-start.26 = (bf16[512,512]{1,0:T(8,128)(2,1)S(1)}, bf16[512,512]{1,0:T(8,128)(2,1)S(1)}, u32[]{:S(2)}, u32[]{:S(2)}) collective-permute-start(bf16[512,512]{1,0:T(8,128)(2,1)S(1)} %pad_maximum_fusion.7.refs_0_), channel_id=1, source_target_pairs={{0,4},{1,5},{2,6},{3,7},{4,0},{5,1},{6,2},{7,3},{8,12},{9,13},{10,... | collective-permute-start | bytes 1572872 | tf_op jit(solution)/shard_map/ppermute | solution.py:102
  175.8 26.7 %collective-permute-start.34 = (bf16[512,2048]{1,0:T(8,128)(2,1)S(1)}, bf16[512,2048]{1,0:T(8,128)(2,1)S(1)}, u32[]{:S(2)}, u32[]{:S(2)}) collective-permute-start(bf16[512,2048]{1,0:T(8,128)(2,1)S(1)} %copy-done.7), channel_id=1, source_target_pairs={{0,2},{1,3},{2,0},{3,1},{4,6},{5,7},{6,4},{7,5},{8,10},{9,11},{10,... | collective-permute-start | bytes 6291464 | tf_op jit(solution)/shard_map/ppermute | solution.py:102
  175.9 26.6 %collective-permute-start.30 = (bf16[512,512]{1,0:T(8,128)(2,1)S(1)}, bf16[512,512]{1,0:T(8,128)(2,1)}, u32[]{:S(2)}, u32[]{:S(2)}) collective-permute-start(bf16[512,512]{1,0:T(8,128)(2,1)S(1)} %pad_maximum_fusion.8.refs_0_), channel_id=1, source_target_pairs={{0,16},{1,17},{2,18},{3,19},{4,20},{5,21},{6,22},{7,23},{8,24},{9,... | collective-permute-start | bytes 1572872 | tf_op jit(solution)/shard_map/ppermute | solution.py:102
  176.7 25.7 %collective-permute-start.31 = (bf16[512,512]{1,0:T(8,128)(2,1)S(1)}, bf16[512,512]{1,0:T(8,128)(2,1)S(1)}, u32[]{:S(2)}, u32[]{:S(2)}) collective-permute-start(bf16[512,512]{1,0:T(8,128)(2,1)S(1)} %pad_maximum_fusion.8.refs_0_), channel_id=1, source_target_pairs={{0,4},{1,5},{2,6},{3,7},{4,0},{5,1},{6,2},{7,3},{8,12},{9,13},{10,... | collective-permute-start | bytes 1572872 | tf_op jit(solution)/shard_map/ppermute | solution.py:102
  178.1 24.4 %collective-permute-start.32 = (bf16[512,512]{1,0:T(8,128)(2,1)S(1)}, bf16[512,512]{1,0:T(8,128)(2,1)S(1)}, u32[]{:S(2)}, u32[]{:S(2)}) collective-permute-start(bf16[512,512]{1,0:T(8,128)(2,1)S(1)} %collective-permute-done.25.refs_1_), channel_id=1, source_target_pairs={{0,4},{1,5},{2,6},{3,7},{4,0},{5,1},{6,2},{7,3},{8,12},{9,13},{10,... | collective-permute-start | bytes 1572872 | tf_op jit(solution)/shard_map/ppermute | solution.py:102
  203.8 27.2 %collective-permute-start.38 = (bf16[512,2048]{1,0:T(8,128)(2,1)}, bf16[512,2048]{1,0:T(8,128)(2,1)S(1)}, u32[]{:S(2)}, u32[]{:S(2)}) collective-permute-start(bf16[512,2048]{1,0:T(8,128)(2,1)} %pack.11.near.refs_3_), channel_id=1, source_target_pairs={{0,2},{1,3},{2,0},{3,1},{4,6},{5,7},{6,4},{7,5},{8,10},{9,11},{10,... | collective-permute-start | bytes 6291464 | tf_op jit(solution)/shard_map/ppermute | solution.py:102
  203.9 26.6 %collective-permute-start.35 = (bf16[512,512]{1,0:T(8,128)(2,1)S(1)}, bf16[512,512]{1,0:T(8,128)(2,1)}, u32[]{:S(2)}, u32[]{:S(2)}) collective-permute-start(bf16[512,512]{1,0:T(8,128)(2,1)S(1)} %pad_maximum_fusion.9.refs_0_), channel_id=1, source_target_pairs={{0,16},{1,17},{2,18},{3,19},{4,20},{5,21},{6,22},{7,23},{8,24},{9,... | collective-permute-start | bytes 1572872 | tf_op jit(solution)/shard_map/ppermute | solution.py:102
  205.6 25.0 %collective-permute-start.36 = (bf16[512,512]{1,0:T(8,128)(2,1)S(1)}, bf16[512,512]{1,0:T(8,128)(2,1)}, u32[]{:S(2)}, u32[]{:S(2)}) collective-permute-start(bf16[512,512]{1,0:T(8,128)(2,1)S(1)} %pad_maximum_fusion.9.refs_0_), channel_id=1, source_target_pairs={{0,4},{1,5},{2,6},{3,7},{4,0},{5,1},{6,2},{7,3},{8,12},{9,13},{10,... | collective-permute-start | bytes 1572872 | tf_op jit(solution)/shard_map/ppermute | solution.py:102
  207.1 23.9 %collective-permute-start.37 = (bf16[512,512]{1,0:T(8,128)(2,1)}, bf16[512,512]{1,0:T(8,128)(2,1)}, u32[]{:S(2)}, u32[]{:S(2)}) collective-permute-start(bf16[512,512]{1,0:T(8,128)(2,1)} %collective-permute-done.30.refs_1_), channel_id=1, source_target_pairs={{0,4},{1,5},{2,6},{3,7},{4,0},{5,1},{6,2},{7,3},{8,12},{9,13},{10,... | collective-permute-start | bytes 1572872 | tf_op jit(solution)/shard_map/ppermute | solution.py:102
  357.9 42.5 %collective-permute-start.59 = (bf16[192,512]{1,0:T(8,128)(2,1)S(1)}, bf16[192,512]{1,0:T(8,128)(2,1)S(1)}, u32[]{:S(2)}, u32[]{:S(2)}) collective-permute-start(bf16[192,512]{1,0:T(8,128)(2,1)S(1)} %get-tuple-element.247), channel_id=1, source_target_pairs={{0,8},{1,9},{2,10},{3,11},{4,12},{5,13},{6,14},{7,15},{8,0},{9,1},... | collective-permute-start | bytes 589832 | tf_op jit(solution)/shard_map/ppermute | solution.py:102
  359.9 41.6 %collective-permute-start.60 = (bf16[192,512]{1,0:T(8,128)(2,1)S(1)}, bf16[192,512]{1,0:T(8,128)(2,1)S(1)}, u32[]{:S(2)}, u32[]{:S(2)}) collective-permute-start(bf16[192,512]{1,0:T(8,128)(2,1)S(1)} %get-tuple-element.248), channel_id=1, source_target_pairs={{0,1},{1,0},{2,3},{3,2},{4,5},{5,4},{6,7},{7,6},{8,9},{9,8},{10,11... | collective-permute-start | bytes 589832 | tf_op jit(solution)/shard_map/ppermute | solution.py:102
  373.6 30.0 %collective-permute-start.63 = (bf16[192,512]{1,0:T(8,128)(2,1)S(1)}, bf16[192,512]{1,0:T(8,128)(2,1)S(1)}, u32[]{:S(2)}, u32[]{:S(2)}) collective-permute-start(bf16[192,512]{1,0:T(8,128)(2,1)S(1)} %get-tuple-element.259), channel_id=1, source_target_pairs={{0,8},{1,9},{2,10},{3,11},{4,12},{5,13},{6,14},{7,15},{8,0},{9,1},... | collective-permute-start | bytes 589832 | tf_op jit(solution)/shard_map/ppermute | solution.py:102
  (116 other events, 1560.6 us)

commit v2 on v1

--- a/solution.py
+++ b/solution.py
@@ -18,13 +18,12 @@
 CHUNKS = (256,) + (512,) * 7 + (160,)
 NEAR = {0: (0,), 1: (1, 2), 3: (3, 4), 5: (5, 6), 7: (7, 8)}
 HIDDEN = (2, 4)
-TABLE = {0: ZLO, 1: ZHI, 6: Y, 8: CORE}
-EARLY = {10: ZHI, 11: Y, 12: CORE}
-EARLY_GROUPS = 4
+TABLE = {1: ZLO, 2: ZHI, 10: Y, 11: CORE}
 GROUPS = ((0,), (1, 2), (3,), (4,), (5,), (6,), (7,), (8,))
 PACKED = (3, 5, 6, 7, 8, 9, 10, 11)
-MOVED = (4, 6, 7, 8, 9, 10, 10, 11)
-COMPUTED = (6, 7, 8, 9, 10, 11, 11, 12)
+MOVED = (4, 6, 7, 8, 8, 9, 10, 11)
+COMPUTED = (6, 7, 7, 8, 8, 9, 10, 11)
+GATHERED = (((0, 1, 2), 9), ((3, 4, 5), 10), ((6, 7), None))
 HIGHEST = lax.Precision.HIGHEST
 NO_COST = pl.CostEstimate(flops=0, bytes_accessed=0, transcendentals=0)
 
@@ -102,56 +101,61 @@
     return lax.ppermute(array, AXES, [(i, i ^ bits) for i in range(32)])
 
 
-def arrange(places, hidden, other):
+def arrange(places, x, hidden, by_z, by_x):
     rows, width = hidden.shape
     block = width // 16
-    step = 128
+    pieces = [*by_z, *by_x]
+    step = pieces[0].shape[0]
     n = rows // step
 
-    def kernel(places, a, b, out):
+    def kernel(places, hidden, *refs):
+        sources, out = refs[:-1], refs[-1]
+
         def put(source):
             for k in range(16):
                 lanes = pl.ds(pl.multiple_of(places[k] * block, block), block)
                 out[:, k * block : (k + 1) * block] = source[:, lanes]
 
+        at = pl.program_id(0)
+
+        @pl.when(at < n)
+        def _():
+            put(hidden)
+
+        for i, source in enumerate(sources):
+
+            @pl.when(at == n + i)
+            def _():
+                put(source)
+
+    def there(i, places):
         own = places[0] // 4 % 2
-        here = pl.program_id(0) // n == own
-
-        @pl.when(here)
-        def _():
-            put(a)
-
-        @pl.when(jnp.logical_not(here))
-        def _():
-            put(b)
-
-    def at(turn):
-        def index(i, places):
-            first = (places[0] // 4 + turn) % 2 * n
-            return jnp.clip(i - first, 0, n - 1), 0
-
-        return pl.BlockSpec((step, width), index)
+        piece = jnp.maximum(i - n, 0)
+        half = (piece // len(by_z) + places[16]) % 2
+        other = (1 - own) * n + half * len(by_z) + piece % len(by_z)
+        return jnp.where(i < n, own * n + i, other), 0
 
     return pl.pallas_call(
         kernel,
         grid_spec=pltpu.PrefetchScalarGridSpec(
             num_scalar_prefetch=1,
             grid=(2 * n,),
-            in_specs=[at(0), at(1)],
-            out_specs=pl.BlockSpec((step, width), lambda i, places: (i, 0)),
+            in_specs=[pl.BlockSpec((step, width), lambda i, places: (jnp.minimum(i, n - 1), 0))]
+            + [pl.BlockSpec((step, width), lambda i, places: (0, 0))] * len(pieces),
+            out_specs=pl.BlockSpec((step, width), there),
         ),
         out_shape=pltpu.VMEM((2 * rows, width), hidden.dtype),
-        compiler_params=pltpu.CompilerParams(vmem_limit_bytes=40 * 2**20),
+        compiler_params=pltpu.CompilerParams(vmem_limit_bytes=24 * 2**20),
         cost_estimate=NO_COST,
         name="arrange",
-    )(places, hidden, other)
+    )(jnp.concatenate([places, x[None]]).astype(jnp.int32), hidden, *pieces)
 
 
 def pack(groups):
     n = len(groups)
-    width = groups[0][0].shape[1]
+    block = groups[0][0].shape[1] // 2
     heights = [group[0].shape[0] for group in groups]
-    step = 128 if all(h % 128 == 0 for h in heights) else heights[0]
+    step = 256 if all(h % 256 == 0 for h in heights) else heights[0]
     ends = [sum(heights[: i + 1]) // step for i in range(n)]
     firsts = [0] + ends[:-1]
 
@@ -161,22 +165,24 @@
 
             @pl.when((pl.program_id(0) >= firsts[i]) & (pl.program_id(0) < ends[i]))
             def _():
-                for k in range(4):
-                    out[:, k * width : (k + 1) * width] = refs[4 * i + k][...]
+                for k in range(8):
+                    out[k] = refs[4 * i + k // 2][:, k % 2 * block : (k % 2 + 1) * block]
 
     specs = []
     for i in range(n):
         last = heights[i] // step - 1
         specs += [
-            pl.BlockSpec((step, width), lambda r, i=i, last=last: (jnp.clip(r - firsts[i], 0, last), 0))
+            pl.BlockSpec(
+                (step, 2 * block), lambda r, i=i, last=last: (jnp.clip(r - firsts[i], 0, last), 0)
+            )
         ] * 4
     return pl.pallas_call(
         kernel,
         grid=(ends[-1],),
         in_specs=specs,
-        out_specs=pl.BlockSpec((step, 4 * width), lambda r: (r, 0)),
-        out_shape=pltpu.HBM((sum(heights), 4 * width), BF16),
-        compiler_params=pltpu.CompilerParams(vmem_limit_bytes=40 * 2**20),
+        out_specs=pl.BlockSpec((8, step, block), lambda r: (0, r, 0)),
+        out_shape=pltpu.HBM((8, sum(heights), block), BF16),
+        compiler_params=pltpu.CompilerParams(vmem_limit_bytes=24 * 2**20),
         cost_estimate=NO_COST,
         name="pack",
     )(*in_hbm(*[a for group in groups for a in group]))
@@ -184,7 +190,7 @@
 
 def forward(lens, rows, near, across, bias, slopes, start):
     tokens, depth = rows.shape
-    wide, deep = near.shape
+    blocks, wide, block = near.shape
     tile = 256
     tiles = -(-wide // tile)
     count = lens.shape[0] // 4
@@ -193,11 +199,12 @@
     def kernel(lens, rows, near, across, bias, *refs):
         slope, reps = refs[-2:]
         by_rows = (((1,), (1,)), ((), ()))
-        logits = (
-            lax.dot_general(rows[:, :deep], near[...], by_rows, preferred_element_type=F32)
-            + lax.dot_general(rows[:, deep:], across[...], by_rows, preferred_element_type=F32)
-            + bias[...]
-        )
+        logits = bias[...]
+        for k in range(2 * blocks):
+            head = (near if k < blocks else across)[k % blocks]
+            logits = logits + lax.dot_general(
+                rows[:, k * block : (k + 1) * block], head, by_rows, preferred_element_type=F32
+            )
         if wide % tile:
             lanes = pl.program_id(0) * tile + lax.broadcasted_iota(jnp.int32, logits.shape, 1)
             logits = jnp.where(lanes < wide, logits, -1.0)
@@ -227,8 +234,8 @@
             grid=(tiles,),
             in_specs=[
                 pl.BlockSpec(memory_space=pltpu.VMEM),
-                pl.BlockSpec((tile, deep), lambda c, lens: (c, 0)),
-                pl.BlockSpec((tile, deep), lambda c, lens: (c, 0)),
+                pl.BlockSpec((blocks, tile, block), lambda c, lens: (0, c, 0)),
+                pl.BlockSpec((blocks, tile, block), lambda c, lens: (0, c, 0)),
                 pl.BlockSpec((1, tile), lambda c, lens: (0, first + c)),
             ]
             + [pl.BlockSpec(memory_space=pl.ANY)] * len(old),
@@ -242,19 +249,23 @@
             jax.ShapeDtypeStruct((2, 2 * count, tiles * tile), F32),
         ],
         input_output_aliases={5: 0} if old else {},
-        compiler_params=pltpu.CompilerParams(vmem_limit_bytes=40 * 2**20),
+        compiler_params=pltpu.CompilerParams(vmem_limit_bytes=24 * 2**20),
         cost_estimate=NO_COST,
         name=f"forward{start}",
-    )(lens, in_vmem(rows), *in_hbm(near, across), bias, *in_hbm(*old))
-
-
-def margins(parts, id_place, teachers, slopes, early, late):
+    )(lens, in_vmem(rows), *in_hbm(near), across, bias, *in_hbm(*old))
+
+
+def margins(parts, id_place, teachers, slopes, gathered):
     tiles, tokens, tile = slopes.shape
     queries, neg_count = teachers.shape
-    pair = early.shape[1] // 8
-    split_at = early.shape[2] // tile
-
-    def kernel(s0, s1, s2, s3, ids, teach, slope, early, late, margin, grad, coeff, coeff_t):
+    pair = queries // 8
+    n = len(gathered)
+    ends = [sum(reps.shape[2] for reps in gathered[: i + 1]) // tile for i in range(n)]
+    firsts = [0] + ends[:-1]
+    batch = 4
+
+    def kernel(s0, s1, s2, s3, ids, teach, slope, *refs):
+        gathered, (margin, grad, coeff, coeff_t) = refs[:n], refs[n:]
         step = pl.program_id(0)
 
         @pl.when(step == 0)
@@ -276,53 +287,55 @@
             coeff[...] = total
             coeff_t[...] = total.T
 
-        def fill(reps):
-            grad_q = jnp.dot(coeff[:pair], reps[1], precision=HIGHEST, preferred_element_type=F32)
-            grad_p = jnp.dot(coeff_t[:pair], reps[0], precision=HIGHEST, preferred_element_type=F32)
+        def fill(t, reps, first):
+            there = pl.ds(pl.multiple_of((step * batch + t - first) * tile, tile), tile)
+            here = pl.ds(pl.multiple_of((step * batch + t) * tile, tile), tile)
+            grad_q = jnp.dot(
+                coeff[:pair], reps[1, :, there], precision=HIGHEST, preferred_element_type=F32
+            )
+            grad_p = jnp.dot(
+                coeff_t[:pair], reps[0, :, there], precision=HIGHEST, preferred_element_type=F32
+            )
             at = 0
             for b in range(2):
                 for span, part in ((LQ, grad_q), (LP, grad_p)):
                     for i in range(pair // 2):
                         row = b * (pair // 2) + i
-                        grad[at : at + span, :] = (
-                            slope[0, at : at + span, :] * part[row : row + 1]
+                        grad[at : at + span, here] = (
+                            slope[t, at : at + span, :] * part[row : row + 1]
                         ).astype(BF16)
                         at += span
 
-        @pl.when(step < split_at)
-        def _():
-            fill(early)
-
-        @pl.when(step >= split_at)
-        def _():
-            fill(late)
+        for t in range(batch):
+            for reps, first, end in zip(gathered, firsts, ends):
+
+                @pl.when((step * batch + t >= first) & (step * batch + t < end))
+                def _():
+                    fill(t, reps, first)
 
     square = pl.BlockSpec((queries, queries), lambda c: (0, 0))
     listed = pl.BlockSpec((queries, neg_count), lambda c: (0, 0))
     return pl.pallas_call(
         kernel,
-        grid=(tiles,),
+        grid=(tiles // batch,),
         in_specs=[square] * 4
         + [listed] * 2
-        + [
-            pl.BlockSpec((1, tokens, tile), lambda c: (c, 0, 0)),
-            pl.BlockSpec((2, queries, tile), lambda c: (0, 0, jnp.minimum(c, split_at - 1))),
-            pl.BlockSpec((2, queries, tile), lambda c: (0, 0, jnp.maximum(c - split_at, 0))),
-        ],
-        out_specs=[listed, pl.BlockSpec((tokens, tile), lambda c: (0, c))],
+        + [pl.BlockSpec((batch, tokens, tile), lambda c: (c, 0, 0))]
+        + [pl.BlockSpec(memory_space=pltpu.VMEM)] * n,
+        out_specs=[listed, pl.BlockSpec(memory_space=pltpu.VMEM)],
         out_shape=[
             jax.ShapeDtypeStruct((queries, neg_count), F32),
             pltpu.VMEM((tokens, tiles * tile), BF16),
         ],
         scratch_shapes=[pltpu.VMEM((queries, queries), F32)] * 2,
-        compiler_params=pltpu.CompilerParams(vmem_limit_bytes=40 * 2**20),
+        compiler_params=pltpu.CompilerParams(vmem_limit_bytes=24 * 2**20),
         name="margins",
-    )(*parts, id_place, teachers, *in_hbm(slopes), early, late)
+    )(*parts, id_place, teachers, *in_hbm(slopes), *gathered)
 
 
 def back_piece(place, grads, heads, piece, pieces):
     n = len(heads)
-    rows, block = grads.shape[0], heads[0].shape[1] // 8
+    rows, block = grads.shape[0], heads[0].shape[2]
     steps = 16 // pieces
     half = rows // 4
 
@@ -330,8 +343,8 @@
         heads, (send_x, keep_x, send_z, keep_z, total) = refs[:n], refs[n:]
         sums, start = None, 0
         for head in heads:
-            wide = head.shape[0]
-            part = jnp.dot(grad[:, start : start + wide], head[...], preferred_element_type=F32)
+            wide = head.shape[1]
+            part = jnp.dot(grad[:, start : start + wide], head[0], preferred_element_type=F32)
             sums = part if sums is None else sums + part
             start += wide
         total[...] = sums
@@ -353,7 +366,7 @@
             send_z[1] = rows_of(1 - zlo, 1 - x).astype(BF16)
 
     some = [
-        pl.BlockSpec((h.shape[0], block), lambda d, place: (0, piece % 2 * steps + d))
+        pl.BlockSpec((1, h.shape[1], block), lambda d, place: (piece % 2 * steps + d, 0, 0))
         for h in heads
     ]
     last = steps // 2 - 1
@@ -374,7 +387,7 @@
             scratch_shapes=[pltpu.VMEM((rows, block), F32)],
         ),
         out_shape=[pltpu.HBM(shape, t) for t in (BF16, F32, BF16, F32)],
-        compiler_params=pltpu.CompilerParams(vmem_limit_bytes=40 * 2**20),
+        compiler_params=pltpu.CompilerParams(vmem_limit_bytes=24 * 2**20),
         cost_estimate=pl.CostEstimate(
             flops=2 * rows * grads.shape[1] * steps * block,
             bytes_accessed=2 * grads.shape[1] * steps * block + 3 * rows * steps * block,
@@ -389,7 +402,7 @@
     rows, width = pairs[0][0].shape
     blocks = 16 // count
     block = width // blocks
-    step = 32
+    step = rows // 2
 
     def kernel(places, *refs):
         out = refs[-1]
@@ -408,7 +421,7 @@
             out_specs=pl.BlockSpec((step, 16 * block), lambda r, places: (r, 0)),
         ),
         out_shape=jax.ShapeDtypeStruct((rows, 16 * block), F32),
-        compiler_params=pltpu.CompilerParams(vmem_limit_bytes=40 * 2**20),
+        compiler_params=pltpu.CompilerParams(vmem_limit_bytes=24 * 2**20),
         name="finish",
     )(places, *[a for pair in pairs for a in pair])
 
@@ -440,13 +453,15 @@
 
     def columns_of(chunks, low):
         first, size = starts[chunks[0]], sum(CHUNKS[c] for c in chunks)
-        return lax.dynamic_slice(head, (low * share + first, 0), (size, depth))
+        return jnp.where(
+            low == 0, head[first : first + size], head[share + first : share + first + size]
+        )
 
     for k, chunks in NEAR.items():
         live["given", k] = columns_of(chunks, 1 - zlo)
     for i, k in enumerate(HIDDEN):
         live["hidden", k] = lax.dynamic_slice(hidden, (x * half + i * piece, 0), (piece, width))
-    table = jnp.concatenate(
+    live["table"] = jnp.concatenate(
         [
             (neg_owner * count + neg_index).astype(F32),
             teacher,
@@ -465,11 +480,11 @@
     def beside(j):
         return jnp.concatenate([columns_of((j,), zlo), near_of(j)], axis=1)
 
-    def all_reps(own, bits):
-        return jnp.concatenate([own, swap(own, bits)], axis=1)
+    def reps_of(groups):
+        return jnp.concatenate([live["reps", g] for g in groups], axis=2)
 
     rows = lens = slopes = None
-    rounds = max(COMPUTED)
+    rounds = max(COMPUTED) + 2
     for k in range(rounds + 1):
         sent = {}
         if 0 <= k - 1 < n:
@@ -480,59 +495,64 @@
             sent["side", j] = swap(live["two", j], Y)
         if 0 <= k - 2 < n:
             sent["beyond", k - 2] = swap(live["far", k - 2], Y)
-        if k in NEAR:
-            sent["near", k] = swap(live["given", k], ZLO)
+        for i in NEAR:
+            if k == max(i - (i == 1), 0):
+                sent["near", i] = swap(live["given", i], ZLO)
         if k in HIDDEN:
             sent["from_z", k] = swap(live["hidden", k], ZLO)
         if k - 1 in HIDDEN:
             sent["from_x", k - 1] = swap(live["from_z", k - 1], X)
+        if k - 1 in TABLE:
+            table, came = live["table"], live["table came"]
+            both = [table, came]
+            if TABLE[k - 1] == ZLO:
+                both = [jnp.where(zlo == 0, table, came), jnp.where(zlo == 0, came, table)]
+            live["table"] = jnp.concatenate(both)
+        if k in TABLE:
+            sent["table came"] = swap(live["table"], TABLE[k])
+        if k == max(HIDDEN) + 2:
+            by_z, by_x = ([live[name, i] for i in HIDDEN] for name in ("from_z", "from_x"))
+            rows = arrange(blocks, x, hidden, by_z, by_x)
+            pair_lens = live["table"][: 2 * count, 2 * neg_count :].astype(jnp.int32)
+            lens = pair_lens.reshape(2, count, 2).transpose(0, 2, 1).reshape(-1)
         for g in range(len(GROUPS)):
             if k == PACKED[g]:
-                sent["quads", g] = pack(
-                    [[live[name, j] for name in ("two", "far", "side", "beyond")] for j in GROUPS[g]]
-                )
+                arrays = [live[name, j] for j in GROUPS[g] for name in ("two", "far", "side", "beyond")]
+                sent["quads", g] = pack([arrays[4 * i : 4 * i + 4] for i in range(len(GROUPS[g]))])
             if k == MOVED[g]:
                 quads = sent if k == PACKED[g] else live
                 sent["across", g] = swap(quads["quads", g], CORE)
-        if k in TABLE:
-            came = swap(table, TABLE[k])
-            both = [table, came]
-            if TABLE[k] == ZLO:
-                both = [jnp.where(zlo == 0, table, came), jnp.where(zlo == 0, came, table)]
-            sent["table"] = jnp.concatenate(both)
-        if k == max(HIDDEN) + 2:
-            by_z, by_x = (
-                jnp.concatenate([live[name, i] for i in HIDDEN]) for name in ("from_z", "from_x")
-            )
-            other = jnp.concatenate(
-                [jnp.where(x == 0, by_z, by_x), jnp.where(x == 0, by_x, by_z)]
-            )
-            rows = arrange(blocks, hidden, other)
-            pair_lens = table[: 2 * count, 2 * neg_count :].astype(jnp.int32)
-            lens = pair_lens.reshape(2, count, 2).transpose(0, 2, 1).reshape(-1)
-        for g in range(len(GROUPS)):
             if k == COMPUTED[g]:
                 first = starts[GROUPS[g][0]]
-                slopes, sent["reps", g] = forward(
-                    lens, rows, live["quads", g], live["across", g], bias, slopes, first
+                quads, across = (
+                    sent[key] if key in sent else live[key] for key in (("quads", g), ("across", g))
                 )
-        if k in EARLY:
-            own = live.get("early")
-            if own is None:
-                own = jnp.concatenate([live["reps", g] for g in range(EARLY_GROUPS)], axis=2)
-            sent["early"] = all_reps(own, EARLY[k])
+                slopes, sent["reps", g] = forward(lens, rows, quads, across, bias, slopes, first)
+        for groups, first in GATHERED:
+            if first is None or not 0 <= k - first <= 3:
+                continue
+            if k == first:
+                own = reps_of(groups)
+            else:
+                own = jnp.concatenate([live["gathered", groups], live["came", groups]], axis=1)
+            live["gathered", groups] = own
+            if k - first < 3:
+                sent["came", groups] = swap(own, (ZHI, Y, CORE)[k - first])
         live.update(sent)
-        if k == rounds:
-            break
+        if k > max(COMPUTED):
+            continue
         held = list(sent)
+        if k == 0:
+            held.remove(("near", 1))
+        if k == 1:
+            held.append(("near", 1))
         if any(k in chunks[1:] for chunks in NEAR.values()):
             live["two", k] = beside(k)
             held.append(("two", k))
         held += [key for key in (("given", k + 1), ("hidden", k + 1)) if key in live]
         live.update(zip(held, lax.optimization_barrier([live[key] for key in held])))
-        table = live["table"]
-    ids = table[:, :neg_count].astype(jnp.int32)
-    teachers = table[:, neg_count : 2 * neg_count]
+    ids = live["table"][:, :neg_count].astype(jnp.int32)
+    teachers = live["table"][:, neg_count : 2 * neg_count]
     owner = ids // count
     order = jnp.array(ORDER[::2], jnp.int32)
     group = jnp.sum(
@@ -541,22 +561,21 @@
     )
     id_place = (group * 2 + ((owner >> 2) & 1)) * count + ids % count
 
-    early = live["early"]
-    late = jnp.concatenate([live["reps", g] for g in range(EARLY_GROUPS, len(GROUPS))], axis=2)
+    late = reps_of(GATHERED[-1][0])
     for bits in (ZHI, Y, CORE):
-        late = all_reps(late, bits)
+        late = jnp.concatenate([late, swap(late, bits)], axis=1)
+    gathered = [live["gathered", groups] for groups, _ in GATHERED[:-1]] + [late]
 
     def scores(reps):
         return lax.dot_general(reps[0], reps[1], (((1,), (1,)), ((), ())), precision=HIGHEST)
 
-    part = scores(early) + scores(late)
+    part = sum(scores(reps) for reps in gathered)
     margin_error, grads = margins(
         (part, swap(part, X), swap(part, ZLO), swap(part, ZLO | X)),
         id_place,
         teachers,
         slopes,
-        early,
-        late,
+        gathered,
     )
 
     pieces = 4

time: 418 us -> 395 us (0.945)
  local copies, waits for them, and re-layouts: 31.1 us -> 11.9 us
  Pallas kernels: 156 us -> 138 us
  other arithmetic: 9.24 us -> 19.8 us
  starting transfers between devices: 77.9 us -> 84.8 us
    select_n x1 -> x5, other arithmetic: 0.21 us -> 9.85 us  [columns_of(): jnp.where(low == 0, head[first:first + size], head[share + first:share +...]
    dynamic_slice x5 -> x0, local copies, waits for them, and re-layouts: 8.65 us -> none  [columns_of(): return lax.dynamic_slice(head, (low * share + first, 0), (size, depth))]
    pallas_call x8, Pallas kernels: 31.4 us -> 22.9 us  [pack(): pl.pallas_call(kernel, grid=(ends[-1],), in_specs=specs, out_specs=pl.Blo...]
    ppermute x73 -> x76, starting transfers between devices: 77.9 us -> 84.8 us  [swap(): return lax.ppermute(array, AXES, [(i, i ^ bits) for i in range(32)])]
    unnamed x141, local copies, waits for them, and re-layouts: 14.1 us -> 7.84 us
    pallas_call x1, Pallas kernels: 13.6 us -> 8.47 us  [margins(): pl.pallas_call(kernel, grid=(tiles // batch,), in_specs=[square] * 4 + [l...]
    ppermute x73 -> x76, waiting for transfers between devices: 140 us -> 138 us  [swap(): return lax.ppermute(array, AXES, [(i, i ^ bits) for i in range(32)])]
  transfers between devices with their start and end apart: 73 -> 76, of which waited for: 28 -> 29; matrix products, arithmetic and copies ran while one was open for 6% -> 6% of each run, Pallas kernels for 28% -> 27%
where the time goes in v2:
time: 395 us
  waiting for transfers between devices  138 us (35%)
  Pallas kernels  138 us (35%)
  starting transfers between devices  84.8 us (21%)
  other arithmetic  19.8 us (5%)
  local copies, waits for them, and re-layouts  11.9 us (3%)
    ppermute x76, waiting for transfers between devices, swap(): return lax.ppermute(array, AXES, [(i, i ^ bits) for i in range(32)])  138 us
    ppermute x76, starting transfers between devices, swap(): return lax.ppermute(array, AXES, [(i, i ^ bits) for i in range(32)])  84.8 us
    pallas_call x8, Pallas kernels, forward(): pl.pallas_call(kernel, grid_spec=pltpu.PrefetchScalarGridSpec(num_scalar_...  57.8 us
    pallas_call x4, Pallas kernels, back_piece(): pl.pallas_call(kernel, grid_spec=pltpu.PrefetchScalarGridSpec(num_scalar_...  43.2 us
    pallas_call x8, Pallas kernels, pack(): pl.pallas_call(kernel, grid=(ends[-1],), in_specs=specs, out_specs=pl.Blo...  22.9 us
    select_n x5, other arithmetic, columns_of(): jnp.where(low == 0, head[first:first + size], head[share + first:share +...  9.85 us
    pallas_call x1, Pallas kernels, margins(): pl.pallas_call(kernel, grid=(tiles // batch,), in_specs=[square] * 4 + [l...  8.47 us
  transfers between devices with their start and end apart: 76, of which 29 were waited for; matrix products, arithmetic and copies ran while one was open for 6% of the time, Pallas kernels for 27%

profile of v2, /device:TPU:0, one launch (start us, length us, event | category | flops | bytes accessed | tf_op | source)
XLA Modules:
  0.0 394.5 jit_solution(4365846689035740668)
XLA Ops:
  20.1 9.2 %collective-permute-done.1.refs_1_ = bf16[256,512]{1,0:T(8,128)(2,1)S(1)} collective-permute-done((bf16[256,512]{1,0:T(8,128)(2,1)S(1)}, bf16[256,512]{1,0:T(8,128)(2,1)S(1)}, u32[]{:S(2)}, u32[]{:S(2)}) %collective-permute-start.1) | collective-permute-done | bytes 262176 | tf_op jit(solution)/shard_map/ppermute | solution.py:101
  39.2 20.4 %collective-permute-done.9 = f32[8,18]{1,0:T(8,128)S(1)} collective-permute-done((f32[8,18]{1,0:T(8,128)S(1)}, f32[8,18]{1,0:T(8,128)S(1)}, u32[]{:S(2)}, u32[]{:S(2)}) %collective-permute-start.9) | collective-permute-done | bytes 608 | tf_op jit(solution)/shard_map/ppermute | solution.py:101
  69.9 15.4 %collective-permute-done.10.refs_5_ = bf16[512,512]{1,0:T(8,128)(2,1)S(1)} collective-permute-done((bf16[512,512]{1,0:T(8,128)(2,1)S(1)}, bf16[512,512]{1,0:T(8,128)(2,1)S(1)}, u32[]{:S(2)}, u32[]{:S(2)}) %collective-permute-start.10) | collective-permute-done | bytes 524320 | tf_op jit(solution)/shard_map/ppermute | solution.py:101
  93.0 23.9 %collective-permute-done.15.refs_1_ = bf16[512,512]{1,0:T(8,128)(2,1)S(1)} collective-permute-done((bf16[512,512]{1,0:T(8,128)(2,1)S(1)}, bf16[512,512]{1,0:T(8,128)(2,1)S(1)}, u32[]{:S(2)}, u32[]{:S(2)}) %collective-permute-start.15) | collective-permute-done | bytes 524320 | tf_op jit(solution)/shard_map/ppermute | solution.py:101
  126.5 5.4 %pack.9.near.refs_1_ = bf16[8,1024,256]{2,1,0:T(8,128)(2,1)} custom-call(bf16[512,512]{1,0:T(8,128)(2,1)} %copy-done.22, bf16[512,512]{1,0:T(8,128)(2,1)} %copy-done.41, bf16[512,512]{1,0:T(8,128)(2,1)} %copy-done.42, bf16[512,512]{1,0:T(8,128)(2,1)} %copy-done.45, bf16[512,512]{1,0:T(8,128)(2,1)} %copy-done.23, bf16[512,512]{1,0:T(8,128)(2,1)} %copy-done.43, ...), custom_call_target="tpu_custom_call" | custom-call | tf_op jit(solution)/shard_map/pack/pallas_call | solution.py:179
  131.9 14.0 %collective-permute-done.20.refs_1_ = bf16[512,512]{1,0:T(8,128)(2,1)} collective-permute-done((bf16[512,512]{1,0:T(8,128)(2,1)S(1)}, bf16[512,512]{1,0:T(8,128)(2,1)}, u32[]{:S(2)}, u32[]{:S(2)}) %collective-permute-start.20) | collective-permute-done | bytes 524320 | tf_op jit(solution)/shard_map/ppermute | solution.py:101
  160.6 5.1 %forward0.1 = (f32[16,768,256]{2,1,0:T(8,128)}, f32[2,8,256]{2,1,0:T(8,128)S(1)}) custom-call(s32[16]{0:T(128)S(1)} %reshape.55.lens, bf16[768,4096]{1,0:T(8,128)(2,1)S(1)} %arrange.1.rows, bf16[8,256,256]{2,1,0:T(8,128)(2,1)} %pack.8.near.refs_0_, bf16[8,256,256]{2,1,0:T(8,128)(2,1)S(1)} %copy-done.7, f32[1,4096]{1,0:T(1,128)S(1)} %bitcast.77), custom_call_target="tpu_custom_call" | custom-call | tf_op jit(solution)/shard_map/forward0/pallas_call | solution.py:230
  165.7 12.7 %collective-permute-done.25.refs_1_ = bf16[512,512]{1,0:T(8,128)(2,1)} collective-permute-done((bf16[512,512]{1,0:T(8,128)(2,1)}, bf16[512,512]{1,0:T(8,128)(2,1)}, u32[]{:S(2)}, u32[]{:S(2)}) %collective-permute-start.25) | collective-permute-done | bytes 524320 | tf_op jit(solution)/shard_map/ppermute | solution.py:101
  184.0 11.6 %forward256.1 = (f32[16,768,256]{2,1,0:T(8,128)}, f32[2,8,1024]{2,1,0:T(8,128)S(1)}) custom-call(s32[16]{0:T(128)S(1)} %reshape.55.lens, bf16[768,4096]{1,0:T(8,128)(2,1)S(1)} %arrange.1.rows, bf16[8,1024,256]{2,1,0:T(8,128)(2,1)} %pack.9.near.refs_1_, bf16[8,1024,256]{2,1,0:T(8,128)(2,1)} %collective-permute-done.28.across.refs_1_, ...), custom_call_target="tpu_custom_call", output_to_operand_aliasing={{0}: (5, {})} | custom-call | tf_op jit(solution)/shard_map/forward256/pallas_call | solution.py:230
  198.2 7.8 %forward1280.1 = (f32[16,768,256]{2,1,0:T(8,128)}, f32[2,8,512]{2,1,0:T(8,128)S(1)}) custom-call(s32[16]{0:T(128)S(1)} %reshape.55.lens, bf16[768,4096]{1,0:T(8,128)(2,1)S(1)} %arrange.1.rows, bf16[8,512,256]{2,1,0:T(8,128)(2,1)} %pack.10.near.refs_2_, ...), custom_call_target="tpu_custom_call", output_to_operand_aliasing={{0}: (5, {})} | custom-call | tf_op jit(solution)/shard_map/forward1280/pallas_call | solution.py:230
  215.3 7.2 %forward1792.1 = (f32[16,768,256]{2,1,0:T(8,128)}, f32[2,8,512]{2,1,0:T(8,128)S(1)}) custom-call(s32[16]{0:T(128)S(1)} %reshape.55.lens, bf16[768,4096]{1,0:T(8,128)(2,1)S(1)} %arrange.1.rows, bf16[8,512,256]{2,1,0:T(8,128)(2,1)} %pack.11.near.refs_3_, ...), custom_call_target="tpu_custom_call", output_to_operand_aliasing={{0}: (5, {})} | custom-call | tf_op jit(solution)/shard_map/forward1792/pallas_call | solution.py:230
  222.5 7.1 %forward2304.1 = (f32[16,768,256]{2,1,0:T(8,128)}, f32[2,8,512]{2,1,0:T(8,128)S(1)}) custom-call(s32[16]{0:T(128)S(1)} %reshape.55.lens, bf16[768,4096]{1,0:T(8,128)(2,1)S(1)} %arrange.1.rows, bf16[8,512,256]{2,1,0:T(8,128)(2,1)} %pack.12.near.refs_4_, ...), custom_call_target="tpu_custom_call", output_to_operand_aliasing={{0}: (5, {})} | custom-call | tf_op jit(solution)/shard_map/forward2304/pallas_call | solution.py:230
  229.7 6.5 %collective-permute-done.34.refs_1_ = bf16[512,512]{1,0:T(8,128)(2,1)S(1)} collective-permute-done((bf16[512,512]{1,0:T(8,128)(2,1)S(1)}, bf16[512,512]{1,0:T(8,128)(2,1)S(1)}, u32[]{:S(2)}, u32[]{:S(2)}) %collective-permute-start.34) | collective-permute-done | bytes 524320 | tf_op jit(solution)/shard_map/ppermute | solution.py:101
  246.0 7.2 %forward2816.1 = (f32[16,768,256]{2,1,0:T(8,128)}, f32[2,8,512]{2,1,0:T(8,128)S(1)}) custom-call(s32[16]{0:T(128)S(1)} %reshape.55.lens, bf16[768,4096]{1,0:T(8,128)(2,1)S(1)} %arrange.1.rows, bf16[8,512,256]{2,1,0:T(8,128)(2,1)} %pack.13.near.refs_5_, ...), custom_call_target="tpu_custom_call", output_to_operand_aliasing={{0}: (5, {})} | custom-call | tf_op jit(solution)/shard_map/forward2816/pallas_call | solution.py:230
  253.2 5.0 %collective-permute-done.43 = f32[2,8,1792]{2,1,0:T(8,128)S(1)} collective-permute-done((f32[2,8,1792]{2,1,0:T(8,128)S(1)}, f32[2,8,1792]{2,1,0:T(8,128)S(1)}, u32[]{:S(2)}, u32[]{:S(2)}) %collective-permute-start.43) | collective-permute-done | bytes 114720 | tf_op jit(solution)/shard_map/ppermute | solution.py:101
  266.6 7.1 %forward3328.1 = (f32[16,768,256]{2,1,0:T(8,128)}, f32[2,8,512]{2,1,0:T(8,128)S(1)}) custom-call(s32[16]{0:T(128)S(1)} %reshape.55.lens, bf16[768,4096]{1,0:T(8,128)(2,1)S(1)} %arrange.1.rows, bf16[8,512,256]{2,1,0:T(8,128)(2,1)} %pack.14.near.refs_6_, ...), custom_call_target="tpu_custom_call", output_to_operand_aliasing={{0}: (5, {})} | custom-call | tf_op jit(solution)/shard_map/forward3328/pallas_call | solution.py:230
  279.2 4.7 %forward3840.1 = (f32[16,768,256]{2,1,0:T(8,128)}, f32[2,8,256]{2,1,0:T(8,128)S(1)}) custom-call(s32[16]{0:T(128)S(1)} %reshape.55.lens, bf16[768,4096]{1,0:T(8,128)(2,1)S(1)} %arrange.1.rows, bf16[8,160,256]{2,1,0:T(8,128)(2,1)} %pack.15.near.refs_7_, ...), custom_call_target="tpu_custom_call", output_to_operand_aliasing={{0}: (5, {})} | custom-call | tf_op jit(solution)/shard_map/forward3840/pallas_call | solution.py:230
  304.2 8.5 %margins.1 = (f32[64,8]{1,0:T(8,128)S(1)}, bf16[768,4096]{1,0:T(8,128)(2,1)S(1)}) custom-call(f32[64,64]{1,0:T(8,128)S(1)} %fusion.s0, f32[64,64]{1,0:T(8,128)S(1)} %collective-permute-done.57.s1, f32[64,64]{1,0:T(8,128)S(1)} %collective-permute-done.58.s2, f32[64,64]{1,0:T(8,128)S(1)} %collective-permute-done.59.s3, s32[64,8]{1,0:T(8,128)S(1)} %fusion.11.ids, ...), custom_call_target="tpu_custom_call" | custom-call | tf_op jit(solution)/shard_map/margins/pallas_call | solution.py:318
  312.7 10.8 %back0.1 = (bf16[2,192,512]{2,1,0:T(8,128)(2,1)}, f32[2,192,512]{2,1,0:T(8,128)}, bf16[2,192,512]{2,1,0:T(8,128)(2,1)}, f32[2,192,512]{2,1,0:T(8,128)}) custom-call(s32[2]{0:T(128)S(1)} %pad_add_fusion.1.place, bf16[768,4096]{1,0:T(8,128)(2,1)S(1)} %get-tuple-element.273.grad, bf16[8,256,256]{2,1,0:T(8,128)(2,1)} %pack.8.near.refs_0_, ...), custom_call_target="tpu_custom_call" | custom-call | flops 6442450944 | bytes 10747904 | tf_op jit(solution)/shard_map/back0/pallas_call | solution.py:380
  324.9 11.0 %back1.1 = (bf16[2,192,512]{2,1,0:T(8,128)(2,1)}, f32[2,192,512]{2,1,0:T(8,128)}, bf16[2,192,512]{2,1,0:T(8,128)(2,1)}, f32[2,192,512]{2,1,0:T(8,128)}) custom-call(s32[2]{0:T(128)S(1)} %pad_add_fusion.1.place, bf16[768,4096]{1,0:T(8,128)(2,1)S(1)} %get-tuple-element.273.grad, bf16[8,256,256]{2,1,0:T(8,128)(2,1)} %pack.8.near.refs_0_, ...), custom_call_target="tpu_custom_call" | custom-call | flops 6442450944 | bytes 10747904 | tf_op jit(solution)/shard_map/back1/pallas_call | solution.py:380
  340.3 10.7 %back2.1 = (bf16[2,192,512]{2,1,0:T(8,128)(2,1)}, f32[2,192,512]{2,1,0:T(8,128)}, bf16[2,192,512]{2,1,0:T(8,128)(2,1)}, f32[2,192,512]{2,1,0:T(8,128)}) custom-call(s32[2]{0:T(128)S(1)} %pad_add_fusion.1.place, bf16[768,4096]{1,0:T(8,128)(2,1)S(1)} %get-tuple-element.273.grad, bf16[8,256,256]{2,1,0:T(8,128)(2,1)} %copy-done.6, ...), custom_call_target="tpu_custom_call" | custom-call | flops 6442450944 | bytes 10747904 | tf_op jit(solution)/shard_map/back2/pallas_call | solution.py:380
  355.5 10.8 %back3.1 = (bf16[2,192,512]{2,1,0:T(8,128)(2,1)}, f32[2,192,512]{2,1,0:T(8,128)}, bf16[2,192,512]{2,1,0:T(8,128)(2,1)}, f32[2,192,512]{2,1,0:T(8,128)}) custom-call(s32[2]{0:T(128)S(1)} %pad_add_fusion.1.place, bf16[768,4096]{1,0:T(8,128)(2,1)S(1)} %get-tuple-element.273.grad, bf16[8,256,256]{2,1,0:T(8,128)(2,1)} %copy-done.6, ...), custom_call_target="tpu_custom_call" | custom-call | flops 6442450944 | bytes 10747904 | tf_op jit(solution)/shard_map/back3/pallas_call | solution.py:380
  369.7 7.0 %collective-permute-done.72 = bf16[2,192,512]{2,1,0:T(8,128)(2,1)S(1)} collective-permute-done((bf16[2,192,512]{2,1,0:T(8,128)(2,1)}, bf16[2,192,512]{2,1,0:T(8,128)(2,1)S(1)}, u32[]{:S(2)}, u32[]{:S(2)}) %collective-permute-start.72) | collective-permute-done | bytes 393248 | tf_op jit(solution)/shard_map/ppermute | solution.py:101
  391.1 3.5 finish.1
  (363 shorter events, 160.6 us)
Async XLA Ops:
  30.2 30.1 %collective-permute-start.8 = (bf16[96,4096]{1,0:T(8,128)(2,1)S(1)}, bf16[96,4096]{1,0:T(8,128)(2,1)S(1)}, u32[]{:S(2)}, u32[]{:S(2)}) collective-permute-start(bf16[96,4096]{1,0:T(8,128)(2,1)S(1)} %get-tuple-element.146), channel_id=1, source_target_pairs={{0,8},{1,9},{2,10},{3,11},{4,12},{5,13},{6,14},{7,15},{8,0},{9,1},... | collective-permute-start | bytes 2359304 | tf_op jit(solution)/shard_map/ppermute | solution.py:101
  34.1 25.5 %collective-permute-start.5 = (bf16[512,512]{1,0:T(8,128)(2,1)S(1)}, bf16[512,512]{1,0:T(8,128)(2,1)S(1)}, u32[]{:S(2)}, u32[]{:S(2)}) collective-permute-start(bf16[512,512]{1,0:T(8,128)(2,1)S(1)} %pad_maximum_fusion.2.refs_0_), channel_id=1, source_target_pairs={{0,16},{1,17},{2,18},{3,19},{4,20},{5,21},{6,22},{7,23},{8,24},{9,... | collective-permute-start | bytes 1572872 | tf_op jit(solution)/shard_map/ppermute | solution.py:101
  35.7 23.9 %collective-permute-start.6 = (bf16[512,512]{1,0:T(8,128)(2,1)S(1)}, bf16[512,512]{1,0:T(8,128)(2,1)S(1)}, u32[]{:S(2)}, u32[]{:S(2)}) collective-permute-start(bf16[512,512]{1,0:T(8,128)(2,1)S(1)} %pad_maximum_fusion.2.refs_0_), channel_id=1, source_target_pairs={{0,4},{1,5},{2,6},{3,7},{4,0},{5,1},{6,2},{7,3},{8,12},{9,13},{10,... | collective-permute-start | bytes 1572872 | tf_op jit(solution)/shard_map/ppermute | solution.py:101
  60.3 26.2 %collective-permute-start.14 = (bf16[96,4096]{1,0:T(8,128)(2,1)S(1)}, bf16[96,4096]{1,0:T(8,128)(2,1)S(1)}, u32[]{:S(2)}, u32[]{:S(2)}) collective-permute-start(bf16[96,4096]{1,0:T(8,128)(2,1)S(1)} %collective-permute-done.8.refs_0_), channel_id=1, source_target_pairs={{0,1},{1,0},{2,3},{3,2},{4,5},{5,4},{6,7},{7,6},{8,9},{9,8},{10,11... | collective-permute-start | bytes 2359304 | tf_op jit(solution)/shard_map/ppermute | solution.py:101
  86.5 31.3 %collective-permute-start.19 = (bf16[8,256,256]{2,1,0:T(8,128)(2,1)}, bf16[8,256,256]{2,1,0:T(8,128)(2,1)S(1)}, u32[]{:S(2)}, u32[]{:S(2)}) collective-permute-start(bf16[8,256,256]{2,1,0:T(8,128)(2,1)} %pack.8.near.refs_0_), channel_id=1, source_target_pairs={{0,2},{1,3},{2,0},{3,1},{4,6},{5,7},{6,4},{7,5},{8,10},{9,11},{10,... | collective-permute-start | bytes 3145736 | tf_op jit(solution)/shard_map/ppermute | solution.py:101
  86.6 31.2 %collective-permute-start.18 = (bf16[96,4096]{1,0:T(8,128)(2,1)S(1)}, bf16[96,4096]{1,0:T(8,128)(2,1)S(1)}, u32[]{:S(2)}, u32[]{:S(2)}) collective-permute-start(bf16[96,4096]{1,0:T(8,128)(2,1)S(1)} %get-tuple-element.156), channel_id=1, source_target_pairs={{0,8},{1,9},{2,10},{3,11},{4,12},{5,13},{6,14},{7,15},{8,0},{9,1},... | collective-permute-start | bytes 2359304 | tf_op jit(solution)/shard_map/ppermute | solution.py:101
  88.3 28.6 %collective-permute-start.15 = (bf16[512,512]{1,0:T(8,128)(2,1)S(1)}, bf16[512,512]{1,0:T(8,128)(2,1)S(1)}, u32[]{:S(2)}, u32[]{:S(2)}) collective-permute-start(bf16[512,512]{1,0:T(8,128)(2,1)S(1)} %pad_maximum_fusion.4.refs_0_), channel_id=1, source_target_pairs={{0,16},{1,17},{2,18},{3,19},{4,20},{5,21},{6,22},{7,23},{8,24},{9,... | collective-permute-start | bytes 1572872 | tf_op jit(solution)/shard_map/ppermute | solution.py:101
  91.0 25.9 %collective-permute-start.16 = (bf16[512,512]{1,0:T(8,128)(2,1)S(1)}, bf16[512,512]{1,0:T(8,128)(2,1)S(1)}, u32[]{:S(2)}, u32[]{:S(2)}) collective-permute-start(bf16[512,512]{1,0:T(8,128)(2,1)S(1)} %pad_maximum_fusion.4.refs_0_), channel_id=1, source_target_pairs={{0,4},{1,5},{2,6},{3,7},{4,0},{5,1},{6,2},{7,3},{8,12},{9,13},{10,... | collective-permute-start | bytes 1572872 | tf_op jit(solution)/shard_map/ppermute | solution.py:101
  92.5 24.4 %collective-permute-start.17 = (bf16[512,512]{1,0:T(8,128)(2,1)S(1)}, bf16[512,512]{1,0:T(8,128)(2,1)S(1)}, u32[]{:S(2)}, u32[]{:S(2)}) collective-permute-start(bf16[512,512]{1,0:T(8,128)(2,1)S(1)} %collective-permute-done.10.refs_5_), channel_id=1, source_target_pairs={{0,4},{1,5},{2,6},{3,7},{4,0},{5,1},{6,2},{7,3},{8,12},{9,13},{10,... | collective-permute-start | bytes 1572872 | tf_op jit(solution)/shard_map/ppermute | solution.py:101
  118.8 28.3 %collective-permute-start.24 = (bf16[96,4096]{1,0:T(8,128)(2,1)S(1)}, bf16[96,4096]{1,0:T(8,128)(2,1)S(1)}, u32[]{:S(2)}, u32[]{:S(2)}) collective-permute-start(bf16[96,4096]{1,0:T(8,128)(2,1)S(1)} %collective-permute-done.18.refs_1_), channel_id=1, source_target_pairs={{0,1},{1,0},{2,3},{3,2},{4,5},{5,4},{6,7},{7,6},{8,9},{9,8},{10,11... | collective-permute-start | bytes 2359304 | tf_op jit(solution)/shard_map/ppermute | solution.py:101
  120.3 25.6 %collective-permute-start.20 = (bf16[512,512]{1,0:T(8,128)(2,1)S(1)}, bf16[512,512]{1,0:T(8,128)(2,1)}, u32[]{:S(2)}, u32[]{:S(2)}) collective-permute-start(bf16[512,512]{1,0:T(8,128)(2,1)S(1)} %pad_maximum_fusion.5.refs_0_), channel_id=1, source_target_pairs={{0,16},{1,17},{2,18},{3,19},{4,20},{5,21},{6,22},{7,23},{8,24},{9,... | collective-permute-start | bytes 1572872 | tf_op jit(solution)/shard_map/ppermute | solution.py:101
  148.1 30.9 %collective-permute-start.28 = (bf16[8,1024,256]{2,1,0:T(8,128)(2,1)}, bf16[8,1024,256]{2,1,0:T(8,128)(2,1)}, u32[]{:S(2)}, u32[]{:S(2)}) collective-permute-start(bf16[8,1024,256]{2,1,0:T(8,128)(2,1)} %pack.9.near.refs_1_), channel_id=1, source_target_pairs={{0,2},{1,3},{2,0},{3,1},{4,6},{5,7},{6,4},{7,5},{8,10},{9,11},{10,... | collective-permute-start | bytes 12582920 | tf_op jit(solution)/shard_map/ppermute | solution.py:101
  151.6 26.8 %collective-permute-start.25 = (bf16[512,512]{1,0:T(8,128)(2,1)}, bf16[512,512]{1,0:T(8,128)(2,1)}, u32[]{:S(2)}, u32[]{:S(2)}) collective-permute-start(bf16[512,512]{1,0:T(8,128)(2,1)} %pad_maximum_fusion.6.refs_0_), channel_id=1, source_target_pairs={{0,16},{1,17},{2,18},{3,19},{4,20},{5,21},{6,22},{7,23},{8,24},{9,... | collective-permute-start | bytes 1572872 | tf_op jit(solution)/shard_map/ppermute | solution.py:101
  153.4 25.0 %collective-permute-start.26 = (bf16[512,512]{1,0:T(8,128)(2,1)}, bf16[512,512]{1,0:T(8,128)(2,1)}, u32[]{:S(2)}, u32[]{:S(2)}) collective-permute-start(bf16[512,512]{1,0:T(8,128)(2,1)} %pad_maximum_fusion.6.refs_0_), channel_id=1, source_target_pairs={{0,4},{1,5},{2,6},{3,7},{4,0},{5,1},{6,2},{7,3},{8,12},{9,13},{10,... | collective-permute-start | bytes 1572872 | tf_op jit(solution)/shard_map/ppermute | solution.py:101
  154.9 24.1 %collective-permute-start.27 = (bf16[512,512]{1,0:T(8,128)(2,1)}, bf16[512,512]{1,0:T(8,128)(2,1)}, u32[]{:S(2)}, u32[]{:S(2)}) collective-permute-start(bf16[512,512]{1,0:T(8,128)(2,1)} %collective-permute-done.20.refs_1_), channel_id=1, source_target_pairs={{0,4},{1,5},{2,6},{3,7},{4,0},{5,1},{6,2},{7,3},{8,12},{9,13},{10,... | collective-permute-start | bytes 1572872 | tf_op jit(solution)/shard_map/ppermute | solution.py:101
  179.0 27.0 %collective-permute-start.29 = (bf16[512,512]{1,0:T(8,128)(2,1)S(1)}, bf16[512,512]{1,0:T(8,128)(2,1)S(1)}, u32[]{:S(2)}, u32[]{:S(2)}) collective-permute-start(bf16[512,512]{1,0:T(8,128)(2,1)S(1)} %pad_maximum_fusion.7.refs_0_), channel_id=1, source_target_pairs={{0,16},{1,17},{2,18},{3,19},{4,20},{5,21},{6,22},{7,23},{8,24},{9,... | collective-permute-start | bytes 1572872 | tf_op jit(solution)/shard_map/ppermute | solution.py:101
  180.2 25.8 %collective-permute-start.30 = (bf16[512,512]{1,0:T(8,128)(2,1)S(1)}, bf16[512,512]{1,0:T(8,128)(2,1)S(1)}, u32[]{:S(2)}, u32[]{:S(2)}) collective-permute-start(bf16[512,512]{1,0:T(8,128)(2,1)S(1)} %pad_maximum_fusion.7.refs_0_), channel_id=1, source_target_pairs={{0,4},{1,5},{2,6},{3,7},{4,0},{5,1},{6,2},{7,3},{8,12},{9,13},{10,... | collective-permute-start | bytes 1572872 | tf_op jit(solution)/shard_map/ppermute | solution.py:101
  181.8 24.3 %collective-permute-start.31 = (bf16[512,512]{1,0:T(8,128)(2,1)}, bf16[512,512]{1,0:T(8,128)(2,1)S(1)}, u32[]{:S(2)}, u32[]{:S(2)}) collective-permute-start(bf16[512,512]{1,0:T(8,128)(2,1)} %collective-permute-done.25.refs_1_), channel_id=1, source_target_pairs={{0,4},{1,5},{2,6},{3,7},{4,0},{5,1},{6,2},{7,3},{8,12},{9,13},{10,... | collective-permute-start | bytes 1572872 | tf_op jit(solution)/shard_map/ppermute | solution.py:101
  182.2 23.8 %collective-permute-start.32 = (bf16[672,256]{1,0:T(8,128)(2,1)S(1)}, bf16[672,256]{1,0:T(8,128)(2,1)S(1)}, u32[]{:S(2)}, u32[]{:S(2)}) collective-permute-start(bf16[672,256]{1,0:T(8,128)(2,1)S(1)} %copy-done.58), channel_id=1, source_target_pairs={{0,8},{1,9},{2,10},{3,11},{4,12},{5,13},{6,14},{7,15},{8,0},{9,1},... | collective-permute-start | bytes 1032200 | tf_op jit(solution)/shard_map/ppermute | solution.py:101
  209.6 26.5 %collective-permute-start.34 = (bf16[512,512]{1,0:T(8,128)(2,1)S(1)}, bf16[512,512]{1,0:T(8,128)(2,1)S(1)}, u32[]{:S(2)}, u32[]{:S(2)}) collective-permute-start(bf16[512,512]{1,0:T(8,128)(2,1)S(1)} %pad_maximum_fusion.8.refs_0_), channel_id=1, source_target_pairs={{0,16},{1,17},{2,18},{3,19},{4,20},{5,21},{6,22},{7,23},{8,24},{9,... | collective-permute-start | bytes 1572872 | tf_op jit(solution)/shard_map/ppermute | solution.py:101
  212.3 23.9 %collective-permute-start.35 = (bf16[512,512]{1,0:T(8,128)(2,1)S(1)}, bf16[512,512]{1,0:T(8,128)(2,1)S(1)}, u32[]{:S(2)}, u32[]{:S(2)}) collective-permute-start(bf16[512,512]{1,0:T(8,128)(2,1)S(1)} %pad_maximum_fusion.8.refs_0_), channel_id=1, source_target_pairs={{0,4},{1,5},{2,6},{3,7},{4,0},{5,1},{6,2},{7,3},{8,12},{9,13},{10,... | collective-permute-start | bytes 1572872 | tf_op jit(solution)/shard_map/ppermute | solution.py:101
  339.0 42.0 %collective-permute-start.62 = (bf16[192,512]{1,0:T(8,128)(2,1)S(1)}, bf16[192,512]{1,0:T(8,128)(2,1)S(1)}, u32[]{:S(2)}, u32[]{:S(2)}) collective-permute-start(bf16[192,512]{1,0:T(8,128)(2,1)S(1)} %get-tuple-element.247), channel_id=1, source_target_pairs={{0,8},{1,9},{2,10},{3,11},{4,12},{5,13},{6,14},{7,15},{8,0},{9,1},... | collective-permute-start | bytes 589832 | tf_op jit(solution)/shard_map/ppermute | solution.py:101
  339.8 42.9 %collective-permute-start.63 = (bf16[192,512]{1,0:T(8,128)(2,1)S(1)}, bf16[192,512]{1,0:T(8,128)(2,1)S(1)}, u32[]{:S(2)}, u32[]{:S(2)}) collective-permute-start(bf16[192,512]{1,0:T(8,128)(2,1)S(1)} %get-tuple-element.248), channel_id=1, source_target_pairs={{0,1},{1,0},{2,3},{3,2},{4,5},{5,4},{6,7},{7,6},{8,9},{9,8},{10,11... | collective-permute-start | bytes 589832 | tf_op jit(solution)/shard_map/ppermute | solution.py:101
  352.0 31.5 %collective-permute-start.66 = (bf16[192,512]{1,0:T(8,128)(2,1)S(1)}, bf16[192,512]{1,0:T(8,128)(2,1)S(1)}, u32[]{:S(2)}, u32[]{:S(2)}) collective-permute-start(bf16[192,512]{1,0:T(8,128)(2,1)S(1)} %get-tuple-element.265), channel_id=1, source_target_pairs={{0,8},{1,9},{2,10},{3,11},{4,12},{5,13},{6,14},{7,15},{8,0},{9,1},... | collective-permute-start | bytes 589832 | tf_op jit(solution)/shard_map/ppermute | solution.py:101
  (120 other events, 2098.4 us)

commit v3 on v2

--- a/solution.py
+++ b/solution.py
@@ -24,6 +24,7 @@
 MOVED = (4, 6, 7, 8, 8, 9, 10, 11)
 COMPUTED = (6, 7, 7, 8, 8, 9, 10, 11)
 GATHERED = (((0, 1, 2), 9), ((3, 4, 5), 10), ((6, 7), None))
+PIECES = ((0, 8), (8, 4), (12, 4))
 HIGHEST = lax.Precision.HIGHEST
 NO_COST = pl.CostEstimate(flops=0, bytes_accessed=0, transcendentals=0)
 
@@ -333,10 +334,9 @@
     )(*parts, id_place, teachers, *in_hbm(slopes), *gathered)
 
 
-def back_piece(place, grads, heads, piece, pieces):
+def back_piece(place, grads, heads, begin, steps):
     n = len(heads)
     rows, block = grads.shape[0], heads[0].shape[2]
-    steps = 16 // pieces
     half = rows // 4
 
     def kernel(place, grad, *refs):
@@ -366,7 +366,7 @@
             send_z[1] = rows_of(1 - zlo, 1 - x).astype(BF16)
 
     some = [
-        pl.BlockSpec((1, h.shape[1], block), lambda d, place: (piece % 2 * steps + d, 0, 0))
+        pl.BlockSpec((1, h.shape[1], block), lambda d, place: (begin % 8 + d, 0, 0))
         for h in heads
     ]
     last = steps // 2 - 1
@@ -393,31 +393,34 @@
             bytes_accessed=2 * grads.shape[1] * steps * block + 3 * rows * steps * block,
             transcendentals=0,
         ),
-        name=f"back{piece}",
+        name=f"back{begin}",
     )(place, in_vmem(grads), *in_hbm(*heads))
 
 
 def finish(places, pairs):
-    count = len(pairs)
-    rows, width = pairs[0][0].shape
-    blocks = 16 // count
-    block = width // blocks
+    rows = pairs[0][0].shape[0]
+    widths = [pair[0].shape[1] for pair in pairs]
+    block = sum(widths) // 16
     step = rows // 2
 
     def kernel(places, *refs):
         out = refs[-1]
-        for i in range(count):
-            for k in range(blocks):
+        at = 0
+        for i, width in enumerate(widths):
+            for k in range(width // block):
                 cols = slice(k * block, (k + 1) * block)
-                lanes = pl.ds(pl.multiple_of(places[i * blocks + k] * block, block), block)
+                lanes = pl.ds(pl.multiple_of(places[at + k] * block, block), block)
                 out[:, lanes] = refs[2 * i][:, cols] + refs[2 * i + 1][:, cols].astype(F32)
+            at += width // block
 
     return pl.pallas_call(
         kernel,
         grid_spec=pltpu.PrefetchScalarGridSpec(
             num_scalar_prefetch=1,
             grid=(rows // step,),
-            in_specs=[pl.BlockSpec((step, width), lambda r, places: (r, 0))] * (2 * count),
+            in_specs=[
+                pl.BlockSpec((step, width), lambda r, places: (r, 0)) for width in widths for _ in range(2)
+            ],
             out_specs=pl.BlockSpec((step, 16 * block), lambda r, places: (r, 0)),
         ),
         out_shape=jax.ShapeDtypeStruct((rows, 16 * block), F32),
@@ -578,8 +581,7 @@
         gathered,
     )
 
-    pieces = 4
-    pairs, first = [], [None] * pieces
+    pairs, first = [], [None] * len(PIECES)
 
     def second(i):
         (keep_x, came_x), (keep_z, came_z) = first[i]
@@ -592,14 +594,14 @@
         pairs.append((keep_x[0] + came_x[0].astype(F32), swap(mid_x, ZLO)))
         pairs.append((keep_z[0] + came_z[0].astype(F32), swap(mid_z, X)))
 
-    for i in range(pieces):
-        heads = [live["quads" if i < 2 else "across", g] for g in range(len(GROUPS))]
-        outs = back_piece(place, grads, heads, i, pieces)
+    for i, (begin, steps) in enumerate(PIECES):
+        heads = [live["quads" if begin < 8 else "across", g] for g in range(len(GROUPS))]
+        outs = back_piece(place, grads, heads, begin, steps)
         send_x, keep_x, send_z, keep_z, grads = lax.optimization_barrier((*outs, grads))
         first[i] = ((keep_x, swap(send_x, X)), (keep_z, swap(send_z, ZLO)))
         if i >= 1:
             second(i - 1)
-    second(pieces - 1)
+    second(len(PIECES) - 1)
     places = []
     for k in range(0, 16, 2):
         base = (me & ~4) ^ ORDER[k]

time: 395 us -> 394 us (level)
  waiting for transfers between devices: 138 us -> 143 us
  Pallas kernels: 138 us -> 134 us
    ppermute x76 -> x72, waiting for transfers between devices: 138 us -> 143 us  [swap(): return lax.ppermute(array, AXES, [(i, i ^ bits) for i in range(32)])]
    ppermute x76 -> x72, starting transfers between devices: 84.8 us -> 81.6 us  [swap(): return lax.ppermute(array, AXES, [(i, i ^ bits) for i in range(32)])]
    pallas_call x4 -> x3, Pallas kernels: 43.2 us -> 40.2 us  [back_piece(): pl.pallas_call(kernel, grid_spec=pltpu.PrefetchScalarGridSpec(num_scalar_...]
  transfers between devices with their start and end apart: 76 -> 72, of which waited for: 29 -> 31; matrix products, arithmetic and copies ran while one was open for 6% -> 6% of each run, Pallas kernels for 27% -> 25%
where the time goes in v3:
time: 394 us; the launch traced here: 393 us
  waiting for transfers between devices  143 us (36%)
  Pallas kernels  134 us (34%)
  starting transfers between devices  81.6 us (21%)
  other arithmetic  20 us (5%)
  local copies, waits for them, and re-layouts  11.8 us (3%)
    ppermute x72, waiting for transfers between devices, swap(): return lax.ppermute(array, AXES, [(i, i ^ bits) for i in range(32)])  143 us
    ppermute x72, starting transfers between devices, swap(): return lax.ppermute(array, AXES, [(i, i ^ bits) for i in range(32)])  81.6 us
    pallas_call x8, Pallas kernels, forward(): pl.pallas_call(kernel, grid_spec=pltpu.PrefetchScalarGridSpec(num_scalar_...  57.7 us
    pallas_call x3, Pallas kernels, back_piece(): pl.pallas_call(kernel, grid_spec=pltpu.PrefetchScalarGridSpec(num_scalar_...  40.2 us
    pallas_call x8, Pallas kernels, pack(): pl.pallas_call(kernel, grid=(ends[-1],), in_specs=specs, out_specs=pl.Blo...  22.8 us
    select_n x5, other arithmetic, columns_of(): jnp.where(low == 0, head[first:first + size], head[share + first:share +...  9.85 us
    pallas_call x1, Pallas kernels, margins(): pl.pallas_call(kernel, grid=(tiles // batch,), in_specs=[square] * 4 + [l...  8.47 us
  transfers between devices with their start and end apart: 72, of which 31 were waited for; matrix products, arithmetic and copies ran while one was open for 6% of the time, Pallas kernels for 25%

profile of v3, /device:TPU:0, one launch (start us, length us, event | category | flops | bytes accessed | tf_op | source)
XLA Modules:
  0.0 393.1 jit_solution(2037661041407225469)
XLA Ops:
  20.1 9.2 %collective-permute-done.1.refs_1_ = bf16[256,512]{1,0:T(8,128)(2,1)S(1)} collective-permute-done((bf16[256,512]{1,0:T(8,128)(2,1)S(1)}, bf16[256,512]{1,0:T(8,128)(2,1)S(1)}, u32[]{:S(2)}, u32[]{:S(2)}) %collective-permute-start.1) | collective-permute-done | bytes 262176 | tf_op jit(solution)/shard_map/ppermute | solution.py:102
  39.2 20.4 %collective-permute-done.9 = f32[8,18]{1,0:T(8,128)S(1)} collective-permute-done((f32[8,18]{1,0:T(8,128)S(1)}, f32[8,18]{1,0:T(8,128)S(1)}, u32[]{:S(2)}, u32[]{:S(2)}) %collective-permute-start.9) | collective-permute-done | bytes 608 | tf_op jit(solution)/shard_map/ppermute | solution.py:102
  69.9 15.4 %collective-permute-done.10.refs_5_ = bf16[512,512]{1,0:T(8,128)(2,1)S(1)} collective-permute-done((bf16[512,512]{1,0:T(8,128)(2,1)S(1)}, bf16[512,512]{1,0:T(8,128)(2,1)S(1)}, u32[]{:S(2)}, u32[]{:S(2)}) %collective-permute-start.10) | collective-permute-done | bytes 524320 | tf_op jit(solution)/shard_map/ppermute | solution.py:102
  93.0 23.9 %collective-permute-done.15.refs_1_ = bf16[512,512]{1,0:T(8,128)(2,1)S(1)} collective-permute-done((bf16[512,512]{1,0:T(8,128)(2,1)S(1)}, bf16[512,512]{1,0:T(8,128)(2,1)S(1)}, u32[]{:S(2)}, u32[]{:S(2)}) %collective-permute-start.15) | collective-permute-done | bytes 524320 | tf_op jit(solution)/shard_map/ppermute | solution.py:102
  126.5 5.4 %pack.9.near.refs_1_ = bf16[8,1024,256]{2,1,0:T(8,128)(2,1)} custom-call(bf16[512,512]{1,0:T(8,128)(2,1)} %copy-done.22, bf16[512,512]{1,0:T(8,128)(2,1)} %copy-done.39, bf16[512,512]{1,0:T(8,128)(2,1)} %copy-done.40, bf16[512,512]{1,0:T(8,128)(2,1)} %copy-done.43, bf16[512,512]{1,0:T(8,128)(2,1)} %copy-done.23, bf16[512,512]{1,0:T(8,128)(2,1)} %copy-done.41, ...), custom_call_target="tpu_custom_call" | custom-call | tf_op jit(solution)/shard_map/pack/pallas_call | solution.py:180
  131.9 13.9 %collective-permute-done.20.refs_1_ = bf16[512,512]{1,0:T(8,128)(2,1)} collective-permute-done((bf16[512,512]{1,0:T(8,128)(2,1)S(1)}, bf16[512,512]{1,0:T(8,128)(2,1)}, u32[]{:S(2)}, u32[]{:S(2)}) %collective-permute-start.20) | collective-permute-done | bytes 524320 | tf_op jit(solution)/shard_map/ppermute | solution.py:102
  160.4 5.1 %forward0.1 = (f32[16,768,256]{2,1,0:T(8,128)}, f32[2,8,256]{2,1,0:T(8,128)S(1)}) custom-call(s32[16]{0:T(128)S(1)} %reshape.45.lens, bf16[768,4096]{1,0:T(8,128)(2,1)S(1)} %arrange.1.rows, bf16[8,256,256]{2,1,0:T(8,128)(2,1)} %pack.8.near.refs_0_, bf16[8,256,256]{2,1,0:T(8,128)(2,1)S(1)} %copy-done.7, f32[1,4096]{1,0:T(1,128)S(1)} %bitcast.69), custom_call_target="tpu_custom_call" | custom-call | tf_op jit(solution)/shard_map/forward0/pallas_call | solution.py:231
  165.5 12.7 %collective-permute-done.25.refs_1_ = bf16[512,512]{1,0:T(8,128)(2,1)} collective-permute-done((bf16[512,512]{1,0:T(8,128)(2,1)}, bf16[512,512]{1,0:T(8,128)(2,1)}, u32[]{:S(2)}, u32[]{:S(2)}) %collective-permute-start.25) | collective-permute-done | bytes 524320 | tf_op jit(solution)/shard_map/ppermute | solution.py:102
  183.9 11.6 %forward256.1 = (f32[16,768,256]{2,1,0:T(8,128)}, f32[2,8,1024]{2,1,0:T(8,128)S(1)}) custom-call(s32[16]{0:T(128)S(1)} %reshape.45.lens, bf16[768,4096]{1,0:T(8,128)(2,1)S(1)} %arrange.1.rows, bf16[8,1024,256]{2,1,0:T(8,128)(2,1)} %pack.9.near.refs_1_, bf16[8,1024,256]{2,1,0:T(8,128)(2,1)} %collective-permute-done.28.across.refs_1_, ...), custom_call_target="tpu_custom_call", output_to_operand_aliasing={{0}: (5, {})} | custom-call | tf_op jit(solution)/shard_map/forward256/pallas_call | solution.py:231
  198.1 7.8 %forward1280.1 = (f32[16,768,256]{2,1,0:T(8,128)}, f32[2,8,512]{2,1,0:T(8,128)S(1)}) custom-call(s32[16]{0:T(128)S(1)} %reshape.45.lens, bf16[768,4096]{1,0:T(8,128)(2,1)S(1)} %arrange.1.rows, bf16[8,512,256]{2,1,0:T(8,128)(2,1)} %pack.10.near.refs_2_, ...), custom_call_target="tpu_custom_call", output_to_operand_aliasing={{0}: (5, {})} | custom-call | tf_op jit(solution)/shard_map/forward1280/pallas_call | solution.py:231
  215.1 7.2 %forward1792.1 = (f32[16,768,256]{2,1,0:T(8,128)}, f32[2,8,512]{2,1,0:T(8,128)S(1)}) custom-call(s32[16]{0:T(128)S(1)} %reshape.45.lens, bf16[768,4096]{1,0:T(8,128)(2,1)S(1)} %arrange.1.rows, bf16[8,512,256]{2,1,0:T(8,128)(2,1)} %pack.11.near.refs_3_, ...), custom_call_target="tpu_custom_call", output_to_operand_aliasing={{0}: (5, {})} | custom-call | tf_op jit(solution)/shard_map/forward1792/pallas_call | solution.py:231
  222.3 7.1 %forward2304.1 = (f32[16,768,256]{2,1,0:T(8,128)}, f32[2,8,512]{2,1,0:T(8,128)S(1)}) custom-call(s32[16]{0:T(128)S(1)} %reshape.45.lens, bf16[768,4096]{1,0:T(8,128)(2,1)S(1)} %arrange.1.rows, bf16[8,512,256]{2,1,0:T(8,128)(2,1)} %pack.12.near.refs_4_, ...), custom_call_target="tpu_custom_call", output_to_operand_aliasing={{0}: (5, {})} | custom-call | tf_op jit(solution)/shard_map/forward2304/pallas_call | solution.py:231
  229.4 6.5 %collective-permute-done.34.refs_1_ = bf16[512,512]{1,0:T(8,128)(2,1)S(1)} collective-permute-done((bf16[512,512]{1,0:T(8,128)(2,1)S(1)}, bf16[512,512]{1,0:T(8,128)(2,1)S(1)}, u32[]{:S(2)}, u32[]{:S(2)}) %collective-permute-start.34) | collective-permute-done | bytes 524320 | tf_op jit(solution)/shard_map/ppermute | solution.py:102
  245.8 7.2 %forward2816.1 = (f32[16,768,256]{2,1,0:T(8,128)}, f32[2,8,512]{2,1,0:T(8,128)S(1)}) custom-call(s32[16]{0:T(128)S(1)} %reshape.45.lens, bf16[768,4096]{1,0:T(8,128)(2,1)S(1)} %arrange.1.rows, bf16[8,512,256]{2,1,0:T(8,128)(2,1)} %pack.13.near.refs_5_, ...), custom_call_target="tpu_custom_call", output_to_operand_aliasing={{0}: (5, {})} | custom-call | tf_op jit(solution)/shard_map/forward2816/pallas_call | solution.py:231
  253.0 5.0 %collective-permute-done.43 = f32[2,8,1792]{2,1,0:T(8,128)S(1)} collective-permute-done((f32[2,8,1792]{2,1,0:T(8,128)S(1)}, f32[2,8,1792]{2,1,0:T(8,128)S(1)}, u32[]{:S(2)}, u32[]{:S(2)}) %collective-permute-start.43) | collective-permute-done | bytes 114720 | tf_op jit(solution)/shard_map/ppermute | solution.py:102
  266.4 7.1 %forward3328.1 = (f32[16,768,256]{2,1,0:T(8,128)}, f32[2,8,512]{2,1,0:T(8,128)S(1)}) custom-call(s32[16]{0:T(128)S(1)} %reshape.45.lens, bf16[768,4096]{1,0:T(8,128)(2,1)S(1)} %arrange.1.rows, bf16[8,512,256]{2,1,0:T(8,128)(2,1)} %pack.14.near.refs_6_, ...), custom_call_target="tpu_custom_call", output_to_operand_aliasing={{0}: (5, {})} | custom-call | tf_op jit(solution)/shard_map/forward3328/pallas_call | solution.py:231
  279.0 4.7 %forward3840.1 = (f32[16,768,256]{2,1,0:T(8,128)}, f32[2,8,256]{2,1,0:T(8,128)S(1)}) custom-call(s32[16]{0:T(128)S(1)} %reshape.45.lens, bf16[768,4096]{1,0:T(8,128)(2,1)S(1)} %arrange.1.rows, bf16[8,160,256]{2,1,0:T(8,128)(2,1)} %pack.15.near.refs_7_, ...), custom_call_target="tpu_custom_call", output_to_operand_aliasing={{0}: (5, {})} | custom-call | tf_op jit(solution)/shard_map/forward3840/pallas_call | solution.py:231
  304.1 8.5 %margins.1 = (f32[64,8]{1,0:T(8,128)S(1)}, bf16[768,4096]{1,0:T(8,128)(2,1)S(1)}) custom-call(f32[64,64]{1,0:T(8,128)S(1)} %fusion.s0, f32[64,64]{1,0:T(8,128)S(1)} %collective-permute-done.57.s1, f32[64,64]{1,0:T(8,128)S(1)} %collective-permute-done.58.s2, f32[64,64]{1,0:T(8,128)S(1)} %collective-permute-done.59.s3, s32[64,8]{1,0:T(8,128)S(1)} %fusion.9.ids, ...), custom_call_target="tpu_custom_call" | custom-call | tf_op jit(solution)/shard_map/margins/pallas_call | solution.py:319
  312.5 18.6 %back0.1 = (bf16[2,192,1024]{2,1,0:T(8,128)(2,1)}, f32[2,192,1024]{2,1,0:T(8,128)}, bf16[2,192,1024]{2,1,0:T(8,128)(2,1)}, f32[2,192,1024]{2,1,0:T(8,128)}) custom-call(s32[2]{0:T(128)S(1)} %pad_add_fusion.1.place, bf16[768,4096]{1,0:T(8,128)(2,1)S(1)} %get-tuple-element.249.grad, bf16[8,256,256]{2,1,0:T(8,128)(2,1)} %pack.8.near.refs_0_, ...), custom_call_target="tpu_custom_call" | custom-call | flops 12884901888 | bytes 21495808 | tf_op jit(solution)/shard_map/back0/pallas_call | solution.py:380
  332.5 11.0 %back8.1 = (bf16[2,192,512]{2,1,0:T(8,128)(2,1)}, f32[2,192,512]{2,1,0:T(8,128)}, bf16[2,192,512]{2,1,0:T(8,128)(2,1)}, f32[2,192,512]{2,1,0:T(8,128)}) custom-call(s32[2]{0:T(128)S(1)} %pad_add_fusion.1.place, bf16[768,4096]{1,0:T(8,128)(2,1)S(1)} %get-tuple-element.249.grad, bf16[8,256,256]{2,1,0:T(8,128)(2,1)} %copy-done.6, ...), custom_call_target="tpu_custom_call" | custom-call | flops 6442450944 | bytes 10747904 | tf_op jit(solution)/shard_map/back8/pallas_call | solution.py:380
  346.3 5.6 %collective-permute-done.60 = bf16[2,192,1024]{2,1,0:T(8,128)(2,1)S(1)} collective-permute-done((bf16[2,192,1024]{2,1,0:T(8,128)(2,1)}, bf16[2,192,1024]{2,1,0:T(8,128)(2,1)S(1)}, u32[]{:S(2)}, u32[]{:S(2)}) %collective-permute-start.60) | collective-permute-done | bytes 786464 | tf_op jit(solution)/shard_map/ppermute | solution.py:102
  353.9 10.7 %back12.1 = (bf16[2,192,512]{2,1,0:T(8,128)(2,1)}, f32[2,192,512]{2,1,0:T(8,128)}, bf16[2,192,512]{2,1,0:T(8,128)(2,1)}, f32[2,192,512]{2,1,0:T(8,128)}) custom-call(s32[2]{0:T(128)S(1)} %pad_add_fusion.1.place, bf16[768,4096]{1,0:T(8,128)(2,1)S(1)} %get-tuple-element.249.grad, bf16[8,256,256]{2,1,0:T(8,128)(2,1)} %copy-done.6, ...), custom_call_target="tpu_custom_call" | custom-call | flops 6442450944 | bytes 10747904 | tf_op jit(solution)/shard_map/back12/pallas_call | solution.py:380
  370.5 6.2 %collective-permute-done.68 = bf16[2,192,512]{2,1,0:T(8,128)(2,1)S(1)} collective-permute-done((bf16[2,192,512]{2,1,0:T(8,128)(2,1)}, bf16[2,192,512]{2,1,0:T(8,128)(2,1)S(1)}, u32[]{:S(2)}, u32[]{:S(2)}) %collective-permute-start.68) | collective-permute-done | bytes 393248 | tf_op jit(solution)/shard_map/ppermute | solution.py:102
  389.7 3.5 finish.1
  (348 shorter events, 157.6 us)
Async XLA Ops:
  30.2 30.1 %collective-permute-start.8 = (bf16[96,4096]{1,0:T(8,128)(2,1)S(1)}, bf16[96,4096]{1,0:T(8,128)(2,1)S(1)}, u32[]{:S(2)}, u32[]{:S(2)}) collective-permute-start(bf16[96,4096]{1,0:T(8,128)(2,1)S(1)} %get-tuple-element.134), channel_id=1, source_target_pairs={{0,8},{1,9},{2,10},{3,11},{4,12},{5,13},{6,14},{7,15},{8,0},{9,1},... | collective-permute-start | bytes 2359304 | tf_op jit(solution)/shard_map/ppermute | solution.py:102
  34.1 25.5 %collective-permute-start.5 = (bf16[512,512]{1,0:T(8,128)(2,1)S(1)}, bf16[512,512]{1,0:T(8,128)(2,1)S(1)}, u32[]{:S(2)}, u32[]{:S(2)}) collective-permute-start(bf16[512,512]{1,0:T(8,128)(2,1)S(1)} %pad_maximum_fusion.2.refs_0_), channel_id=1, source_target_pairs={{0,16},{1,17},{2,18},{3,19},{4,20},{5,21},{6,22},{7,23},{8,24},{9,... | collective-permute-start | bytes 1572872 | tf_op jit(solution)/shard_map/ppermute | solution.py:102
  35.7 23.9 %collective-permute-start.6 = (bf16[512,512]{1,0:T(8,128)(2,1)S(1)}, bf16[512,512]{1,0:T(8,128)(2,1)S(1)}, u32[]{:S(2)}, u32[]{:S(2)}) collective-permute-start(bf16[512,512]{1,0:T(8,128)(2,1)S(1)} %pad_maximum_fusion.2.refs_0_), channel_id=1, source_target_pairs={{0,4},{1,5},{2,6},{3,7},{4,0},{5,1},{6,2},{7,3},{8,12},{9,13},{10,... | collective-permute-start | bytes 1572872 | tf_op jit(solution)/shard_map/ppermute | solution.py:102
  60.3 26.2 %collective-permute-start.14 = (bf16[96,4096]{1,0:T(8,128)(2,1)S(1)}, bf16[96,4096]{1,0:T(8,128)(2,1)S(1)}, u32[]{:S(2)}, u32[]{:S(2)}) collective-permute-start(bf16[96,4096]{1,0:T(8,128)(2,1)S(1)} %collective-permute-done.8.refs_0_), channel_id=1, source_target_pairs={{0,1},{1,0},{2,3},{3,2},{4,5},{5,4},{6,7},{7,6},{8,9},{9,8},{10,11... | collective-permute-start | bytes 2359304 | tf_op jit(solution)/shard_map/ppermute | solution.py:102
  61.8 23.5 %collective-permute-start.10 = (bf16[512,512]{1,0:T(8,128)(2,1)S(1)}, bf16[512,512]{1,0:T(8,128)(2,1)S(1)}, u32[]{:S(2)}, u32[]{:S(2)}) collective-permute-start(bf16[512,512]{1,0:T(8,128)(2,1)S(1)} %pad_maximum_fusion.3.refs_4_), channel_id=1, source_target_pairs={{0,16},{1,17},{2,18},{3,19},{4,20},{5,21},{6,22},{7,23},{8,24},{9,... | collective-permute-start | bytes 1572872 | tf_op jit(solution)/shard_map/ppermute | solution.py:102
  86.5 31.3 %collective-permute-start.19 = (bf16[8,256,256]{2,1,0:T(8,128)(2,1)}, bf16[8,256,256]{2,1,0:T(8,128)(2,1)S(1)}, u32[]{:S(2)}, u32[]{:S(2)}) collective-permute-start(bf16[8,256,256]{2,1,0:T(8,128)(2,1)} %pack.8.near.refs_0_), channel_id=1, source_target_pairs={{0,2},{1,3},{2,0},{3,1},{4,6},{5,7},{6,4},{7,5},{8,10},{9,11},{10,... | collective-permute-start | bytes 3145736 | tf_op jit(solution)/shard_map/ppermute | solution.py:102
  86.6 31.2 %collective-permute-start.18 = (bf16[96,4096]{1,0:T(8,128)(2,1)S(1)}, bf16[96,4096]{1,0:T(8,128)(2,1)S(1)}, u32[]{:S(2)}, u32[]{:S(2)}) collective-permute-start(bf16[96,4096]{1,0:T(8,128)(2,1)S(1)} %get-tuple-element.144), channel_id=1, source_target_pairs={{0,8},{1,9},{2,10},{3,11},{4,12},{5,13},{6,14},{7,15},{8,0},{9,1},... | collective-permute-start | bytes 2359304 | tf_op jit(solution)/shard_map/ppermute | solution.py:102
  88.3 28.6 %collective-permute-start.15 = (bf16[512,512]{1,0:T(8,128)(2,1)S(1)}, bf16[512,512]{1,0:T(8,128)(2,1)S(1)}, u32[]{:S(2)}, u32[]{:S(2)}) collective-permute-start(bf16[512,512]{1,0:T(8,128)(2,1)S(1)} %pad_maximum_fusion.4.refs_0_), channel_id=1, source_target_pairs={{0,16},{1,17},{2,18},{3,19},{4,20},{5,21},{6,22},{7,23},{8,24},{9,... | collective-permute-start | bytes 1572872 | tf_op jit(solution)/shard_map/ppermute | solution.py:102
  91.0 25.9 %collective-permute-start.16 = (bf16[512,512]{1,0:T(8,128)(2,1)S(1)}, bf16[512,512]{1,0:T(8,128)(2,1)S(1)}, u32[]{:S(2)}, u32[]{:S(2)}) collective-permute-start(bf16[512,512]{1,0:T(8,128)(2,1)S(1)} %pad_maximum_fusion.4.refs_0_), channel_id=1, source_target_pairs={{0,4},{1,5},{2,6},{3,7},{4,0},{5,1},{6,2},{7,3},{8,12},{9,13},{10,... | collective-permute-start | bytes 1572872 | tf_op jit(solution)/shard_map/ppermute | solution.py:102
  92.5 24.4 %collective-permute-start.17 = (bf16[512,512]{1,0:T(8,128)(2,1)S(1)}, bf16[512,512]{1,0:T(8,128)(2,1)S(1)}, u32[]{:S(2)}, u32[]{:S(2)}) collective-permute-start(bf16[512,512]{1,0:T(8,128)(2,1)S(1)} %collective-permute-done.10.refs_5_), channel_id=1, source_target_pairs={{0,4},{1,5},{2,6},{3,7},{4,0},{5,1},{6,2},{7,3},{8,12},{9,13},{10,... | collective-permute-start | bytes 1572872 | tf_op jit(solution)/shard_map/ppermute | solution.py:102
  118.8 28.3 %collective-permute-start.24 = (bf16[96,4096]{1,0:T(8,128)(2,1)S(1)}, bf16[96,4096]{1,0:T(8,128)(2,1)S(1)}, u32[]{:S(2)}, u32[]{:S(2)}) collective-permute-start(bf16[96,4096]{1,0:T(8,128)(2,1)S(1)} %collective-permute-done.18.refs_1_), channel_id=1, source_target_pairs={{0,1},{1,0},{2,3},{3,2},{4,5},{5,4},{6,7},{7,6},{8,9},{9,8},{10,11... | collective-permute-start | bytes 2359304 | tf_op jit(solution)/shard_map/ppermute | solution.py:102
  120.3 25.6 %collective-permute-start.20 = (bf16[512,512]{1,0:T(8,128)(2,1)S(1)}, bf16[512,512]{1,0:T(8,128)(2,1)}, u32[]{:S(2)}, u32[]{:S(2)}) collective-permute-start(bf16[512,512]{1,0:T(8,128)(2,1)S(1)} %pad_maximum_fusion.5.refs_0_), channel_id=1, source_target_pairs={{0,16},{1,17},{2,18},{3,19},{4,20},{5,21},{6,22},{7,23},{8,24},{9,... | collective-permute-start | bytes 1572872 | tf_op jit(solution)/shard_map/ppermute | solution.py:102
  122.9 22.9 %collective-permute-start.21 = (bf16[512,512]{1,0:T(8,128)(2,1)S(1)}, bf16[512,512]{1,0:T(8,128)(2,1)S(1)}, u32[]{:S(2)}, u32[]{:S(2)}) collective-permute-start(bf16[512,512]{1,0:T(8,128)(2,1)S(1)} %pad_maximum_fusion.5.refs_0_), channel_id=1, source_target_pairs={{0,4},{1,5},{2,6},{3,7},{4,0},{5,1},{6,2},{7,3},{8,12},{9,13},{10,... | collective-permute-start | bytes 1572872 | tf_op jit(solution)/shard_map/ppermute | solution.py:102
  148.0 30.9 %collective-permute-start.28 = (bf16[8,1024,256]{2,1,0:T(8,128)(2,1)}, bf16[8,1024,256]{2,1,0:T(8,128)(2,1)}, u32[]{:S(2)}, u32[]{:S(2)}) collective-permute-start(bf16[8,1024,256]{2,1,0:T(8,128)(2,1)} %pack.9.near.refs_1_), channel_id=1, source_target_pairs={{0,2},{1,3},{2,0},{3,1},{4,6},{5,7},{6,4},{7,5},{8,10},{9,11},{10,... | collective-permute-start | bytes 12582920 | tf_op jit(solution)/shard_map/ppermute | solution.py:102
  151.5 26.8 %collective-permute-start.25 = (bf16[512,512]{1,0:T(8,128)(2,1)}, bf16[512,512]{1,0:T(8,128)(2,1)}, u32[]{:S(2)}, u32[]{:S(2)}) collective-permute-start(bf16[512,512]{1,0:T(8,128)(2,1)} %pad_maximum_fusion.6.refs_0_), channel_id=1, source_target_pairs={{0,16},{1,17},{2,18},{3,19},{4,20},{5,21},{6,22},{7,23},{8,24},{9,... | collective-permute-start | bytes 1572872 | tf_op jit(solution)/shard_map/ppermute | solution.py:102
  153.3 24.9 %collective-permute-start.26 = (bf16[512,512]{1,0:T(8,128)(2,1)}, bf16[512,512]{1,0:T(8,128)(2,1)}, u32[]{:S(2)}, u32[]{:S(2)}) collective-permute-start(bf16[512,512]{1,0:T(8,128)(2,1)} %pad_maximum_fusion.6.refs_0_), channel_id=1, source_target_pairs={{0,4},{1,5},{2,6},{3,7},{4,0},{5,1},{6,2},{7,3},{8,12},{9,13},{10,... | collective-permute-start | bytes 1572872 | tf_op jit(solution)/shard_map/ppermute | solution.py:102
  154.8 24.1 %collective-permute-start.27 = (bf16[512,512]{1,0:T(8,128)(2,1)}, bf16[512,512]{1,0:T(8,128)(2,1)}, u32[]{:S(2)}, u32[]{:S(2)}) collective-permute-start(bf16[512,512]{1,0:T(8,128)(2,1)} %collective-permute-done.20.refs_1_), channel_id=1, source_target_pairs={{0,4},{1,5},{2,6},{3,7},{4,0},{5,1},{6,2},{7,3},{8,12},{9,13},{10,... | collective-permute-start | bytes 1572872 | tf_op jit(solution)/shard_map/ppermute | solution.py:102
  178.9 26.9 %collective-permute-start.29 = (bf16[512,512]{1,0:T(8,128)(2,1)S(1)}, bf16[512,512]{1,0:T(8,128)(2,1)S(1)}, u32[]{:S(2)}, u32[]{:S(2)}) collective-permute-start(bf16[512,512]{1,0:T(8,128)(2,1)S(1)} %pad_maximum_fusion.7.refs_0_), channel_id=1, source_target_pairs={{0,16},{1,17},{2,18},{3,19},{4,20},{5,21},{6,22},{7,23},{8,24},{9,... | collective-permute-start | bytes 1572872 | tf_op jit(solution)/shard_map/ppermute | solution.py:102
  180.1 25.8 %collective-permute-start.30 = (bf16[512,512]{1,0:T(8,128)(2,1)S(1)}, bf16[512,512]{1,0:T(8,128)(2,1)S(1)}, u32[]{:S(2)}, u32[]{:S(2)}) collective-permute-start(bf16[512,512]{1,0:T(8,128)(2,1)S(1)} %pad_maximum_fusion.7.refs_0_), channel_id=1, source_target_pairs={{0,4},{1,5},{2,6},{3,7},{4,0},{5,1},{6,2},{7,3},{8,12},{9,13},{10,... | collective-permute-start | bytes 1572872 | tf_op jit(solution)/shard_map/ppermute | solution.py:102
  181.6 24.3 %collective-permute-start.31 = (bf16[512,512]{1,0:T(8,128)(2,1)}, bf16[512,512]{1,0:T(8,128)(2,1)S(1)}, u32[]{:S(2)}, u32[]{:S(2)}) collective-permute-start(bf16[512,512]{1,0:T(8,128)(2,1)} %collective-permute-done.25.refs_1_), channel_id=1, source_target_pairs={{0,4},{1,5},{2,6},{3,7},{4,0},{5,1},{6,2},{7,3},{8,12},{9,13},{10,... | collective-permute-start | bytes 1572872 | tf_op jit(solution)/shard_map/ppermute | solution.py:102
  182.1 23.8 %collective-permute-start.32 = (bf16[672,256]{1,0:T(8,128)(2,1)S(1)}, bf16[672,256]{1,0:T(8,128)(2,1)S(1)}, u32[]{:S(2)}, u32[]{:S(2)}) collective-permute-start(bf16[672,256]{1,0:T(8,128)(2,1)S(1)} %copy-done.56), channel_id=1, source_target_pairs={{0,8},{1,9},{2,10},{3,11},{4,12},{5,13},{6,14},{7,15},{8,0},{9,1},... | collective-permute-start | bytes 1032200 | tf_op jit(solution)/shard_map/ppermute | solution.py:102
  209.4 26.5 %collective-permute-start.34 = (bf16[512,512]{1,0:T(8,128)(2,1)S(1)}, bf16[512,512]{1,0:T(8,128)(2,1)S(1)}, u32[]{:S(2)}, u32[]{:S(2)}) collective-permute-start(bf16[512,512]{1,0:T(8,128)(2,1)S(1)} %pad_maximum_fusion.8.refs_0_), channel_id=1, source_target_pairs={{0,16},{1,17},{2,18},{3,19},{4,20},{5,21},{6,22},{7,23},{8,24},{9,... | collective-permute-start | bytes 1572872 | tf_op jit(solution)/shard_map/ppermute | solution.py:102
  212.1 23.9 %collective-permute-start.35 = (bf16[512,512]{1,0:T(8,128)(2,1)S(1)}, bf16[512,512]{1,0:T(8,128)(2,1)S(1)}, u32[]{:S(2)}, u32[]{:S(2)}) collective-permute-start(bf16[512,512]{1,0:T(8,128)(2,1)S(1)} %pad_maximum_fusion.8.refs_0_), channel_id=1, source_target_pairs={{0,4},{1,5},{2,6},{3,7},{4,0},{5,1},{6,2},{7,3},{8,12},{9,13},{10,... | collective-permute-start | bytes 1572872 | tf_op jit(solution)/shard_map/ppermute | solution.py:102
  213.6 23.7 %collective-permute-start.36 = (bf16[512,512]{1,0:T(8,128)(2,1)S(1)}, bf16[512,512]{1,0:T(8,128)(2,1)S(1)}, u32[]{:S(2)}, u32[]{:S(2)}) collective-permute-start(bf16[512,512]{1,0:T(8,128)(2,1)S(1)} %collective-permute-done.29.refs_1_), channel_id=1, source_target_pairs={{0,4},{1,5},{2,6},{3,7},{4,0},{5,1},{6,2},{7,3},{8,12},{9,13},{10,... | collective-permute-start | bytes 1572872 | tf_op jit(solution)/shard_map/ppermute | solution.py:102
  (114 other events, 2046.5 us)

commit v4 on v3

--- a/solution.py
+++ b/solution.py
@@ -565,8 +565,8 @@
     id_place = (group * 2 + ((owner >> 2) & 1)) * count + ids % count
 
     late = reps_of(GATHERED[-1][0])
-    for bits in (ZHI, Y, CORE):
-        late = jnp.concatenate([late, swap(late, bits)], axis=1)
+    late = jnp.concatenate([late] + [swap(late, bits) for bits in (ZHI, Y, ZHI | Y)], axis=1)
+    late = jnp.concatenate([late, swap(late, CORE)], axis=1)
     gathered = [live["gathered", groups] for groups, _ in GATHERED[:-1]] + [late]
 
     def scores(reps):

time: 394 us -> 393 us (level)
    ppermute x72 -> x73, waiting for transfers between devices: 143 us -> 141 us  [swap(): return lax.ppermute(array, AXES, [(i, i ^ bits) for i in range(32)])]
    ppermute x72 -> x73, starting transfers between devices: 81.6 us -> 82.1 us  [swap(): return lax.ppermute(array, AXES, [(i, i ^ bits) for i in range(32)])]
  transfers between devices with their start and end apart: 72 -> 73, of which waited for: 31 -> 31; matrix products, arithmetic and copies ran while one was open for 6% -> 6% of each run, Pallas kernels for 25% -> 25%
where the time goes in v4:
time: 393 us; the launch traced here: 392 us
  waiting for transfers between devices  141 us (36%)
  Pallas kernels  134 us (34%)
  starting transfers between devices  82.1 us (21%)
  other arithmetic  19.9 us (5%)
  local copies, waits for them, and re-layouts  11.8 us (3%)
    ppermute x73, waiting for transfers between devices, swap(): return lax.ppermute(array, AXES, [(i, i ^ bits) for i in range(32)])  141 us
    ppermute x73, starting transfers between devices, swap(): return lax.ppermute(array, AXES, [(i, i ^ bits) for i in range(32)])  82.1 us
    pallas_call x8, Pallas kernels, forward(): pl.pallas_call(kernel, grid_spec=pltpu.PrefetchScalarGridSpec(num_scalar_...  57.7 us
    pallas_call x3, Pallas kernels, back_piece(): pl.pallas_call(kernel, grid_spec=pltpu.PrefetchScalarGridSpec(num_scalar_...  40.2 us
    pallas_call x8, Pallas kernels, pack(): pl.pallas_call(kernel, grid=(ends[-1],), in_specs=specs, out_specs=pl.Blo...  22.8 us
    select_n x5, other arithmetic, columns_of(): jnp.where(low == 0, head[first:first + size], head[share + first:share +...  9.84 us
    pallas_call x1, Pallas kernels, margins(): pl.pallas_call(kernel, grid=(tiles // batch,), in_specs=[square] * 4 + [l...  8.47 us
  transfers between devices with their start and end apart: 73, of which 31 were waited for; matrix products, arithmetic and copies ran while one was open for 6% of the time, Pallas kernels for 25%

profile of v4, /device:TPU:0, one launch (start us, length us, event | category | flops | bytes accessed | tf_op | source)
XLA Modules:
  0.0 391.9 jit_solution(3432863308325815949)
XLA Ops:
  20.1 9.2 %collective-permute-done.1.refs_1_ = bf16[256,512]{1,0:T(8,128)(2,1)S(1)} collective-permute-done((bf16[256,512]{1,0:T(8,128)(2,1)S(1)}, bf16[256,512]{1,0:T(8,128)(2,1)S(1)}, u32[]{:S(2)}, u32[]{:S(2)}) %collective-permute-start.1) | collective-permute-done | bytes 262176 | tf_op jit(solution)/shard_map/ppermute | solution.py:102
  39.2 20.4 %collective-permute-done.9 = f32[8,18]{1,0:T(8,128)S(1)} collective-permute-done((f32[8,18]{1,0:T(8,128)S(1)}, f32[8,18]{1,0:T(8,128)S(1)}, u32[]{:S(2)}, u32[]{:S(2)}) %collective-permute-start.9) | collective-permute-done | bytes 608 | tf_op jit(solution)/shard_map/ppermute | solution.py:102
  69.9 15.4 %collective-permute-done.10.refs_5_ = bf16[512,512]{1,0:T(8,128)(2,1)S(1)} collective-permute-done((bf16[512,512]{1,0:T(8,128)(2,1)S(1)}, bf16[512,512]{1,0:T(8,128)(2,1)S(1)}, u32[]{:S(2)}, u32[]{:S(2)}) %collective-permute-start.10) | collective-permute-done | bytes 524320 | tf_op jit(solution)/shard_map/ppermute | solution.py:102
  93.0 23.9 %collective-permute-done.15.refs_1_ = bf16[512,512]{1,0:T(8,128)(2,1)S(1)} collective-permute-done((bf16[512,512]{1,0:T(8,128)(2,1)S(1)}, bf16[512,512]{1,0:T(8,128)(2,1)S(1)}, u32[]{:S(2)}, u32[]{:S(2)}) %collective-permute-start.15) | collective-permute-done | bytes 524320 | tf_op jit(solution)/shard_map/ppermute | solution.py:102
  126.5 5.4 %pack.9.near.refs_1_ = bf16[8,1024,256]{2,1,0:T(8,128)(2,1)} custom-call(bf16[512,512]{1,0:T(8,128)(2,1)} %copy-done.22, bf16[512,512]{1,0:T(8,128)(2,1)} %copy-done.39, bf16[512,512]{1,0:T(8,128)(2,1)} %copy-done.40, bf16[512,512]{1,0:T(8,128)(2,1)} %copy-done.43, bf16[512,512]{1,0:T(8,128)(2,1)} %copy-done.23, bf16[512,512]{1,0:T(8,128)(2,1)} %copy-done.41, ...), custom_call_target="tpu_custom_call" | custom-call | tf_op jit(solution)/shard_map/pack/pallas_call | solution.py:180
  131.9 13.9 %collective-permute-done.20.refs_1_ = bf16[512,512]{1,0:T(8,128)(2,1)} collective-permute-done((bf16[512,512]{1,0:T(8,128)(2,1)S(1)}, bf16[512,512]{1,0:T(8,128)(2,1)}, u32[]{:S(2)}, u32[]{:S(2)}) %collective-permute-start.20) | collective-permute-done | bytes 524320 | tf_op jit(solution)/shard_map/ppermute | solution.py:102
  160.4 5.1 %forward0.1 = (f32[16,768,256]{2,1,0:T(8,128)}, f32[2,8,256]{2,1,0:T(8,128)S(1)}) custom-call(s32[16]{0:T(128)S(1)} %reshape.45.lens, bf16[768,4096]{1,0:T(8,128)(2,1)S(1)} %arrange.1.rows, bf16[8,256,256]{2,1,0:T(8,128)(2,1)} %pack.8.near.refs_0_, bf16[8,256,256]{2,1,0:T(8,128)(2,1)S(1)} %copy-done.7, f32[1,4096]{1,0:T(1,128)S(1)} %bitcast.69), custom_call_target="tpu_custom_call" | custom-call | tf_op jit(solution)/shard_map/forward0/pallas_call | solution.py:231
  165.6 12.7 %collective-permute-done.25.refs_1_ = bf16[512,512]{1,0:T(8,128)(2,1)} collective-permute-done((bf16[512,512]{1,0:T(8,128)(2,1)}, bf16[512,512]{1,0:T(8,128)(2,1)}, u32[]{:S(2)}, u32[]{:S(2)}) %collective-permute-start.25) | collective-permute-done | bytes 524320 | tf_op jit(solution)/shard_map/ppermute | solution.py:102
  183.9 11.6 %forward256.1 = (f32[16,768,256]{2,1,0:T(8,128)}, f32[2,8,1024]{2,1,0:T(8,128)S(1)}) custom-call(s32[16]{0:T(128)S(1)} %reshape.45.lens, bf16[768,4096]{1,0:T(8,128)(2,1)S(1)} %arrange.1.rows, bf16[8,1024,256]{2,1,0:T(8,128)(2,1)} %pack.9.near.refs_1_, bf16[8,1024,256]{2,1,0:T(8,128)(2,1)} %collective-permute-done.28.across.refs_1_, ...), custom_call_target="tpu_custom_call", output_to_operand_aliasing={{0}: (5, {})} | custom-call | tf_op jit(solution)/shard_map/forward256/pallas_call | solution.py:231
  198.1 7.8 %forward1280.1 = (f32[16,768,256]{2,1,0:T(8,128)}, f32[2,8,512]{2,1,0:T(8,128)S(1)}) custom-call(s32[16]{0:T(128)S(1)} %reshape.45.lens, bf16[768,4096]{1,0:T(8,128)(2,1)S(1)} %arrange.1.rows, bf16[8,512,256]{2,1,0:T(8,128)(2,1)} %pack.10.near.refs_2_, ...), custom_call_target="tpu_custom_call", output_to_operand_aliasing={{0}: (5, {})} | custom-call | tf_op jit(solution)/shard_map/forward1280/pallas_call | solution.py:231
  215.2 7.2 %forward1792.1 = (f32[16,768,256]{2,1,0:T(8,128)}, f32[2,8,512]{2,1,0:T(8,128)S(1)}) custom-call(s32[16]{0:T(128)S(1)} %reshape.45.lens, bf16[768,4096]{1,0:T(8,128)(2,1)S(1)} %arrange.1.rows, bf16[8,512,256]{2,1,0:T(8,128)(2,1)} %pack.11.near.refs_3_, ...), custom_call_target="tpu_custom_call", output_to_operand_aliasing={{0}: (5, {})} | custom-call | tf_op jit(solution)/shard_map/forward1792/pallas_call | solution.py:231
  222.4 7.1 %forward2304.1 = (f32[16,768,256]{2,1,0:T(8,128)}, f32[2,8,512]{2,1,0:T(8,128)S(1)}) custom-call(s32[16]{0:T(128)S(1)} %reshape.45.lens, bf16[768,4096]{1,0:T(8,128)(2,1)S(1)} %arrange.1.rows, bf16[8,512,256]{2,1,0:T(8,128)(2,1)} %pack.12.near.refs_4_, ...), custom_call_target="tpu_custom_call", output_to_operand_aliasing={{0}: (5, {})} | custom-call | tf_op jit(solution)/shard_map/forward2304/pallas_call | solution.py:231
  229.5 6.5 %collective-permute-done.34.refs_1_ = bf16[512,512]{1,0:T(8,128)(2,1)S(1)} collective-permute-done((bf16[512,512]{1,0:T(8,128)(2,1)S(1)}, bf16[512,512]{1,0:T(8,128)(2,1)S(1)}, u32[]{:S(2)}, u32[]{:S(2)}) %collective-permute-start.34) | collective-permute-done | bytes 524320 | tf_op jit(solution)/shard_map/ppermute | solution.py:102
  245.9 7.2 %forward2816.1 = (f32[16,768,256]{2,1,0:T(8,128)}, f32[2,8,512]{2,1,0:T(8,128)S(1)}) custom-call(s32[16]{0:T(128)S(1)} %reshape.45.lens, bf16[768,4096]{1,0:T(8,128)(2,1)S(1)} %arrange.1.rows, bf16[8,512,256]{2,1,0:T(8,128)(2,1)} %pack.13.near.refs_5_, ...), custom_call_target="tpu_custom_call", output_to_operand_aliasing={{0}: (5, {})} | custom-call | tf_op jit(solution)/shard_map/forward2816/pallas_call | solution.py:231
  253.1 5.0 %collective-permute-done.43 = f32[2,8,1792]{2,1,0:T(8,128)S(1)} collective-permute-done((f32[2,8,1792]{2,1,0:T(8,128)S(1)}, f32[2,8,1792]{2,1,0:T(8,128)S(1)}, u32[]{:S(2)}, u32[]{:S(2)}) %collective-permute-start.43) | collective-permute-done | bytes 114720 | tf_op jit(solution)/shard_map/ppermute | solution.py:102
  266.5 7.1 %forward3328.1 = (f32[16,768,256]{2,1,0:T(8,128)}, f32[2,8,512]{2,1,0:T(8,128)S(1)}) custom-call(s32[16]{0:T(128)S(1)} %reshape.45.lens, bf16[768,4096]{1,0:T(8,128)(2,1)S(1)} %arrange.1.rows, bf16[8,512,256]{2,1,0:T(8,128)(2,1)} %pack.14.near.refs_6_, ...), custom_call_target="tpu_custom_call", output_to_operand_aliasing={{0}: (5, {})} | custom-call | tf_op jit(solution)/shard_map/forward3328/pallas_call | solution.py:231
  279.0 4.7 %forward3840.1 = (f32[16,768,256]{2,1,0:T(8,128)}, f32[2,8,256]{2,1,0:T(8,128)S(1)}) custom-call(s32[16]{0:T(128)S(1)} %reshape.45.lens, bf16[768,4096]{1,0:T(8,128)(2,1)S(1)} %arrange.1.rows, bf16[8,160,256]{2,1,0:T(8,128)(2,1)} %pack.15.near.refs_7_, ...), custom_call_target="tpu_custom_call", output_to_operand_aliasing={{0}: (5, {})} | custom-call | tf_op jit(solution)/shard_map/forward3840/pallas_call | solution.py:231
  302.7 8.5 %margins.1 = (f32[64,8]{1,0:T(8,128)S(1)}, bf16[768,4096]{1,0:T(8,128)(2,1)S(1)}) custom-call(f32[64,64]{1,0:T(8,128)S(1)} %fusion.s0, f32[64,64]{1,0:T(8,128)S(1)} %collective-permute-done.58.s1, f32[64,64]{1,0:T(8,128)S(1)} %collective-permute-done.59.s2, f32[64,64]{1,0:T(8,128)S(1)} %collective-permute-done.60.s3, s32[64,8]{1,0:T(8,128)S(1)} %fusion.9.ids, ...), custom_call_target="tpu_custom_call" | custom-call | tf_op jit(solution)/shard_map/margins/pallas_call | solution.py:319
  311.2 18.5 %back0.1 = (bf16[2,192,1024]{2,1,0:T(8,128)(2,1)}, f32[2,192,1024]{2,1,0:T(8,128)}, bf16[2,192,1024]{2,1,0:T(8,128)(2,1)}, f32[2,192,1024]{2,1,0:T(8,128)}) custom-call(s32[2]{0:T(128)S(1)} %pad_add_fusion.1.place, bf16[768,4096]{1,0:T(8,128)(2,1)S(1)} %get-tuple-element.249.grad, bf16[8,256,256]{2,1,0:T(8,128)(2,1)} %pack.8.near.refs_0_, ...), custom_call_target="tpu_custom_call" | custom-call | flops 12884901888 | bytes 21495808 | tf_op jit(solution)/shard_map/back0/pallas_call | solution.py:380
  331.0 11.0 %back8.1 = (bf16[2,192,512]{2,1,0:T(8,128)(2,1)}, f32[2,192,512]{2,1,0:T(8,128)}, bf16[2,192,512]{2,1,0:T(8,128)(2,1)}, f32[2,192,512]{2,1,0:T(8,128)}) custom-call(s32[2]{0:T(128)S(1)} %pad_add_fusion.1.place, bf16[768,4096]{1,0:T(8,128)(2,1)S(1)} %get-tuple-element.249.grad, bf16[8,256,256]{2,1,0:T(8,128)(2,1)} %copy-done.6, ...), custom_call_target="tpu_custom_call" | custom-call | flops 6442450944 | bytes 10747904 | tf_op jit(solution)/shard_map/back8/pallas_call | solution.py:380
  344.9 5.6 %collective-permute-done.61 = bf16[2,192,1024]{2,1,0:T(8,128)(2,1)S(1)} collective-permute-done((bf16[2,192,1024]{2,1,0:T(8,128)(2,1)}, bf16[2,192,1024]{2,1,0:T(8,128)(2,1)S(1)}, u32[]{:S(2)}, u32[]{:S(2)}) %collective-permute-start.61) | collective-permute-done | bytes 786464 | tf_op jit(solution)/shard_map/ppermute | solution.py:102
  352.5 10.7 %back12.1 = (bf16[2,192,512]{2,1,0:T(8,128)(2,1)}, f32[2,192,512]{2,1,0:T(8,128)}, bf16[2,192,512]{2,1,0:T(8,128)(2,1)}, f32[2,192,512]{2,1,0:T(8,128)}) custom-call(s32[2]{0:T(128)S(1)} %pad_add_fusion.1.place, bf16[768,4096]{1,0:T(8,128)(2,1)S(1)} %get-tuple-element.249.grad, bf16[8,256,256]{2,1,0:T(8,128)(2,1)} %copy-done.6, ...), custom_call_target="tpu_custom_call" | custom-call | flops 6442450944 | bytes 10747904 | tf_op jit(solution)/shard_map/back12/pallas_call | solution.py:380
  369.0 6.2 %collective-permute-done.69 = bf16[2,192,512]{2,1,0:T(8,128)(2,1)S(1)} collective-permute-done((bf16[2,192,512]{2,1,0:T(8,128)(2,1)}, bf16[2,192,512]{2,1,0:T(8,128)(2,1)S(1)}, u32[]{:S(2)}, u32[]{:S(2)}) %collective-permute-start.69) | collective-permute-done | bytes 393248 | tf_op jit(solution)/shard_map/ppermute | solution.py:102
  388.4 3.5 finish.1
  (352 shorter events, 156.2 us)
Async XLA Ops:
  30.2 30.1 %collective-permute-start.8 = (bf16[96,4096]{1,0:T(8,128)(2,1)S(1)}, bf16[96,4096]{1,0:T(8,128)(2,1)S(1)}, u32[]{:S(2)}, u32[]{:S(2)}) collective-permute-start(bf16[96,4096]{1,0:T(8,128)(2,1)S(1)} %get-tuple-element.134), channel_id=1, source_target_pairs={{0,8},{1,9},{2,10},{3,11},{4,12},{5,13},{6,14},{7,15},{8,0},{9,1},... | collective-permute-start | bytes 2359304 | tf_op jit(solution)/shard_map/ppermute | solution.py:102
  34.1 25.5 %collective-permute-start.5 = (bf16[512,512]{1,0:T(8,128)(2,1)S(1)}, bf16[512,512]{1,0:T(8,128)(2,1)S(1)}, u32[]{:S(2)}, u32[]{:S(2)}) collective-permute-start(bf16[512,512]{1,0:T(8,128)(2,1)S(1)} %pad_maximum_fusion.2.refs_0_), channel_id=1, source_target_pairs={{0,16},{1,17},{2,18},{3,19},{4,20},{5,21},{6,22},{7,23},{8,24},{9,... | collective-permute-start | bytes 1572872 | tf_op jit(solution)/shard_map/ppermute | solution.py:102
  35.7 23.9 %collective-permute-start.6 = (bf16[512,512]{1,0:T(8,128)(2,1)S(1)}, bf16[512,512]{1,0:T(8,128)(2,1)S(1)}, u32[]{:S(2)}, u32[]{:S(2)}) collective-permute-start(bf16[512,512]{1,0:T(8,128)(2,1)S(1)} %pad_maximum_fusion.2.refs_0_), channel_id=1, source_target_pairs={{0,4},{1,5},{2,6},{3,7},{4,0},{5,1},{6,2},{7,3},{8,12},{9,13},{10,... | collective-permute-start | bytes 1572872 | tf_op jit(solution)/shard_map/ppermute | solution.py:102
  60.3 26.2 %collective-permute-start.14 = (bf16[96,4096]{1,0:T(8,128)(2,1)S(1)}, bf16[96,4096]{1,0:T(8,128)(2,1)S(1)}, u32[]{:S(2)}, u32[]{:S(2)}) collective-permute-start(bf16[96,4096]{1,0:T(8,128)(2,1)S(1)} %collective-permute-done.8.refs_0_), channel_id=1, source_target_pairs={{0,1},{1,0},{2,3},{3,2},{4,5},{5,4},{6,7},{7,6},{8,9},{9,8},{10,11... | collective-permute-start | bytes 2359304 | tf_op jit(solution)/shard_map/ppermute | solution.py:102
  61.8 23.5 %collective-permute-start.10 = (bf16[512,512]{1,0:T(8,128)(2,1)S(1)}, bf16[512,512]{1,0:T(8,128)(2,1)S(1)}, u32[]{:S(2)}, u32[]{:S(2)}) collective-permute-start(bf16[512,512]{1,0:T(8,128)(2,1)S(1)} %pad_maximum_fusion.3.refs_4_), channel_id=1, source_target_pairs={{0,16},{1,17},{2,18},{3,19},{4,20},{5,21},{6,22},{7,23},{8,24},{9,... | collective-permute-start | bytes 1572872 | tf_op jit(solution)/shard_map/ppermute | solution.py:102
  86.5 31.3 %collective-permute-start.19 = (bf16[8,256,256]{2,1,0:T(8,128)(2,1)}, bf16[8,256,256]{2,1,0:T(8,128)(2,1)S(1)}, u32[]{:S(2)}, u32[]{:S(2)}) collective-permute-start(bf16[8,256,256]{2,1,0:T(8,128)(2,1)} %pack.8.near.refs_0_), channel_id=1, source_target_pairs={{0,2},{1,3},{2,0},{3,1},{4,6},{5,7},{6,4},{7,5},{8,10},{9,11},{10,... | collective-permute-start | bytes 3145736 | tf_op jit(solution)/shard_map/ppermute | solution.py:102
  86.6 31.2 %collective-permute-start.18 = (bf16[96,4096]{1,0:T(8,128)(2,1)S(1)}, bf16[96,4096]{1,0:T(8,128)(2,1)S(1)}, u32[]{:S(2)}, u32[]{:S(2)}) collective-permute-start(bf16[96,4096]{1,0:T(8,128)(2,1)S(1)} %get-tuple-element.144), channel_id=1, source_target_pairs={{0,8},{1,9},{2,10},{3,11},{4,12},{5,13},{6,14},{7,15},{8,0},{9,1},... | collective-permute-start | bytes 2359304 | tf_op jit(solution)/shard_map/ppermute | solution.py:102
  88.3 28.6 %collective-permute-start.15 = (bf16[512,512]{1,0:T(8,128)(2,1)S(1)}, bf16[512,512]{1,0:T(8,128)(2,1)S(1)}, u32[]{:S(2)}, u32[]{:S(2)}) collective-permute-start(bf16[512,512]{1,0:T(8,128)(2,1)S(1)} %pad_maximum_fusion.4.refs_0_), channel_id=1, source_target_pairs={{0,16},{1,17},{2,18},{3,19},{4,20},{5,21},{6,22},{7,23},{8,24},{9,... | collective-permute-start | bytes 1572872 | tf_op jit(solution)/shard_map/ppermute | solution.py:102
  91.0 25.9 %collective-permute-start.16 = (bf16[512,512]{1,0:T(8,128)(2,1)S(1)}, bf16[512,512]{1,0:T(8,128)(2,1)S(1)}, u32[]{:S(2)}, u32[]{:S(2)}) collective-permute-start(bf16[512,512]{1,0:T(8,128)(2,1)S(1)} %pad_maximum_fusion.4.refs_0_), channel_id=1, source_target_pairs={{0,4},{1,5},{2,6},{3,7},{4,0},{5,1},{6,2},{7,3},{8,12},{9,13},{10,... | collective-permute-start | bytes 1572872 | tf_op jit(solution)/shard_map/ppermute | solution.py:102
  92.5 24.4 %collective-permute-start.17 = (bf16[512,512]{1,0:T(8,128)(2,1)S(1)}, bf16[512,512]{1,0:T(8,128)(2,1)S(1)}, u32[]{:S(2)}, u32[]{:S(2)}) collective-permute-start(bf16[512,512]{1,0:T(8,128)(2,1)S(1)} %collective-permute-done.10.refs_5_), channel_id=1, source_target_pairs={{0,4},{1,5},{2,6},{3,7},{4,0},{5,1},{6,2},{7,3},{8,12},{9,13},{10,... | collective-permute-start | bytes 1572872 | tf_op jit(solution)/shard_map/ppermute | solution.py:102
  118.8 28.3 %collective-permute-start.24 = (bf16[96,4096]{1,0:T(8,128)(2,1)S(1)}, bf16[96,4096]{1,0:T(8,128)(2,1)S(1)}, u32[]{:S(2)}, u32[]{:S(2)}) collective-permute-start(bf16[96,4096]{1,0:T(8,128)(2,1)S(1)} %collective-permute-done.18.refs_1_), channel_id=1, source_target_pairs={{0,1},{1,0},{2,3},{3,2},{4,5},{5,4},{6,7},{7,6},{8,9},{9,8},{10,11... | collective-permute-start | bytes 2359304 | tf_op jit(solution)/shard_map/ppermute | solution.py:102
  120.2 25.6 %collective-permute-start.20 = (bf16[512,512]{1,0:T(8,128)(2,1)S(1)}, bf16[512,512]{1,0:T(8,128)(2,1)}, u32[]{:S(2)}, u32[]{:S(2)}) collective-permute-start(bf16[512,512]{1,0:T(8,128)(2,1)S(1)} %pad_maximum_fusion.5.refs_0_), channel_id=1, source_target_pairs={{0,16},{1,17},{2,18},{3,19},{4,20},{5,21},{6,22},{7,23},{8,24},{9,... | collective-permute-start | bytes 1572872 | tf_op jit(solution)/shard_map/ppermute | solution.py:102
  122.9 22.9 %collective-permute-start.21 = (bf16[512,512]{1,0:T(8,128)(2,1)S(1)}, bf16[512,512]{1,0:T(8,128)(2,1)S(1)}, u32[]{:S(2)}, u32[]{:S(2)}) collective-permute-start(bf16[512,512]{1,0:T(8,128)(2,1)S(1)} %pad_maximum_fusion.5.refs_0_), channel_id=1, source_target_pairs={{0,4},{1,5},{2,6},{3,7},{4,0},{5,1},{6,2},{7,3},{8,12},{9,13},{10,... | collective-permute-start | bytes 1572872 | tf_op jit(solution)/shard_map/ppermute | solution.py:102
  148.0 30.9 %collective-permute-start.28 = (bf16[8,1024,256]{2,1,0:T(8,128)(2,1)}, bf16[8,1024,256]{2,1,0:T(8,128)(2,1)}, u32[]{:S(2)}, u32[]{:S(2)}) collective-permute-start(bf16[8,1024,256]{2,1,0:T(8,128)(2,1)} %pack.9.near.refs_1_), channel_id=1, source_target_pairs={{0,2},{1,3},{2,0},{3,1},{4,6},{5,7},{6,4},{7,5},{8,10},{9,11},{10,... | collective-permute-start | bytes 12582920 | tf_op jit(solution)/shard_map/ppermute | solution.py:102
  151.5 26.8 %collective-permute-start.25 = (bf16[512,512]{1,0:T(8,128)(2,1)}, bf16[512,512]{1,0:T(8,128)(2,1)}, u32[]{:S(2)}, u32[]{:S(2)}) collective-permute-start(bf16[512,512]{1,0:T(8,128)(2,1)} %pad_maximum_fusion.6.refs_0_), channel_id=1, source_target_pairs={{0,16},{1,17},{2,18},{3,19},{4,20},{5,21},{6,22},{7,23},{8,24},{9,... | collective-permute-start | bytes 1572872 | tf_op jit(solution)/shard_map/ppermute | solution.py:102
  153.3 24.9 %collective-permute-start.26 = (bf16[512,512]{1,0:T(8,128)(2,1)}, bf16[512,512]{1,0:T(8,128)(2,1)}, u32[]{:S(2)}, u32[]{:S(2)}) collective-permute-start(bf16[512,512]{1,0:T(8,128)(2,1)} %pad_maximum_fusion.6.refs_0_), channel_id=1, source_target_pairs={{0,4},{1,5},{2,6},{3,7},{4,0},{5,1},{6,2},{7,3},{8,12},{9,13},{10,... | collective-permute-start | bytes 1572872 | tf_op jit(solution)/shard_map/ppermute | solution.py:102
  154.9 24.1 %collective-permute-start.27 = (bf16[512,512]{1,0:T(8,128)(2,1)}, bf16[512,512]{1,0:T(8,128)(2,1)}, u32[]{:S(2)}, u32[]{:S(2)}) collective-permute-start(bf16[512,512]{1,0:T(8,128)(2,1)} %collective-permute-done.20.refs_1_), channel_id=1, source_target_pairs={{0,4},{1,5},{2,6},{3,7},{4,0},{5,1},{6,2},{7,3},{8,12},{9,13},{10,... | collective-permute-start | bytes 1572872 | tf_op jit(solution)/shard_map/ppermute | solution.py:102
  179.0 27.0 %collective-permute-start.29 = (bf16[512,512]{1,0:T(8,128)(2,1)S(1)}, bf16[512,512]{1,0:T(8,128)(2,1)S(1)}, u32[]{:S(2)}, u32[]{:S(2)}) collective-permute-start(bf16[512,512]{1,0:T(8,128)(2,1)S(1)} %pad_maximum_fusion.7.refs_0_), channel_id=1, source_target_pairs={{0,16},{1,17},{2,18},{3,19},{4,20},{5,21},{6,22},{7,23},{8,24},{9,... | collective-permute-start | bytes 1572872 | tf_op jit(solution)/shard_map/ppermute | solution.py:102
  180.1 25.8 %collective-permute-start.30 = (bf16[512,512]{1,0:T(8,128)(2,1)S(1)}, bf16[512,512]{1,0:T(8,128)(2,1)S(1)}, u32[]{:S(2)}, u32[]{:S(2)}) collective-permute-start(bf16[512,512]{1,0:T(8,128)(2,1)S(1)} %pad_maximum_fusion.7.refs_0_), channel_id=1, source_target_pairs={{0,4},{1,5},{2,6},{3,7},{4,0},{5,1},{6,2},{7,3},{8,12},{9,13},{10,... | collective-permute-start | bytes 1572872 | tf_op jit(solution)/shard_map/ppermute | solution.py:102
  181.6 24.3 %collective-permute-start.31 = (bf16[512,512]{1,0:T(8,128)(2,1)}, bf16[512,512]{1,0:T(8,128)(2,1)S(1)}, u32[]{:S(2)}, u32[]{:S(2)}) collective-permute-start(bf16[512,512]{1,0:T(8,128)(2,1)} %collective-permute-done.25.refs_1_), channel_id=1, source_target_pairs={{0,4},{1,5},{2,6},{3,7},{4,0},{5,1},{6,2},{7,3},{8,12},{9,13},{10,... | collective-permute-start | bytes 1572872 | tf_op jit(solution)/shard_map/ppermute | solution.py:102
  182.1 23.8 %collective-permute-start.32 = (bf16[672,256]{1,0:T(8,128)(2,1)S(1)}, bf16[672,256]{1,0:T(8,128)(2,1)S(1)}, u32[]{:S(2)}, u32[]{:S(2)}) collective-permute-start(bf16[672,256]{1,0:T(8,128)(2,1)S(1)} %copy-done.56), channel_id=1, source_target_pairs={{0,8},{1,9},{2,10},{3,11},{4,12},{5,13},{6,14},{7,15},{8,0},{9,1},... | collective-permute-start | bytes 1032200 | tf_op jit(solution)/shard_map/ppermute | solution.py:102
  209.5 26.5 %collective-permute-start.34 = (bf16[512,512]{1,0:T(8,128)(2,1)S(1)}, bf16[512,512]{1,0:T(8,128)(2,1)S(1)}, u32[]{:S(2)}, u32[]{:S(2)}) collective-permute-start(bf16[512,512]{1,0:T(8,128)(2,1)S(1)} %pad_maximum_fusion.8.refs_0_), channel_id=1, source_target_pairs={{0,16},{1,17},{2,18},{3,19},{4,20},{5,21},{6,22},{7,23},{8,24},{9,... | collective-permute-start | bytes 1572872 | tf_op jit(solution)/shard_map/ppermute | solution.py:102
  212.1 23.9 %collective-permute-start.35 = (bf16[512,512]{1,0:T(8,128)(2,1)S(1)}, bf16[512,512]{1,0:T(8,128)(2,1)S(1)}, u32[]{:S(2)}, u32[]{:S(2)}) collective-permute-start(bf16[512,512]{1,0:T(8,128)(2,1)S(1)} %pad_maximum_fusion.8.refs_0_), channel_id=1, source_target_pairs={{0,4},{1,5},{2,6},{3,7},{4,0},{5,1},{6,2},{7,3},{8,12},{9,13},{10,... | collective-permute-start | bytes 1572872 | tf_op jit(solution)/shard_map/ppermute | solution.py:102
  213.7 23.7 %collective-permute-start.36 = (bf16[512,512]{1,0:T(8,128)(2,1)S(1)}, bf16[512,512]{1,0:T(8,128)(2,1)S(1)}, u32[]{:S(2)}, u32[]{:S(2)}) collective-permute-start(bf16[512,512]{1,0:T(8,128)(2,1)S(1)} %collective-permute-done.29.refs_1_), channel_id=1, source_target_pairs={{0,4},{1,5},{2,6},{3,7},{4,0},{5,1},{6,2},{7,3},{8,12},{9,13},{10,... | collective-permute-start | bytes 1572872 | tf_op jit(solution)/shard_map/ppermute | solution.py:102
  (115 other events, 2047.7 us)

commit v5 on v4

--- a/solution.py
+++ b/solution.py
@@ -246,14 +246,14 @@
             ],
         ),
         out_shape=[
-            pltpu.HBM((bias.shape[1] // tile, tokens, tile), F32),
+            pltpu.VMEM((bias.shape[1] // tile, tokens, tile), F32),
             jax.ShapeDtypeStruct((2, 2 * count, tiles * tile), F32),
         ],
         input_output_aliases={5: 0} if old else {},
         compiler_params=pltpu.CompilerParams(vmem_limit_bytes=24 * 2**20),
         cost_estimate=NO_COST,
         name=f"forward{start}",
-    )(lens, in_vmem(rows), *in_hbm(near), across, bias, *in_hbm(*old))
+    )(lens, in_vmem(rows), *in_hbm(near), across, bias, *map(in_vmem, old))
 
 
 def margins(parts, id_place, teachers, slopes, gathered):
@@ -331,7 +331,7 @@
         scratch_shapes=[pltpu.VMEM((queries, queries), F32)] * 2,
         compiler_params=pltpu.CompilerParams(vmem_limit_bytes=24 * 2**20),
         name="margins",
-    )(*parts, id_place, teachers, *in_hbm(slopes), *gathered)
+    )(*parts, id_place, teachers, in_vmem(slopes), *gathered)
 
 
 def back_piece(place, grads, heads, begin, steps):

time: 393 us -> 397 us (1.010)
  Pallas kernels: 134 us -> 124 us
  local copies, waits for them, and re-layouts: 11.8 us -> 20.9 us
  waiting for transfers between devices: 141 us -> 145 us
    unnamed x140 -> x144, local copies, waits for them, and re-layouts: 7.72 us -> 16.9 us
    pallas_call x8, Pallas kernels: 57.7 us -> 50.6 us  [forward(): pl.pallas_call(kernel, grid_spec=pltpu.PrefetchScalarGridSpec(num_scalar_...]
    ppermute x73, waiting for transfers between devices: 141 us -> 145 us  [swap(): return lax.ppermute(array, AXES, [(i, i ^ bits) for i in range(32)])]
  transfers between devices with their start and end apart: 73 -> 73, of which waited for: 31 -> 29; matrix products, arithmetic and copies ran while one was open for 6% -> 6% of each run, Pallas kernels for 25% -> 23%
where the time goes in v5:
time: 397 us; the launch traced here: 396 us
  waiting for transfers between devices  145 us (37%)
  Pallas kernels  124 us (31%)
  starting transfers between devices  82.3 us (21%)
  local copies, waits for them, and re-layouts  20.9 us (5%)
  other arithmetic  20 us (5%)
    ppermute x73, waiting for transfers between devices, swap(): return lax.ppermute(array, AXES, [(i, i ^ bits) for i in range(32)])  145 us
    ppermute x73, starting transfers between devices, swap(): return lax.ppermute(array, AXES, [(i, i ^ bits) for i in range(32)])  82.3 us
    pallas_call x8, Pallas kernels, forward(): pl.pallas_call(kernel, grid_spec=pltpu.PrefetchScalarGridSpec(num_scalar_...  50.6 us
    pallas_call x3, Pallas kernels, back_piece(): pl.pallas_call(kernel, grid_spec=pltpu.PrefetchScalarGridSpec(num_scalar_...  40.2 us
    pallas_call x8, Pallas kernels, pack(): pl.pallas_call(kernel, grid=(ends[-1],), in_specs=specs, out_specs=pl.Blo...  22.8 us
    unnamed x144, local copies, waits for them, and re-layouts  16.9 us
    select_n x5, other arithmetic, columns_of(): jnp.where(low == 0, head[first:first + size], head[share + first:share +...  9.84 us
  transfers between devices with their start and end apart: 73, of which 29 were waited for; matrix products, arithmetic and copies ran while one was open for 6% of the time, Pallas kernels for 23%

profile of v5, /device:TPU:0, one launch (start us, length us, event | category | flops | bytes accessed | tf_op | source)
XLA Modules:
  0.0 395.9 jit_solution(5308693943925924719)
XLA Ops:
  20.1 9.2 %collective-permute-done.1.refs_1_ = bf16[256,512]{1,0:T(8,128)(2,1)S(1)} collective-permute-done((bf16[256,512]{1,0:T(8,128)(2,1)S(1)}, bf16[256,512]{1,0:T(8,128)(2,1)S(1)}, u32[]{:S(2)}, u32[]{:S(2)}) %collective-permute-start.1) | collective-permute-done | bytes 262176 | tf_op jit(solution)/shard_map/ppermute | solution.py:102
  39.2 20.4 %collective-permute-done.9 = f32[8,18]{1,0:T(8,128)S(1)} collective-permute-done((f32[8,18]{1,0:T(8,128)S(1)}, f32[8,18]{1,0:T(8,128)S(1)}, u32[]{:S(2)}, u32[]{:S(2)}) %collective-permute-start.9) | collective-permute-done | bytes 608 | tf_op jit(solution)/shard_map/ppermute | solution.py:102
  69.9 15.4 %collective-permute-done.10.refs_5_ = bf16[512,512]{1,0:T(8,128)(2,1)S(1)} collective-permute-done((bf16[512,512]{1,0:T(8,128)(2,1)S(1)}, bf16[512,512]{1,0:T(8,128)(2,1)S(1)}, u32[]{:S(2)}, u32[]{:S(2)}) %collective-permute-start.10) | collective-permute-done | bytes 524320 | tf_op jit(solution)/shard_map/ppermute | solution.py:102
  93.0 23.9 %collective-permute-done.15.refs_1_ = bf16[512,512]{1,0:T(8,128)(2,1)S(1)} collective-permute-done((bf16[512,512]{1,0:T(8,128)(2,1)S(1)}, bf16[512,512]{1,0:T(8,128)(2,1)S(1)}, u32[]{:S(2)}, u32[]{:S(2)}) %collective-permute-start.15) | collective-permute-done | bytes 524320 | tf_op jit(solution)/shard_map/ppermute | solution.py:102
  126.5 5.4 %pack.9.near.refs_1_ = bf16[8,1024,256]{2,1,0:T(8,128)(2,1)} custom-call(bf16[512,512]{1,0:T(8,128)(2,1)} %copy-done.24, bf16[512,512]{1,0:T(8,128)(2,1)} %copy-done.41, bf16[512,512]{1,0:T(8,128)(2,1)} %copy-done.42, bf16[512,512]{1,0:T(8,128)(2,1)} %copy-done.45, bf16[512,512]{1,0:T(8,128)(2,1)} %copy-done.25, bf16[512,512]{1,0:T(8,128)(2,1)} %copy-done.43, ...), custom_call_target="tpu_custom_call" | custom-call | tf_op jit(solution)/shard_map/pack/pallas_call | solution.py:180
  131.9 14.0 %collective-permute-done.20.refs_1_ = bf16[512,512]{1,0:T(8,128)(2,1)} collective-permute-done((bf16[512,512]{1,0:T(8,128)(2,1)S(1)}, bf16[512,512]{1,0:T(8,128)(2,1)}, u32[]{:S(2)}, u32[]{:S(2)}) %collective-permute-start.20) | collective-permute-done | bytes 524320 | tf_op jit(solution)/shard_map/ppermute | solution.py:102
  160.5 4.2 %forward0.1 = (f32[16,768,256]{2,1,0:T(8,128)S(1)}, f32[2,8,256]{2,1,0:T(8,128)S(1)}) custom-call(s32[16]{0:T(128)S(1)} %reshape.45.lens, bf16[768,4096]{1,0:T(8,128)(2,1)S(1)} %arrange.1.rows, bf16[8,256,256]{2,1,0:T(8,128)(2,1)} %pack.8.near.refs_0_, bf16[8,256,256]{2,1,0:T(8,128)(2,1)S(1)} %copy-done.9, f32[1,4096]{1,0:T(1,128)S(1)} %bitcast.69), custom_call_target="tpu_custom_call" | custom-call | tf_op jit(solution)/shard_map/forward0/pallas_call | solution.py:231
  164.8 13.5 %collective-permute-done.25.refs_1_ = bf16[512,512]{1,0:T(8,128)(2,1)} collective-permute-done((bf16[512,512]{1,0:T(8,128)(2,1)}, bf16[512,512]{1,0:T(8,128)(2,1)}, u32[]{:S(2)}, u32[]{:S(2)}) %collective-permute-start.25) | collective-permute-done | bytes 524320 | tf_op jit(solution)/shard_map/ppermute | solution.py:102
  183.9 10.7 %forward256.1 = (f32[16,768,256]{2,1,0:T(8,128)S(1)}, f32[2,8,1024]{2,1,0:T(8,128)S(1)}) custom-call(s32[16]{0:T(128)S(1)} %reshape.45.lens, bf16[768,4096]{1,0:T(8,128)(2,1)S(1)} %arrange.1.rows, bf16[8,1024,256]{2,1,0:T(8,128)(2,1)} %pack.9.near.refs_1_, ...), custom_call_target="tpu_custom_call", output_to_operand_aliasing={{0}: (5, {})} | custom-call | tf_op jit(solution)/shard_map/forward256/pallas_call | solution.py:231
  197.3 6.9 %forward1280.1 = (f32[16,768,256]{2,1,0:T(8,128)S(1)}, f32[2,8,512]{2,1,0:T(8,128)S(1)}) custom-call(s32[16]{0:T(128)S(1)} %reshape.45.lens, bf16[768,4096]{1,0:T(8,128)(2,1)S(1)} %arrange.1.rows, bf16[8,512,256]{2,1,0:T(8,128)(2,1)} %pack.10.near.refs_2_, ...), custom_call_target="tpu_custom_call", output_to_operand_aliasing={{0}: (5, {})} | custom-call | tf_op jit(solution)/shard_map/forward1280/pallas_call | solution.py:231
  213.8 6.3 %forward1792.1 = (f32[16,768,256]{2,1,0:T(8,128)S(1)}, f32[2,8,512]{2,1,0:T(8,128)S(1)}) custom-call(s32[16]{0:T(128)S(1)} %reshape.45.lens, bf16[768,4096]{1,0:T(8,128)(2,1)S(1)} %arrange.1.rows, bf16[8,512,256]{2,1,0:T(8,128)(2,1)} %pack.11.near.refs_3_, ...), custom_call_target="tpu_custom_call", output_to_operand_aliasing={{0}: (5, {})} | custom-call | tf_op jit(solution)/shard_map/forward1792/pallas_call | solution.py:231
  220.1 6.2 %forward2304.1 = (f32[16,768,256]{2,1,0:T(8,128)S(1)}, f32[2,8,512]{2,1,0:T(8,128)S(1)}) custom-call(s32[16]{0:T(128)S(1)} %reshape.45.lens, bf16[768,4096]{1,0:T(8,128)(2,1)S(1)} %arrange.1.rows, bf16[8,512,256]{2,1,0:T(8,128)(2,1)} %pack.12.near.refs_4_, ...), custom_call_target="tpu_custom_call", output_to_operand_aliasing={{0}: (5, {})} | custom-call | tf_op jit(solution)/shard_map/forward2304/pallas_call | solution.py:231
  226.4 9.1 %collective-permute-done.34.refs_1_ = bf16[512,512]{1,0:T(8,128)(2,1)S(1)} collective-permute-done((bf16[512,512]{1,0:T(8,128)(2,1)S(1)}, bf16[512,512]{1,0:T(8,128)(2,1)S(1)}, u32[]{:S(2)}, u32[]{:S(2)}) %collective-permute-start.34) | collective-permute-done | bytes 524320 | tf_op jit(solution)/shard_map/ppermute | solution.py:102
  244.5 6.3 %forward2816.1 = (f32[16,768,256]{2,1,0:T(8,128)S(1)}, f32[2,8,512]{2,1,0:T(8,128)S(1)}) custom-call(s32[16]{0:T(128)S(1)} %reshape.45.lens, bf16[768,4096]{1,0:T(8,128)(2,1)S(1)} %arrange.1.rows, bf16[8,512,256]{2,1,0:T(8,128)(2,1)} %pack.13.near.refs_5_, ...), custom_call_target="tpu_custom_call", output_to_operand_aliasing={{0}: (5, {})} | custom-call | tf_op jit(solution)/shard_map/forward2816/pallas_call | solution.py:231
  250.8 5.9 %collective-permute-done.43 = f32[2,8,1792]{2,1,0:T(8,128)S(1)} collective-permute-done((f32[2,8,1792]{2,1,0:T(8,128)S(1)}, f32[2,8,1792]{2,1,0:T(8,128)S(1)}, u32[]{:S(2)}, u32[]{:S(2)}) %collective-permute-start.43) | collective-permute-done | bytes 114720 | tf_op jit(solution)/shard_map/ppermute | solution.py:102
  265.6 6.3 %forward3328.1 = (f32[16,768,256]{2,1,0:T(8,128)S(1)}, f32[2,8,512]{2,1,0:T(8,128)S(1)}) custom-call(s32[16]{0:T(128)S(1)} %reshape.45.lens, bf16[768,4096]{1,0:T(8,128)(2,1)S(1)} %arrange.1.rows, bf16[8,512,256]{2,1,0:T(8,128)(2,1)} %pack.14.near.refs_6_, ...), custom_call_target="tpu_custom_call", output_to_operand_aliasing={{0}: (5, {})} | custom-call | tf_op jit(solution)/shard_map/forward3328/pallas_call | solution.py:231
  281.4 4.6 %copy-done = f32[16,768,256]{2,1,0:T(8,128)} copy-done((f32[16,768,256]{2,1,0:T(8,128)}, f32[16,768,256]{2,1,0:T(8,128)S(1)}, u32[]{:S(2)}) %copy-start) | copy-done | bytes 12582936
  305.2 4.6 %copy-done.1 = f32[16,768,256]{2,1,0:T(8,128)S(1)} copy-done((f32[16,768,256]{2,1,0:T(8,128)S(1)}, f32[16,768,256]{2,1,0:T(8,128)}, u32[]{:S(2)}) %copy-start.1) | copy-done | bytes 12582936
  309.8 5.5 %margins.1 = (f32[64,8]{1,0:T(8,128)S(1)}, bf16[768,4096]{1,0:T(8,128)(2,1)S(1)}) custom-call(f32[64,64]{1,0:T(8,128)S(1)} %fusion.s0, f32[64,64]{1,0:T(8,128)S(1)} %collective-permute-done.58.s1, f32[64,64]{1,0:T(8,128)S(1)} %collective-permute-done.59.s2, f32[64,64]{1,0:T(8,128)S(1)} %collective-permute-done.60.s3, s32[64,8]{1,0:T(8,128)S(1)} %fusion.9.ids, ...), custom_call_target="tpu_custom_call" | custom-call | tf_op jit(solution)/shard_map/margins/pallas_call | solution.py:319
  315.2 18.5 %back0.1 = (bf16[2,192,1024]{2,1,0:T(8,128)(2,1)}, f32[2,192,1024]{2,1,0:T(8,128)}, bf16[2,192,1024]{2,1,0:T(8,128)(2,1)}, f32[2,192,1024]{2,1,0:T(8,128)}) custom-call(s32[2]{0:T(128)S(1)} %pad_add_fusion.1.place, bf16[768,4096]{1,0:T(8,128)(2,1)S(1)} %get-tuple-element.249.grad, bf16[8,256,256]{2,1,0:T(8,128)(2,1)} %pack.8.near.refs_0_, ...), custom_call_target="tpu_custom_call" | custom-call | flops 12884901888 | bytes 21495808 | tf_op jit(solution)/shard_map/back0/pallas_call | solution.py:380
  335.1 11.0 %back8.1 = (bf16[2,192,512]{2,1,0:T(8,128)(2,1)}, f32[2,192,512]{2,1,0:T(8,128)}, bf16[2,192,512]{2,1,0:T(8,128)(2,1)}, f32[2,192,512]{2,1,0:T(8,128)}) custom-call(s32[2]{0:T(128)S(1)} %pad_add_fusion.1.place, bf16[768,4096]{1,0:T(8,128)(2,1)S(1)} %get-tuple-element.249.grad, bf16[8,256,256]{2,1,0:T(8,128)(2,1)} %copy-done.8, ...), custom_call_target="tpu_custom_call" | custom-call | flops 6442450944 | bytes 10747904 | tf_op jit(solution)/shard_map/back8/pallas_call | solution.py:380
  348.9 5.6 %collective-permute-done.61 = bf16[2,192,1024]{2,1,0:T(8,128)(2,1)S(1)} collective-permute-done((bf16[2,192,1024]{2,1,0:T(8,128)(2,1)}, bf16[2,192,1024]{2,1,0:T(8,128)(2,1)S(1)}, u32[]{:S(2)}, u32[]{:S(2)}) %collective-permute-start.61) | collective-permute-done | bytes 786464 | tf_op jit(solution)/shard_map/ppermute | solution.py:102
  356.5 10.7 %back12.1 = (bf16[2,192,512]{2,1,0:T(8,128)(2,1)}, f32[2,192,512]{2,1,0:T(8,128)}, bf16[2,192,512]{2,1,0:T(8,128)(2,1)}, f32[2,192,512]{2,1,0:T(8,128)}) custom-call(s32[2]{0:T(128)S(1)} %pad_add_fusion.1.place, bf16[768,4096]{1,0:T(8,128)(2,1)S(1)} %get-tuple-element.249.grad, bf16[8,256,256]{2,1,0:T(8,128)(2,1)} %copy-done.8, ...), custom_call_target="tpu_custom_call" | custom-call | flops 6442450944 | bytes 10747904 | tf_op jit(solution)/shard_map/back12/pallas_call | solution.py:380
  373.1 6.1 %collective-permute-done.69 = bf16[2,192,512]{2,1,0:T(8,128)(2,1)S(1)} collective-permute-done((bf16[2,192,512]{2,1,0:T(8,128)(2,1)}, bf16[2,192,512]{2,1,0:T(8,128)(2,1)S(1)}, u32[]{:S(2)}, u32[]{:S(2)}) %collective-permute-start.69) | collective-permute-done | bytes 393248 | tf_op jit(solution)/shard_map/ppermute | solution.py:102
  (356 shorter events, 164.1 us)
Async XLA Ops:
  30.2 30.1 %collective-permute-start.8 = (bf16[96,4096]{1,0:T(8,128)(2,1)S(1)}, bf16[96,4096]{1,0:T(8,128)(2,1)S(1)}, u32[]{:S(2)}, u32[]{:S(2)}) collective-permute-start(bf16[96,4096]{1,0:T(8,128)(2,1)S(1)} %get-tuple-element.134), channel_id=1, source_target_pairs={{0,8},{1,9},{2,10},{3,11},{4,12},{5,13},{6,14},{7,15},{8,0},{9,1},... | collective-permute-start | bytes 2359304 | tf_op jit(solution)/shard_map/ppermute | solution.py:102
  34.1 25.5 %collective-permute-start.5 = (bf16[512,512]{1,0:T(8,128)(2,1)S(1)}, bf16[512,512]{1,0:T(8,128)(2,1)S(1)}, u32[]{:S(2)}, u32[]{:S(2)}) collective-permute-start(bf16[512,512]{1,0:T(8,128)(2,1)S(1)} %pad_maximum_fusion.2.refs_0_), channel_id=1, source_target_pairs={{0,16},{1,17},{2,18},{3,19},{4,20},{5,21},{6,22},{7,23},{8,24},{9,... | collective-permute-start | bytes 1572872 | tf_op jit(solution)/shard_map/ppermute | solution.py:102
  35.7 23.9 %collective-permute-start.6 = (bf16[512,512]{1,0:T(8,128)(2,1)S(1)}, bf16[512,512]{1,0:T(8,128)(2,1)S(1)}, u32[]{:S(2)}, u32[]{:S(2)}) collective-permute-start(bf16[512,512]{1,0:T(8,128)(2,1)S(1)} %pad_maximum_fusion.2.refs_0_), channel_id=1, source_target_pairs={{0,4},{1,5},{2,6},{3,7},{4,0},{5,1},{6,2},{7,3},{8,12},{9,13},{10,... | collective-permute-start | bytes 1572872 | tf_op jit(solution)/shard_map/ppermute | solution.py:102
  60.3 26.2 %collective-permute-start.14 = (bf16[96,4096]{1,0:T(8,128)(2,1)S(1)}, bf16[96,4096]{1,0:T(8,128)(2,1)S(1)}, u32[]{:S(2)}, u32[]{:S(2)}) collective-permute-start(bf16[96,4096]{1,0:T(8,128)(2,1)S(1)} %collective-permute-done.8.refs_0_), channel_id=1, source_target_pairs={{0,1},{1,0},{2,3},{3,2},{4,5},{5,4},{6,7},{7,6},{8,9},{9,8},{10,11... | collective-permute-start | bytes 2359304 | tf_op jit(solution)/shard_map/ppermute | solution.py:102
  61.8 23.5 %collective-permute-start.10 = (bf16[512,512]{1,0:T(8,128)(2,1)S(1)}, bf16[512,512]{1,0:T(8,128)(2,1)S(1)}, u32[]{:S(2)}, u32[]{:S(2)}) collective-permute-start(bf16[512,512]{1,0:T(8,128)(2,1)S(1)} %pad_maximum_fusion.3.refs_4_), channel_id=1, source_target_pairs={{0,16},{1,17},{2,18},{3,19},{4,20},{5,21},{6,22},{7,23},{8,24},{9,... | collective-permute-start | bytes 1572872 | tf_op jit(solution)/shard_map/ppermute | solution.py:102
  86.5 31.3 %collective-permute-start.19 = (bf16[8,256,256]{2,1,0:T(8,128)(2,1)}, bf16[8,256,256]{2,1,0:T(8,128)(2,1)S(1)}, u32[]{:S(2)}, u32[]{:S(2)}) collective-permute-start(bf16[8,256,256]{2,1,0:T(8,128)(2,1)} %pack.8.near.refs_0_), channel_id=1, source_target_pairs={{0,2},{1,3},{2,0},{3,1},{4,6},{5,7},{6,4},{7,5},{8,10},{9,11},{10,... | collective-permute-start | bytes 3145736 | tf_op jit(solution)/shard_map/ppermute | solution.py:102
  86.6 31.2 %collective-permute-start.18 = (bf16[96,4096]{1,0:T(8,128)(2,1)S(1)}, bf16[96,4096]{1,0:T(8,128)(2,1)S(1)}, u32[]{:S(2)}, u32[]{:S(2)}) collective-permute-start(bf16[96,4096]{1,0:T(8,128)(2,1)S(1)} %get-tuple-element.144), channel_id=1, source_target_pairs={{0,8},{1,9},{2,10},{3,11},{4,12},{5,13},{6,14},{7,15},{8,0},{9,1},... | collective-permute-start | bytes 2359304 | tf_op jit(solution)/shard_map/ppermute | solution.py:102
  88.3 28.6 %collective-permute-start.15 = (bf16[512,512]{1,0:T(8,128)(2,1)S(1)}, bf16[512,512]{1,0:T(8,128)(2,1)S(1)}, u32[]{:S(2)}, u32[]{:S(2)}) collective-permute-start(bf16[512,512]{1,0:T(8,128)(2,1)S(1)} %pad_maximum_fusion.4.refs_0_), channel_id=1, source_target_pairs={{0,16},{1,17},{2,18},{3,19},{4,20},{5,21},{6,22},{7,23},{8,24},{9,... | collective-permute-start | bytes 1572872 | tf_op jit(solution)/shard_map/ppermute | solution.py:102
  91.0 25.9 %collective-permute-start.16 = (bf16[512,512]{1,0:T(8,128)(2,1)S(1)}, bf16[512,512]{1,0:T(8,128)(2,1)S(1)}, u32[]{:S(2)}, u32[]{:S(2)}) collective-permute-start(bf16[512,512]{1,0:T(8,128)(2,1)S(1)} %pad_maximum_fusion.4.refs_0_), channel_id=1, source_target_pairs={{0,4},{1,5},{2,6},{3,7},{4,0},{5,1},{6,2},{7,3},{8,12},{9,13},{10,... | collective-permute-start | bytes 1572872 | tf_op jit(solution)/shard_map/ppermute | solution.py:102
  92.5 24.4 %collective-permute-start.17 = (bf16[512,512]{1,0:T(8,128)(2,1)S(1)}, bf16[512,512]{1,0:T(8,128)(2,1)S(1)}, u32[]{:S(2)}, u32[]{:S(2)}) collective-permute-start(bf16[512,512]{1,0:T(8,128)(2,1)S(1)} %collective-permute-done.10.refs_5_), channel_id=1, source_target_pairs={{0,4},{1,5},{2,6},{3,7},{4,0},{5,1},{6,2},{7,3},{8,12},{9,13},{10,... | collective-permute-start | bytes 1572872 | tf_op jit(solution)/shard_map/ppermute | solution.py:102
  118.8 28.3 %collective-permute-start.24 = (bf16[96,4096]{1,0:T(8,128)(2,1)S(1)}, bf16[96,4096]{1,0:T(8,128)(2,1)S(1)}, u32[]{:S(2)}, u32[]{:S(2)}) collective-permute-start(bf16[96,4096]{1,0:T(8,128)(2,1)S(1)} %collective-permute-done.18.refs_1_), channel_id=1, source_target_pairs={{0,1},{1,0},{2,3},{3,2},{4,5},{5,4},{6,7},{7,6},{8,9},{9,8},{10,11... | collective-permute-start | bytes 2359304 | tf_op jit(solution)/shard_map/ppermute | solution.py:102
  120.3 25.6 %collective-permute-start.20 = (bf16[512,512]{1,0:T(8,128)(2,1)S(1)}, bf16[512,512]{1,0:T(8,128)(2,1)}, u32[]{:S(2)}, u32[]{:S(2)}) collective-permute-start(bf16[512,512]{1,0:T(8,128)(2,1)S(1)} %pad_maximum_fusion.5.refs_0_), channel_id=1, source_target_pairs={{0,16},{1,17},{2,18},{3,19},{4,20},{5,21},{6,22},{7,23},{8,24},{9,... | collective-permute-start | bytes 1572872 | tf_op jit(solution)/shard_map/ppermute | solution.py:102
  122.9 22.9 %collective-permute-start.21 = (bf16[512,512]{1,0:T(8,128)(2,1)S(1)}, bf16[512,512]{1,0:T(8,128)(2,1)S(1)}, u32[]{:S(2)}, u32[]{:S(2)}) collective-permute-start(bf16[512,512]{1,0:T(8,128)(2,1)S(1)} %pad_maximum_fusion.5.refs_0_), channel_id=1, source_target_pairs={{0,4},{1,5},{2,6},{3,7},{4,0},{5,1},{6,2},{7,3},{8,12},{9,13},{10,... | collective-permute-start | bytes 1572872 | tf_op jit(solution)/shard_map/ppermute | solution.py:102
  124.5 22.6 %collective-permute-start.22 = (bf16[512,512]{1,0:T(8,128)(2,1)S(1)}, bf16[512,512]{1,0:T(8,128)(2,1)S(1)}, u32[]{:S(2)}, u32[]{:S(2)}) collective-permute-start(bf16[512,512]{1,0:T(8,128)(2,1)S(1)} %collective-permute-done.15.refs_1_), channel_id=1, source_target_pairs={{0,4},{1,5},{2,6},{3,7},{4,0},{5,1},{6,2},{7,3},{8,12},{9,13},{10,... | collective-permute-start | bytes 1572872 | tf_op jit(solution)/shard_map/ppermute | solution.py:102
  148.1 30.9 %collective-permute-start.28 = (bf16[8,1024,256]{2,1,0:T(8,128)(2,1)}, bf16[8,1024,256]{2,1,0:T(8,128)(2,1)}, u32[]{:S(2)}, u32[]{:S(2)}) collective-permute-start(bf16[8,1024,256]{2,1,0:T(8,128)(2,1)} %pack.9.near.refs_1_), channel_id=1, source_target_pairs={{0,2},{1,3},{2,0},{3,1},{4,6},{5,7},{6,4},{7,5},{8,10},{9,11},{10,... | collective-permute-start | bytes 12582920 | tf_op jit(solution)/shard_map/ppermute | solution.py:102
  151.5 26.8 %collective-permute-start.25 = (bf16[512,512]{1,0:T(8,128)(2,1)}, bf16[512,512]{1,0:T(8,128)(2,1)}, u32[]{:S(2)}, u32[]{:S(2)}) collective-permute-start(bf16[512,512]{1,0:T(8,128)(2,1)} %pad_maximum_fusion.6.refs_0_), channel_id=1, source_target_pairs={{0,16},{1,17},{2,18},{3,19},{4,20},{5,21},{6,22},{7,23},{8,24},{9,... | collective-permute-start | bytes 1572872 | tf_op jit(solution)/shard_map/ppermute | solution.py:102
  153.4 24.9 %collective-permute-start.26 = (bf16[512,512]{1,0:T(8,128)(2,1)}, bf16[512,512]{1,0:T(8,128)(2,1)}, u32[]{:S(2)}, u32[]{:S(2)}) collective-permute-start(bf16[512,512]{1,0:T(8,128)(2,1)} %pad_maximum_fusion.6.refs_0_), channel_id=1, source_target_pairs={{0,4},{1,5},{2,6},{3,7},{4,0},{5,1},{6,2},{7,3},{8,12},{9,13},{10,... | collective-permute-start | bytes 1572872 | tf_op jit(solution)/shard_map/ppermute | solution.py:102
  154.9 24.1 %collective-permute-start.27 = (bf16[512,512]{1,0:T(8,128)(2,1)}, bf16[512,512]{1,0:T(8,128)(2,1)}, u32[]{:S(2)}, u32[]{:S(2)}) collective-permute-start(bf16[512,512]{1,0:T(8,128)(2,1)} %collective-permute-done.20.refs_1_), channel_id=1, source_target_pairs={{0,4},{1,5},{2,6},{3,7},{4,0},{5,1},{6,2},{7,3},{8,12},{9,13},{10,... | collective-permute-start | bytes 1572872 | tf_op jit(solution)/shard_map/ppermute | solution.py:102
  179.0 26.5 %collective-permute-start.29 = (bf16[512,512]{1,0:T(8,128)(2,1)S(1)}, bf16[512,512]{1,0:T(8,128)(2,1)S(1)}, u32[]{:S(2)}, u32[]{:S(2)}) collective-permute-start(bf16[512,512]{1,0:T(8,128)(2,1)S(1)} %pad_maximum_fusion.7.refs_0_), channel_id=1, source_target_pairs={{0,16},{1,17},{2,18},{3,19},{4,20},{5,21},{6,22},{7,23},{8,24},{9,... | collective-permute-start | bytes 1572872 | tf_op jit(solution)/shard_map/ppermute | solution.py:102
  180.1 25.3 %collective-permute-start.30 = (bf16[512,512]{1,0:T(8,128)(2,1)S(1)}, bf16[512,512]{1,0:T(8,128)(2,1)S(1)}, u32[]{:S(2)}, u32[]{:S(2)}) collective-permute-start(bf16[512,512]{1,0:T(8,128)(2,1)S(1)} %pad_maximum_fusion.7.refs_0_), channel_id=1, source_target_pairs={{0,4},{1,5},{2,6},{3,7},{4,0},{5,1},{6,2},{7,3},{8,12},{9,13},{10,... | collective-permute-start | bytes 1572872 | tf_op jit(solution)/shard_map/ppermute | solution.py:102
  181.7 23.8 %collective-permute-start.31 = (bf16[512,512]{1,0:T(8,128)(2,1)}, bf16[512,512]{1,0:T(8,128)(2,1)S(1)}, u32[]{:S(2)}, u32[]{:S(2)}) collective-permute-start(bf16[512,512]{1,0:T(8,128)(2,1)} %collective-permute-done.25.refs_1_), channel_id=1, source_target_pairs={{0,4},{1,5},{2,6},{3,7},{4,0},{5,1},{6,2},{7,3},{8,12},{9,13},{10,... | collective-permute-start | bytes 1572872 | tf_op jit(solution)/shard_map/ppermute | solution.py:102
  209.0 26.5 %collective-permute-start.34 = (bf16[512,512]{1,0:T(8,128)(2,1)S(1)}, bf16[512,512]{1,0:T(8,128)(2,1)S(1)}, u32[]{:S(2)}, u32[]{:S(2)}) collective-permute-start(bf16[512,512]{1,0:T(8,128)(2,1)S(1)} %pad_maximum_fusion.8.refs_0_), channel_id=1, source_target_pairs={{0,16},{1,17},{2,18},{3,19},{4,20},{5,21},{6,22},{7,23},{8,24},{9,... | collective-permute-start | bytes 1572872 | tf_op jit(solution)/shard_map/ppermute | solution.py:102
  210.7 24.8 %collective-permute-start.35 = (bf16[512,512]{1,0:T(8,128)(2,1)S(1)}, bf16[512,512]{1,0:T(8,128)(2,1)S(1)}, u32[]{:S(2)}, u32[]{:S(2)}) collective-permute-start(bf16[512,512]{1,0:T(8,128)(2,1)S(1)} %pad_maximum_fusion.8.refs_0_), channel_id=1, source_target_pairs={{0,4},{1,5},{2,6},{3,7},{4,0},{5,1},{6,2},{7,3},{8,12},{9,13},{10,... | collective-permute-start | bytes 1572872 | tf_op jit(solution)/shard_map/ppermute | solution.py:102
  212.2 23.8 %collective-permute-start.36 = (bf16[512,512]{1,0:T(8,128)(2,1)S(1)}, bf16[512,512]{1,0:T(8,128)(2,1)S(1)}, u32[]{:S(2)}, u32[]{:S(2)}) collective-permute-start(bf16[512,512]{1,0:T(8,128)(2,1)S(1)} %collective-permute-done.29.refs_1_), channel_id=1, source_target_pairs={{0,4},{1,5},{2,6},{3,7},{4,0},{5,1},{6,2},{7,3},{8,12},{9,13},{10,... | collective-permute-start | bytes 1572872 | tf_op jit(solution)/shard_map/ppermute | solution.py:102
  (117 other events, 2050.3 us)
